TPU v7x, 32 devices: a whole 2x2x4 slice. The times are simulated.
32 devices in a mesh: gx: 4 (over x, core), gy: 8 (over z, y).
Axes of the slice: x: 2, y: 2, z: 4, core: 2. Of those that a mesh axis runs over, the one named last changes fastest.
Arguments:
- velocity: float32 [2, 1, 2048, 2048], P(None, None, 'gy', 'gx'), may hold values from -6 to 6
- weights_x: float32 [4, 4096], replicated, may hold values from -0.25 to 0.75
- weights_y: float32 [4, 4096], replicated, may hold values from -0.25 to 0.75
- acoustic: bfloat16 [4, 1, 4096, 4096], P(None, None, 'gy', 'gx'), may hold values from -6 to 6
- wall_mask: int32 [1, 4096, 4096], P(None, 'gy', 'gx'), may hold values 0 or 1
Outputs:
- advanced: bfloat16 [4, 1, 4096, 4096], P(None, None, 'gy', 'gx')
All inputs are finite; a program needn't handle non-finite values. No bound on the sum of `wall_mask` on one device may be relied on, other than what follows from the above.
Results may differ from a plain program's by a relative error of at most 0.002.
Values sent between devices are 32-bit elements; how exact they have to be, the bound alone decides.
No kernel may reach another device: no remote copies, remote signals or barrier semaphores. Data moves between devices by JAX's collectives and lax.ppermute only.
A program may use at most 128 MiB of HBM per device.

v0:
```python
import functools
import math

import jax
import jax.numpy as jnp
import ml_dtypes
import numpy as np
from jax import lax
from jax.experimental import pallas as pl
from jax.experimental.pallas import tpu as pltpu
from jax.sharding import PartitionSpec as P

stencil_weights = (0.75, -0.15, 1.0 / 60.0)
mean_flow = 0.3
time_step = 0.5
whole_weights = (45.0, -9.0, 1.0)

LANES = 128
RADIX = 8
HALO = 8
MARGIN = 16
TILE = 128
ROOT = math.sqrt(0.5)
STRIP = {2: (0, 6), 3: (6, 6), 1: (12, 3), 4: (15, 3), 5: (20, 4)}
STRIP_ROWS = 24
PARTS = 4
BF16 = jnp.bfloat16
F32 = jnp.float32


def halves(table):
    high = table.astype(np.float32).astype(ml_dtypes.bfloat16)
    low = (table - high.astype(np.float64)).astype(np.float32).astype(ml_dtypes.bfloat16)
    return high, low


def packed_columns(cosine, sine):
    half = LANES // 2
    parts = []
    for first in range(0, cosine.shape[1], half):
        parts += [cosine[:, first : first + half], sine[:, first : first + half]]
    return np.concatenate(parts, axis=1)


@functools.lru_cache(maxsize=None)
def x_tables(length):
    base = length // RADIX
    m = np.arange(base)[:, None]
    q = np.arange(base)[None, :]
    angle = 2.0 * np.pi * ((m * q) % base) / base
    cosine, sine = np.cos(angle), np.sin(angle)
    full = np.concatenate([packed_columns(cosine, -sine), packed_columns(sine, cosine)], axis=0)
    half = base // 2
    zero_cos, zero_sin = cosine[:, :half].copy(), -sine[:, :half]
    zero_cos[:, 0] = 0.0
    zero_sin = zero_sin.copy()
    zero_sin[:, 0] = (-1.0) ** np.arange(base)
    zero = packed_columns(zero_cos, zero_sin)
    shifted = 2.0 * np.pi * ((m * (RADIX * q[:, :half] + RADIX // 2)) % length) / length
    middle = packed_columns(np.cos(shifted), -np.sin(shifted))
    turns = 2.0 * np.pi * np.arange(1, RADIX // 2)[:, None] * np.arange(base)[None, :] / length
    return full, zero, middle, np.cos(turns), np.sin(turns)


@functools.lru_cache(maxsize=None)
def y_tables(length):
    base = length // RADIX
    index = np.arange(base)
    angle = 2.0 * np.pi * ((index[:, None] * index[None, :]) % base) / base
    both = np.concatenate([np.cos(angle), np.sin(angle)], axis=0)
    turns = 2.0 * np.pi * np.arange(RADIX)[:, None] * index[None, :] / length
    turns = np.concatenate([np.cos(turns), np.sin(turns)], axis=0).T
    high, rest = halves(turns)
    low = turns - high.astype(np.float64) - rest.astype(np.float64)
    return both, np.concatenate([high, rest, low.astype(ml_dtypes.bfloat16)], axis=1)


@functools.lru_cache(maxsize=None)
def wave_table(length, count):
    slots = LANES // 4
    base = length // RADIX
    waves = []
    for residue in (1, 2, 3):
        waves.append(RADIX * np.arange(base) + residue)
    waves.append(RADIX * np.arange(base // 2))
    waves.append(RADIX * np.arange(base // 2) + RADIX // 2)
    waves = np.concatenate(waves)
    waves = np.where(waves == 0, length // 2, waves)
    waves = np.where(waves < length // 2, waves, waves - length).reshape(count, slots)
    return np.tile(waves, (1, 4)).astype(np.float32)


@functools.lru_cache(maxsize=None)
def band_tables(rows):
    across = np.zeros((4 * LANES, 2 * LANES))
    column = np.arange(2 * LANES)
    down = np.zeros((rows, rows))
    for index, weight in enumerate(whole_weights):
        distance = index + 1
        across[column + LANES + distance, column] = weight
        across[column + LANES - distance, column] = -weight
        down += weight * (np.eye(rows, k=distance) - np.eye(rows, k=-distance))
    return across.astype(ml_dtypes.bfloat16), down.astype(ml_dtypes.bfloat16)


def beside(*tables):
    high, low = halves(np.concatenate(tables, axis=1))
    return np.concatenate([high, low], axis=0)


def split(values):
    high = values.astype(BF16)
    return high, (values - high.astype(F32)).astype(BF16)


def dot(left, right):
    return jnp.dot(left, right, preferred_element_type=F32)


def exact_dot(left, right):
    left_high, left_low = left
    right_high, right_low = right
    return dot(left_high, right_high) + (dot(left_low, right_high) + dot(left_high, right_low))


def lane_index(shape):
    return lax.broadcasted_iota(jnp.int32, shape, len(shape) - 1)


def spin(values, shift):
    return pltpu.roll(values, shift % values.shape[-1], values.ndim - 1)


def lane_tile(values, index):
    return values[:, index * LANES : (index + 1) * LANES]


def x_parts(tables, base):
    wide = 2 * base
    full = (tables[:wide], tables[wide : 2 * wide])
    at = 2 * wide
    high, low = tables[at : at + base], tables[at + base : at + 2 * base]
    return full, (high[:, :base], low[:, :base]), (high[:, base:], low[:, base:])


def pieces_kernel(place, velocity, *pieces):
    rows = pieces[0].shape[1]
    for mask, piece in enumerate(pieces):
        start = pl.multiple_of((place[0] ^ mask) * rows, 8)
        for c in range(2):
            piece[c] = velocity[c, 0, pl.ds(start, rows), :]


def rows_kernel(place, top, low, top_wall, low_wall, top_flow, low_flow, first, last, mark):
    small, width = top.shape[2], top_flow.shape[3]
    mark[0] = place[0]
    first[...] = jnp.zeros(first.shape, F32)
    last[...] = jnp.zeros(last.shape, F32)
    for k, (start, rows) in STRIP.items():
        lanes = slice(0, width) if k == PARTS + 1 else slice(None)
        if k < PARTS:
            upper, lower = top[k, 0].astype(F32)[:HALO], low[k, 0].astype(F32)[small - HALO :]
        elif k == PARTS:
            upper, lower = 1.0 - top_wall[0].astype(F32), 1.0 - low_wall[0].astype(F32)
        else:
            upper, lower = top_flow[0, 0], low_flow[0, 0]
        first[start : start + rows, lanes] = upper[:rows]
        last[start : start + rows, lanes] = lower[HALO - rows :]


def strip(ref, k, upper, lanes=slice(None)):
    if k not in STRIP:
        return jnp.zeros((HALO, ref[0:1, lanes].shape[1]), F32)
    start, rows = STRIP[k]
    values = ref[start : start + rows, lanes]
    blank = jnp.zeros((HALO - rows, values.shape[1]), F32)
    return jnp.concatenate([blank, values] if upper else [values, blank], axis=0)


def columns_kernel(
    has, left, right, left_wall, right_wall, left_flow, right_flow, above, below, to_right, to_left
):
    parts = left.shape[0]
    wide, flow_wide = above.shape[1], above.shape[1] // 2
    gap = jnp.zeros((LANES - 2 * HALO, LANES), F32)

    def tall(k, inner, first, sides):
        lanes = slice(first, first + LANES)
        over, under = strip(above, k, True, lanes), strip(below, k, False, lanes)
        return jnp.concatenate([inner, under * sides[1], gap, over * sides[0]], axis=0).T

    for k in range(parts + 1):
        at = slice(k * HALO, (k + 1) * HALO)
        if k < parts:
            near, far = left[k, 0].astype(F32), right[k, 0].astype(F32)
        else:
            near, far = 1.0 - left_wall[0].astype(F32), 1.0 - right_wall[0].astype(F32)
        sides = (has[2], has[3])
        to_left[at, :] = tall(k, near, 0, sides)[:HALO]
        to_right[at, :] = tall(k, far, wide - LANES, sides)[LANES - HALO :]
    k = parts + 1
    at = slice(k * HALO, (k + 1) * HALO)
    size = left_flow.shape[2] + LANES
    blank = jnp.zeros((HALO, to_left.shape[1] - size), F32)
    to_left[at, :size] = tall(k, left_flow[0, 0], 0, (1.0, 1.0))[:HALO]
    to_right[at, :size] = tall(k, right_flow[0, 0], flow_wide - LANES, (1.0, 1.0))[LANES - HALO :]
    to_left[at, size:] = blank
    to_right[at, size:] = blank


def sides_kernel(has, place, velocity, above, below, from_left, from_right, sides, squares, mark):
    parts, tall, _ = sides.shape
    gap = jnp.zeros((LANES - 2 * HALO, tall), F32)
    for k in range(parts):
        at = slice(k * HALO, (k + 1) * HALO)
        tile = [from_right[at, :] * has[1], gap, from_left[at, :] * has[0]]
        sides[k] = jnp.concatenate(tile, axis=0).T
    at = slice(parts * HALO, (parts + 1) * HALO)
    rows, local = velocity.shape[2:]
    size = rows + LANES
    tile = [from_right[at, :size], gap[:, :size], from_left[at, :size]]
    tile = jnp.concatenate(tile, axis=0).T
    tile = tile * tile
    mark[0] = place[0]
    over, under = (strip(ref, parts, ref is above, slice(0, local)) for ref in (above, below))
    squares[:HALO, :local] = over * over
    squares[HALO : HALO + rows, :local] = velocity[0, 0] * velocity[0, 0]
    squares[HALO + rows :, :local] = under * under
    squares[:HALO, local:] = tile[size - HALO :]
    squares[HALO : HALO + rows, local:] = tile[:rows]
    squares[HALO + rows :, local:] = tile[rows : rows + HALO]


def forward_x_kernel(place, *refs):
    *pieces, tables, turns, out, total, lines, made, sent = refs
    count, _, rows, local = lines.shape
    for mask, piece in enumerate(pieces):
        lines[place[0] ^ mask] = piece[...]
    base = turns.shape[1]
    per = local // base
    u = [lines[t // per, 0, :, (t % per) * base : (t % per + 1) * base] for t in range(RADIX)]
    v = [lines[t // per, 1, :, (t % per) * base : (t % per + 1) * base] for t in range(RADIX)]
    energy = sum(b * b for b in v)
    energy = jnp.sum(energy.reshape(rows // 8, 8, base), axis=0)
    total[...] = sum(energy[:, k : k + LANES] for k in range(0, base, LANES))
    fields = ([a * a - b * b for a, b in zip(u, v)], [2.0 * a * b for a, b in zip(u, v)])
    zeros, mids, reals, imags = [], [], [[], [], []], [[], [], []]
    for a in fields:
        s04, s26, s15, s37 = a[0] + a[4], a[2] + a[6], a[1] + a[5], a[3] + a[7]
        d04, d26, d15, d37 = a[0] - a[4], a[2] - a[6], a[1] - a[5], a[3] - a[7]
        zeros.append((s04 + s26) + (s15 + s37))
        mids.append((s04 + s26) - (s15 + s37))
        minus, plus = ROOT * (d15 - d37), ROOT * (d15 + d37)
        turned = (
            (d04 + minus, -d26 - plus),
            (s04 - s26, s37 - s15),
            (d04 - minus, d26 - plus),
        )
        for index, (real, imag) in enumerate(turned):
            c, s = turns[index : index + 1, :], turns[index + 3 : index + 4, :]
            reals[index].append(real * c + imag * s)
            imags[index].append(imag * c - real * s)
    stacked = jnp.concatenate(
        [
            jnp.concatenate([jnp.concatenate(reals[i], axis=0) for i in range(3)], axis=0),
            jnp.concatenate([jnp.concatenate(imags[i], axis=0) for i in range(3)], axis=0),
        ],
        axis=1,
    )
    full, zero, middle = x_parts(tables, base)
    full = exact_dot(split(stacked), full)
    zero = exact_dot(split(jnp.concatenate(zeros, axis=0)), zero)
    middle = exact_dot(split(jnp.concatenate(mids, axis=0)), middle)
    low = lane_index((rows, LANES)) % 64 < 32
    target, copies = 0, []
    blocks = [full[2 * rows * i : 2 * rows * (i + 1)] for i in range(3)] + [zero, middle]
    for block in blocks:
        start = target
        for first in range(0, block.shape[1], LANES):
            a = block[:rows, first : first + LANES]
            c = block[rows:, first : first + LANES]
            made[target] = jnp.where(low, a, spin(c, 32))
            made[target + 1] = jnp.where(low, spin(a, -32), c)
            target += 2
        group = pl.ds(start, target - start)
        copies.append(pltpu.make_async_copy(made.at[group], out.at[group], sent.at[len(copies)]))
        copies[-1].start()
    for copy in copies:
        copy.wait()


def eighths(x, turn):
    s04, s26, s15, s37 = x[0] + x[4], x[2] + x[6], x[1] + x[5], x[3] + x[7]
    d04, d26, d15, d37 = x[0] - x[4], x[2] - x[6], x[1] - x[5], x[3] - x[7]
    quarter = turn(s15 - s37)
    spun_26, spun_37 = turn(d26), turn(d37)
    one, three = d15 + spun_37, d15 - spun_37
    spun_one, spun_three = turn(one), turn(three)
    one = ROOT * (one + spun_one)
    three = ROOT * (spun_three - three)
    return [
        (s04 + s26) + (s15 + s37),
        (d04 + spun_26) + one,
        (s04 - s26) + quarter,
        (d04 - spun_26) + three,
        (s04 + s26) - (s15 + s37),
        (d04 + spun_26) - one,
        (s04 - s26) - quarter,
        (d04 - spun_26) - three,
    ]


def solve_y_kernel(count_x, _, lines, total, wave, both, turns, out, held, spread, made, sent):
    count, rows, _ = lines.shape
    base = turns.shape[0]
    length = count * rows
    block = count_x * rows
    per = base // rows
    lanes = lane_index((base, LANES))
    sign = jnp.where(lanes < 64, 1.0, -1.0).astype(F32)

    def minus_i(z):
        return spin(z, 64) * sign

    def plus_i(z):
        return spin(z, 64) * -sign

    fields = [
        jnp.concatenate([lines[t * per + k] for k in range(per)], axis=0) for t in range(RADIX)
    ]
    mixed = eighths(fields, minus_i)
    terms, columns = turns.shape[1], 2 * RADIX
    picked = lax.broadcasted_iota(jnp.int32, (terms, columns * LANES), 0) % columns
    lane = lane_index(picked.shape)
    value = jnp.where((lane >= RADIX * LANES) & (lane % LANES >= 64), -1.0, 1.0)
    spread[...] = dot(turns[...], jnp.where(picked == lane // LANES, value, 0.0).astype(BF16))
    cosines = [spread[:, r * LANES : (r + 1) * LANES] for r in range(RADIX)]
    sines = [spread[:, (r + RADIX) * LANES : (r + RADIX + 1) * LANES] for r in range(RADIX)]
    mixed = [mixed[0]] + [
        mixed[r] * cosines[r] + spin(mixed[r], 64) * sines[r] for r in range(1, RADIX)
    ]
    tables = (both[: 2 * base], both[2 * base :])
    product = exact_dot(tables, split(jnp.concatenate(mixed, axis=1)))
    kx = wave[0:1, :]
    first = lanes % 64 < 32
    edge = jnp.float32(length // 2)
    alone = jnp.where(first, kx * kx, 0.0)
    slope = jnp.where(first | (kx == -edge), 0.0, jnp.broadcast_to(kx, lanes.shape))
    q = lax.broadcasted_iota(jnp.int32, lanes.shape, 0)
    low_ky = RADIX * (q - jnp.where(q < base // 2, 0, base)).astype(F32)
    terms = []
    for r in range(RADIX):
        at = slice(r * LANES, (r + 1) * LANES)
        spectrum = product[:base, at] + minus_i(product[base:, at])
        ky = low_ky + float(r)
        symbol = alone + slope * ky
        if r == 0:
            corner = jnp.where((kx == -edge) & ~first, edge * edge, 0.0)
            symbol = jnp.where(ky == -edge, jnp.where(first, alone, corner), symbol)
        terms.append(symbol * pl.reciprocal(kx * kx + ky * ky) * spectrum)
    pairs = [
        jnp.where(first, low + spin(low, -32), high + spin(high, 32))
        for low, high in zip(terms[:4], terms[4:])
    ]
    product = exact_dot(tables, split(jnp.concatenate(pairs, axis=1)))
    mixed = []
    for r in range(RADIX // 2):
        at = slice(r * LANES, (r + 1) * LANES)
        value = product[:base, at] + plus_i(product[base:, at])
        cosine = jnp.where(first, cosines[r], cosines[r + 4])
        sine = jnp.where(first, sines[r], sines[r + 4])
        value = value * cosine - spin(value, 64) * sine
        value = jnp.where(first, value + spin(value, -32), spin(value, 32) - value)
        if r == 2:
            value = jnp.where(first, value, plus_i(value))
        elif r:
            turned = plus_i(value)
            odd = value + turned if r == 1 else turned - value
            value = jnp.where(first, value, ROOT * odd)
        mixed.append(value)
    even, odd = mixed[0] + mixed[2], mixed[0] - mixed[2]
    side, turned = mixed[1] + mixed[3], plus_i(mixed[1] - mixed[3])
    for t, values in enumerate((even + side, odd + turned, even - side, odd - turned)):
        start = MARGIN + 2 * t * base
        held[start : start + base, :] = values
        held[start + base : start + 2 * base, :] = spin(values, -32)
    held[0:MARGIN, :] = held[length : length + MARGIN, :]
    held[length + MARGIN : length + 2 * MARGIN, :] = held[MARGIN : 2 * MARGIN, :]
    spare = total[...] + spin(total[...], 32)
    kept = rows + 2 * MARGIN // count_x
    half = made.shape[1]
    rest = kept - half
    low = lane_index((8, LANES)) % 64 < 32
    copies = []
    for target in range(count):
        start = (target // count_x) * block + (target % count_x) * kept
        for row in range(0, half, 8):
            a = held[start + row : start + row + 8, :]
            if row < rest:
                b = spin(held[start + half + row : start + half + row + 8, :], 32)
            else:
                b = spare
            made[target, row : row + 8, :] = jnp.where(low, a, b)
        if (target + 1) % RADIX == 0:
            group = pl.ds(target + 1 - RADIX, RADIX)
            copies.append(pltpu.make_async_copy(made.at[group], out.at[group], sent.at[len(copies)]))
            copies[-1].start()
    for copy in copies:
        copy.wait()


def inverse_x_kernel(
    kept, scale, place, lines, tables, turns, *refs
):
    *outs, held = refs
    count, half, _ = lines.shape
    base = turns.shape[1]
    length = RADIX * base
    rest = kept - half
    low = lane_index((half, LANES)) % 64 < 32
    groups, spare = [], None
    for first in range(0, count, 2):
        even, odd = lines[first], lines[first + 1]
        a = jnp.where(low, even, spin(odd, 32))
        b = jnp.where(low, spin(even, -32), odd)
        groups.append(jnp.concatenate([a, b[:rest]], axis=0))
        extra = b[rest : rest + 8]
        spare = extra if spare is None else spare + extra
    mean = jnp.sum(spare) * scale
    wide = 2 * base // LANES
    narrow = base // LANES
    stacked = jnp.concatenate(
        [jnp.concatenate(groups[i * wide : (i + 1) * wide], axis=1) for i in range(3)], axis=0
    )
    at = 3 * wide
    zeros = jnp.concatenate(groups[at : at + narrow], axis=1)
    mids = jnp.concatenate(groups[at + narrow : at + 2 * narrow], axis=1)
    full, zero, middle = x_parts(tables, base)
    full = exact_dot(split(stacked), full)
    zero = exact_dot(split(zeros), zero) * scale
    mid = exact_dot(split(mids), middle) * scale
    turned = []
    for i in range(3):
        real = full[i * kept : (i + 1) * kept, :base]
        imag = full[i * kept : (i + 1) * kept, base:]
        c = turns[i : i + 1, :] * (2.0 * scale)
        s = turns[i + 3 : i + 4, :] * (2.0 * scale)
        turned.append((real * c - imag * s, real * s + imag * c))
    for t in range(RADIX):
        value = zero + mid if t % 2 == 0 else zero - mid
        for i, (real, imag) in enumerate(turned):
            eighth = t * (i + 1) % RADIX
            c = (1.0, ROOT, 0.0, -ROOT, -1.0, -ROOT, 0.0, ROOT)[eighth]
            s = (0.0, ROOT, 1.0, ROOT, 0.0, -ROOT, -1.0, -ROOT)[eighth]
            if c:
                value = value + c * real
            if s:
                value = value - s * imag
        held[:, t * base : (t + 1) * base] = mean - value
    targets, local = len(outs), outs[0].shape[1] - LANES
    right = lane_index((kept, LANES)) < 64
    for mask, out in enumerate(outs):
        start = pl.multiple_of((place[0] ^ mask) * local, LANES)
        after = pl.multiple_of(jnp.where(start + local == length, 0, start + local), LANES)
        before = pl.multiple_of(jnp.where(start == 0, length, start) - LANES, LANES)
        out[:, :local] = held[:, pl.ds(start, local)]
        out[:, local:] = jnp.where(
            right, held[:, pl.ds(after, LANES)], held[:, pl.ds(before, LANES)]
        )


def slopes_x(parts, band, with_edge):
    tiles = parts[0].shape[-1] // LANES
    pieces = []
    for first in list(range(0, tiles - 1, 2)) + ([tiles - 1] if with_edge else []):
        steps = (-1, 0, 1, 2) if first < tiles - 1 else (-1, 0, 1)
        table = band[...] if first < tiles - 1 else band[: 3 * LANES, :LANES]
        order = [(first + step) % tiles for step in steps]
        piece = None
        for part in parts:
            term = dot(jnp.concatenate([lane_tile(part, t) for t in order], axis=1), table)
            piece = term if piece is None else piece + term
        pieces.append(piece)
    return jnp.concatenate(pieces, axis=1)


def slope_y(read):
    value = read(3) - read(-3)
    for index in (0, 1):
        value = value + whole_weights[index] * (read(index + 1) - read(-index - 1))
    return value


def edged(k, side, center, up, down, above, below, sides, has, first=0):
    step = pl.program_id(0) + first
    tile, width = center.shape
    tall = sides.shape[1]
    last = (tall - LANES) // tile - 1
    base = pl.multiple_of(step * tile, 8)
    before = pl.multiple_of(jnp.where(step == 0, tall, base) - HALO, 8)
    over = jnp.where(step == 0, strip(above, k, True) * has[2], up)
    under = jnp.where(step == last, strip(below, k, False) * has[3], down)
    rows = (
        (over, sides[side, pl.ds(before, HALO), :]),
        (center, sides[side, pl.ds(base, tile), :]),
        (under, sides[side, pl.ds(pl.multiple_of(base + tile, 8), HALO), :]),
    )
    return jnp.concatenate([jnp.concatenate(pair, axis=1) for pair in rows], axis=0)


def edged_open(k, side, wall, wall_up, wall_down, above, below, sides, has, first=0):
    open_cells = [1.0 - ref[0].astype(F32) for ref in (wall, wall_up, wall_down)]
    return edged(k, side, *open_cells, above, below, sides, has, first)


def quiet_step_kernel(
    first, has, place, center, up, down, wall, wall_up, wall_down, above, below, sides, across, along, along_inner, calm, density, shown_open, mark
):
    parts, _, tile, width = center.shape
    high = tile + 2 * HALO
    opened = edged_open(parts, parts, wall, wall_up, wall_down, above, below, sides, has, first)
    values = []
    for k in range(parts):
        value = edged(
            k,
            k,
            center[k, 0].astype(F32),
            up[k, 0].astype(F32)[up.shape[2] - HALO :],
            down[k, 0].astype(F32)[:HALO],
            above,
            below,
            sides,
            has,
            first,
        )
        values.append(value)

    def drops(x, along_b, along_p):
        diverge = x[1] + along_b
        return (
            diverge + mean_flow * x[0],
            x[3] + mean_flow * x[1],
            along_p + mean_flow * x[2],
            diverge + mean_flow * x[3],
        )

    short = [value.astype(BF16) for value in values]
    x = slopes_x((jnp.concatenate(short, axis=0),), across, True)
    x = [x[k * high : (k + 1) * high] for k in range(parts)]
    table = along[...]
    dropped = drops(x, dot(table, short[2]), dot(table, short[3]))
    middle = [opened * (v - (time_step / 60.0) * d) for v, d in zip(values, dropped)]
    inner = slice(HALO, HALO + tile)
    x = slopes_x(split(jnp.concatenate([value[inner] for value in middle], axis=0)), across, False)
    x = [x[k * tile : (k + 1) * tile] for k in range(parts)]
    table = along_inner[...]
    y = [sum(dot(table, part) for part in split(middle[k][:, :width])) for k in (2, 3)]
    dropped = drops(x, *y)
    shown = opened[inner, :width]
    for k in range(parts):
        start = 0.5 * values[k][inner, :width] - (0.5 * time_step / 60.0) * dropped[k]
        value = shown * start + 0.5 * middle[k][inner, :width]
        if k == 0:
            density[0, 0] = value.astype(BF16)
        else:
            calm[k - 1] = value
    shown_open[0] = opened.astype(BF16)
    mark[0] = place[0]


def tables_kernel(place, weights_x, weights_y, rise_x, rise_y, mark):
    mark[0] = place[0]
    tiles, reach_x, lanes = rise_x.shape
    wide, length_x = (tiles - 1) * lanes, weights_x.shape[1]
    first = place[0] * wide
    half = LANES // 2

    def weights(ref, start, size):
        length = ref.shape[1]
        start = jnp.where(start < 0, start + length, jnp.where(start >= length, start - length, start))
        return ref[:, pl.ds(pl.multiple_of(start, LANES), size)]

    cells = lax.broadcasted_iota(jnp.int32, (reach_x, lanes), 0)
    fine = lax.broadcasted_iota(jnp.int32, (reach_x, lanes), 1)
    right, left = weights(weights_x, first + wide, LANES), weights(weights_x, first - LANES, LANES)
    edge = jnp.where(lane_index(right.shape) < half, right, left)
    edge = jnp.concatenate([edge, edge], axis=1)
    for k in range(tiles):
        own = weights(weights_x, first + k * lanes, lanes) if k < tiles - 1 else edge
        target = fine // 2 - 1
        if k == tiles - 1:
            target = jnp.where(fine < half, target, target + half)
        value = jnp.zeros(fine.shape, F32)
        for t in range(4):
            value = jnp.where(cells == (target + t) % reach_x, own[t : t + 1, :], value)
        rise_x[k] = value
    steps, high, reach = rise_y.shape
    tall = steps * TILE
    first = place[1] * tall
    own = [weights(weights_y, first + k * LANES, LANES) for k in range(-1, tall // LANES + 1)]
    own = jnp.concatenate([jnp.concatenate(own, axis=1), jnp.zeros((4, tall + 2 * LANES), F32)], axis=0).T
    cells = lax.broadcasted_iota(jnp.int32, (high, reach), 1) % (reach // 3)
    target = lax.broadcasted_iota(jnp.int32, (high, reach), 0) // 2 + (HALO // 2 - 1)
    for k in range(steps):
        start = LANES - HALO + k * TILE
        value = jnp.zeros((high, reach), F32)
        for t in range(4):
            value = jnp.where(cells == target + t, own[start : start + high, t : t + 1], value)
        rise_y[k] = value


def source_kernel(place, squares, opened, rise_x, rise_y, quiet, across, _, *refs):
    *lines, out, squared, cells_open, matrix, rows_matrix, calm, band, held, raised, forced, done, fetched, kept = refs
    steps = done.shape[0]
    tile, width = calm.shape[2:]
    high = tile + 2 * HALO
    rows = lines[0].shape[0]

    def tile_copies(k):
        part = quiet.at[:, pl.ds(k * tile, tile), :]
        return (
            pltpu.make_async_copy(part, calm.at[k % 2], fetched.at[k % 2]),
            pltpu.make_async_copy(opened.at[k], cells_open.at[k % 2], fetched.at[2 + k % 2]),
        )

    def done_copy(k):
        part = out.at[1:, 0, pl.ds(k * tile, tile), :]
        return pltpu.make_async_copy(done.at[k], part, kept.at[k])

    arrays = ((squares, squared), (rise_x, matrix), (rise_y, rows_matrix), (across, band))
    copies = [
        pltpu.make_async_copy(source, target, fetched.at[4 + k])
        for k, (source, target) in enumerate(arrays)
    ]
    pieces = [
        pltpu.make_async_copy(
            piece,
            held.at[pl.ds(pl.multiple_of((place[0] ^ mask) * rows, 8), rows), :],
            fetched.at[4 + len(arrays) + mask],
        )
        for mask, piece in enumerate(lines)
    ]
    for copy in pieces + copies[:2]:
        copy.start()
    for copy in pieces + copies[:1]:
        copy.wait()

    level = held[MARGIN - HALO : MARGIN - HALO + squared.shape[0], :] - squared[...]
    count = level.shape[1] // LANES
    near = lane_index((level.shape[0], LANES)) < 64
    around = []
    for k in range(count):
        after, before = lane_tile(level, (k + 1) % count), lane_tile(level, (k - 1) % count)
        around.append(split(jnp.concatenate([lane_tile(level, k), jnp.where(near, after, before)], axis=1)))
    copies[1].wait()
    for copy in (copies[2], *tile_copies(0), copies[3], *tile_copies(1)):
        copy.start()
    for k in range(count):
        lanes = 2 * LANES if k < count - 1 else LANES
        value = split(exact_dot(around[k], split(matrix[k][:, :lanes])))
        for part in range(2):
            raised[part, :, 2 * k * LANES : 2 * k * LANES + lanes] = value[part]
    for copy in copies[2:]:
        copy.wait()

    reach = rows_matrix.shape[2] // 3
    third = lane_index((high, 3 * reach)) >= 2 * reach
    for k in range(steps):
        start = k * (tile // 2)
        window = [raised[part, start : start + reach, :] for part in (0, 1, 0)]
        weights = split(rows_matrix[k])
        weights = jnp.where(third, weights[1], weights[0])
        calm_here, open_here = tile_copies(k)
        open_here.wait()
        free = time_step * cells_open[k % 2].astype(F32)
        value = free * dot(weights, jnp.concatenate(window, axis=0))
        forced[k % 2] = value
        inner = value[HALO : HALO + tile]
        shown = (0.5 / 60.0) * free[HALO : HALO + tile, :width]
        x = shown * slopes_x(split(inner), band, False)
        y = shown * slope_y(lambda d: forced[k % 2, HALO + d : HALO + d + tile, :width])
        calm_here.wait()
        still = calm.at[k % 2]
        done[k, 0] = (still[0] - x).astype(BF16)
        done[k, 1] = (still[1] - y).astype(BF16)
        done[k, 2] = (still[2] + inner[:, :width] - mean_flow * x).astype(BF16)
        done_copy(k).start()
        if k + 2 < steps:
            for copy in tile_copies(k + 2):
                copy.start()
    for k in range(steps):
        done_copy(k).wait()


def call(
    kernel, operands, outs, scratch=(), steps=0, specs=None, out_specs=None, after=(), aliases=None, megabytes=24, flops=0, moved=0, name=None
):
    count = len(operands)

    def body(*refs):
        kernel(*refs[:count], *refs[count + len(after) :])

    def whole(array):
        zeros = (0,) * len(array.shape)
        return pl.BlockSpec(array.shape, lambda *_: zeros)

    arguments = {}
    chosen = specs or {}
    if steps:
        arguments["grid"] = (steps,)
        in_specs = [chosen.get(i, whole(o)) for i, o in enumerate(operands)]
        arguments["out_specs"] = jax.tree.map(whole, outs) if out_specs is None else out_specs
    else:
        local = pl.BlockSpec(memory_space=pltpu.VMEM)
        in_specs = [chosen.get(i, local) for i in range(count)]
        if out_specs is not None:
            arguments["out_specs"] = out_specs
    return pl.pallas_call(
        body,
        out_shape=outs,
        in_specs=in_specs + [pl.BlockSpec(memory_space=pl.ANY)] * len(after),
        scratch_shapes=list(scratch),
        input_output_aliases=aliases or {},
        compiler_params=pltpu.CompilerParams(vmem_limit_bytes=megabytes << 20),
        cost_estimate=pl.CostEstimate(flops=flops, bytes_accessed=moved, transcendentals=0),
        name=name,
        **arguments,
    )(*operands, *after)


def ring(array, axis, step):
    size = lax.axis_size(axis)
    return lax.ppermute(array, axis, [(i, (i + step) % size) for i in range(size)])


def swap(array, axis, mask):
    return lax.ppermute(array, axis, [(i, i ^ mask) for i in range(lax.axis_size(axis))])


def shaped(*shape, kind=F32):
    return jax.ShapeDtypeStruct(shape, kind)


def pressure_lines(pieces, place_x, gathered, spread, stepped):
    _, rows, local_x = pieces[0].shape
    count_x, count_y = lax.axis_size("gx"), lax.axis_size("gy")
    count = count_x * count_y
    scalars = {0: pl.BlockSpec(memory_space=pltpu.SMEM)}
    length_x, length_y = local_x * count_x, rows * count
    full, zero, middle, cos_turn, sin_turn = x_tables(length_x)
    turns = np.zeros((8, cos_turn.shape[1]), np.float32)
    turns[0:3], turns[3:6] = cos_turn, sin_turn
    spectra, total = call(
        forward_x_kernel,
        (place_x, *pieces, np.concatenate([beside(full), beside(zero, middle)]), turns),
        (shaped(count, rows, LANES), shaped(8, LANES)),
        (
            pltpu.VMEM((count_x, 2, rows, local_x), F32),
            pltpu.VMEM((count, rows, LANES), F32),
            pltpu.SemaphoreType.DMA((5,)),
        ),
        specs=scalars,
        out_specs=(pl.BlockSpec(memory_space=pl.ANY), pl.BlockSpec(memory_space=pltpu.VMEM)),
        after=gathered,
        flops=10**9,
        moved=4 << 20,
        name="forward_x",
    )
    spectra = lax.all_to_all(spectra, ("gy", "gx"), 0, 0, tiled=True)
    place = lax.axis_index("gy") * count_x + lax.axis_index("gx")
    waves = jnp.asarray(wave_table(length_x, count))
    wave = lax.dynamic_slice(waves, (place, 0), (1, LANES))
    both, turns_y = y_tables(length_y)
    kept = rows + 2 * MARGIN // count_x
    half = (kept // 2 + 8) // 8 * 8
    solved = call(
        functools.partial(solve_y_kernel, count_x),
        (spread, spectra, total, wave, beside(both), turns_y),
        shaped(count, half, LANES),
        (
            pltpu.VMEM((length_y + 2 * MARGIN, LANES), F32),
            pltpu.VMEM((length_y // RADIX, 2 * RADIX * LANES), F32),
            pltpu.VMEM((count, half, LANES), F32),
            pltpu.SemaphoreType.DMA((count // RADIX,)),
        ),
        specs=scalars,
        out_specs=pl.BlockSpec(memory_space=pl.ANY),
        flops=4 * 10**9,
        moved=6 << 20,
        name="solve_y",
    )
    solved = lax.all_to_all(solved, ("gy", "gx"), 0, 0, tiled=True)
    back = 2.0 * zero.T
    back[LANES // 2] *= 0.5
    tables = np.concatenate(
        [beside(full.T), beside(back, 2.0 * middle.T)]
    )
    pressed = call(
        functools.partial(inverse_x_kernel, kept, 1.0 / (length_x * length_y)),
        (stepped, solved, tables, turns),
        (shaped(kept, local_x + LANES),) * count_x,
        (pltpu.VMEM((kept, length_x), F32),),
        specs=scalars,
        flops=10**9,
        moved=4 << 20,
        name="inverse_x",
    )
    return [piece if mask == 0 else swap(piece, "gx", mask) for mask, piece in enumerate(pressed)]


def fast_shards(velocity, weights_x, weights_y, acoustic, wall_mask):
    parts, _, tall, wide = acoustic.shape
    _, _, local_y, local_x = velocity.shape
    count_x, count_y = lax.axis_size("gx"), lax.axis_size("gy")
    place_x, place_y = lax.axis_index("gx"), lax.axis_index("gy")
    full, high, steps = wide + LANES, TILE + 2 * HALO, tall // TILE
    strips = (parts + 2) * HALO
    small = 2 * HALO
    has = jnp.stack([place_x > 0, place_x < count_x - 1, place_y > 0, place_y < count_y - 1])
    has = has.astype(F32)
    scalars = pl.BlockSpec(memory_space=pltpu.SMEM)

    def at(block, *index):
        return pl.BlockSpec(block, lambda i: index)

    own = place_x.astype(jnp.int32).reshape(1)
    first, last, cut = call(
        rows_kernel,
        (own, acoustic, acoustic, wall_mask, wall_mask, velocity, velocity),
        (shaped(STRIP_ROWS, wide),) * 2 + (shaped(1, kind=jnp.int32),),
        steps=1,
        specs={
            0: scalars,
            1: at((parts, 1, small, wide), 0, 0, 0, 0),
            2: at((parts, 1, small, wide), 0, 0, tall // small - 1, 0),
            3: at((1, HALO, wide), 0, 0, 0),
            4: at((1, HALO, wide), 0, tall // HALO - 1, 0),
            5: at((1, 1, HALO, local_x), 1, 0, 0, 0),
            6: at((1, 1, HALO, local_x), 1, 0, local_y // HALO - 1, 0),
        },
        out_specs=(at((STRIP_ROWS, wide), 0, 0),) * 2 + (scalars,),
        moved=2 << 20,
        megabytes=54,
        name="rows",
    )
    sent = call(
        pieces_kernel,
        (cut, velocity),
        (shaped(2, local_y // count_x, local_x),) * count_x,
        specs={0: scalars},
        moved=2 << 20,
        megabytes=8,
        name="pieces",
    )
    moved = [piece if mask == 0 else swap(piece, "gx", mask) for mask, piece in enumerate(sent)]
    above, below = ring(last, "gy", 1), ring(first, "gy", -1)
    to_right, to_left = call(
        columns_kernel,
        (has, acoustic, acoustic, wall_mask, wall_mask, velocity, velocity, above, below),
        (shaped(strips, tall + LANES), shaped(strips, tall + LANES)),
        steps=1,
        specs={
            0: scalars,
            1: at((parts, 1, tall, LANES), 0, 0, 0, 0),
            2: at((parts, 1, tall, LANES), 0, 0, 0, wide // LANES - 1),
            3: at((1, tall, LANES), 0, 0, 0),
            4: at((1, tall, LANES), 0, 0, wide // LANES - 1),
            5: at((1, 1, local_y, LANES), 1, 0, 0, 0),
            6: at((1, 1, local_y, LANES), 1, 0, 0, local_x // LANES - 1),
        },
        moved=8 << 20,
        megabytes=54,
        name="columns",
    )
    from_left, from_right = ring(to_right, "gx", 1), ring(to_left, "gx", -1)
    local_memory = pl.BlockSpec(memory_space=pltpu.VMEM)
    tiles = wide // (2 * LANES) + 1
    rise_x, rise_y, listed = call(
        tables_kernel,
        (jnp.stack([place_x, place_y]).astype(jnp.int32), weights_x, weights_y),
        (
            shaped(tiles, 2 * LANES, 2 * LANES),
            shaped(steps, high, 3 * (high // 2 + HALO)),
            shaped(1, kind=jnp.int32),
        ),
        specs={0: scalars},
        out_specs=(local_memory, local_memory, scalars),
        moved=4 << 20,
        megabytes=54,
        name="tables",
    )
    sides, squares, beside = call(
        sides_kernel,
        (has, listed, velocity, above, below, from_left, from_right),
        (
            shaped(parts + 1, tall + LANES, LANES),
            shaped(local_y + 2 * HALO, local_x + LANES),
            shaped(1, kind=jnp.int32),
        ),
        steps=1,
        specs={0: scalars, 1: scalars, 2: at((1, 1, local_y, local_x), 1, 0, 0, 0)},
        out_specs=(
            at((parts + 1, tall + LANES, LANES), 0, 0, 0),
            at((local_y + 2 * HALO, local_x + LANES), 0, 0),
            scalars,
        ),
        moved=8 << 20,
        megabytes=54,
        name="sides",
    )
    across, along = band_tables(high)
    along_inner = along[HALO : HALO + TILE]
    per, rows = TILE // small, TILE // HALO

    def tiled(first):
        walls = (
            pl.BlockSpec((1, TILE, wide), lambda i: (0, i + first, 0)),
            pl.BlockSpec((1, HALO, wide), lambda i: (0, jnp.maximum((i + first) * rows - 1, 0), 0)),
            pl.BlockSpec(
                (1, HALO, wide),
                lambda i: (0, jnp.minimum((i + first + 1) * rows, steps * rows - 1), 0),
            ),
        )
        cells = (
            pl.BlockSpec((parts, 1, TILE, wide), lambda i: (0, 0, i + first, 0)),
            pl.BlockSpec(
                (parts, 1, small, wide), lambda i: (0, 0, jnp.maximum((i + first) * per - 1, 0), 0)
            ),
            pl.BlockSpec(
                (parts, 1, small, wide),
                lambda i: (0, 0, jnp.minimum((i + first + 1) * per, steps * per - 1), 0),
            ),
        )
        return cells, walls

    def quiet_tiles(first, count, before):
        cells, walls = tiled(first)
        operands = (has, own, acoustic, acoustic, acoustic, wall_mask, wall_mask, wall_mask, above, below, sides)
        operands = operands + (across, along, along_inner)
        return call(
            functools.partial(quiet_step_kernel, first),
            operands,
            (
                shaped(parts - 1, tall, wide),
                shaped(*acoustic.shape, kind=BF16),
                shaped(steps, high, full, kind=BF16),
                shaped(1, kind=jnp.int32),
            ),
            steps=count,
            specs=dict(enumerate((scalars, scalars) + cells + walls)),
            out_specs=(
                pl.BlockSpec((parts - 1, TILE, wide), lambda i: (0, i + first, 0)),
                pl.BlockSpec((1, 1, TILE, wide), lambda i: (0, 0, i + first, 0)),
                pl.BlockSpec((1, high, full), lambda i: (i + first, 0, 0)),
                scalars,
            ),
            after=before,
            aliases={len(operands) + k: k for k in range(len(before))},
            megabytes=54 if first == 0 else 53,
            flops=3 * 10**9 * count,
            moved=(12 << 20) * count,
            name="quiet_step",
        )

    early = max(steps * 3 // 4, 1)
    *begun, stepped = quiet_tiles(0, early, ())
    if early < steps:
        *begun, _ = quiet_tiles(early, steps - early, begun)
    quiet, final, opened = begun
    lines = pressure_lines(moved, own, (above, below), beside, stepped)
    operands = (own, squares, opened, rise_x, rise_y, quiet, across, final, *lines)
    anywhere = pl.BlockSpec(memory_space=pl.ANY)
    specs = {k: anywhere for k in range(1, len(operands))}
    scratch = (
        pltpu.VMEM(squares.shape, F32),
        pltpu.VMEM((2,) + opened.shape[1:], BF16),
        pltpu.VMEM(rise_x.shape, F32),
        pltpu.VMEM(rise_y.shape, F32),
        pltpu.VMEM((2, parts - 1, TILE, wide), F32),
        pltpu.VMEM(across.shape, BF16),
        pltpu.VMEM((local_y + 2 * MARGIN, local_x + LANES), F32),
        pltpu.VMEM((2, local_y + 2 * HALO, full), BF16),
        pltpu.VMEM((2, high, full), F32),
        pltpu.VMEM((steps, parts - 1, TILE, wide), BF16),
        pltpu.SemaphoreType.DMA((8 + count_x,)),
        pltpu.SemaphoreType.DMA((steps,)),
    )
    return call(
        source_kernel,
        operands,
        shaped(*acoustic.shape, kind=BF16),
        scratch,
        specs={0: scalars, **specs},
        out_specs=anywhere,
        aliases={7: 0},
        megabytes=55,
        flops=4 * 10**9,
        moved=16 << 20,
        name="source_step",
    )


def fits(count_x, count_y, velocity, acoustic):
    _, planes, local_y, local_x = velocity
    _, _, tall, wide = acoustic
    length_x, length_y = local_x * count_x, local_y * count_y
    rows = local_y // count_x
    base_x, base_y = length_x // RADIX, length_y // RADIX
    return (
        planes == 1
        and acoustic[0] == PARTS
        and length_x * 2 == count_x * count_y * LANES
        and base_x % (2 * LANES) == 0
        and local_x % base_x == 0
        and rows % 8 == 0
        and base_y % rows == 0
        and base_y % 8 == 0
        and count_x * count_y % RADIX == 0
        and MARGIN * 2 % (8 * count_x) == 0
        and tall == 2 * local_y
        and wide == 2 * local_x
        and tall % TILE == 0
        and tall % LANES == 0
        and tall >= 2 * TILE
        and count_x & (count_x - 1) == 0
        and wide % (2 * LANES) == 0
    )


def extended(array, sides, width):
    for axis, dim in sides:
        size, length = (lax.axis_size(axis), array.shape[dim])
        up = [(i, (i + 1) % size) for i in range(size - 1)]
        down = [(j, i) for i, j in up]
        last = lax.slice_in_dim(array, length - width, length, axis=dim)
        leading = lax.slice_in_dim(array, 0, width, axis=dim)
        before = lax.ppermute(last, axis, up)
        after = lax.ppermute(leading, axis, down)
        array = jnp.concatenate([before, array, after], axis=dim)
    return array


def gradients(padded):
    height = padded.shape[-2] - 6
    breadth = padded.shape[-1] - 6
    rows_mid = padded[..., 3 : 3 + height, :]
    cols_mid = padded[..., :, 3 : 3 + breadth]
    along_x = jnp.zeros_like(padded[..., 3 : 3 + height, 3 : 3 + breadth])
    along_y = jnp.zeros_like(along_x)
    for index, weight in enumerate(stencil_weights):
        distance = index + 1
        along_x = along_x + weight * (
            rows_mid[..., 3 + distance : 3 + distance + breadth]
            - rows_mid[..., 3 - distance : 3 - distance + breadth]
        )
        along_y = along_y + weight * (
            cols_mid[..., 3 + distance : 3 + distance + height, :]
            - cols_mid[..., 3 - distance : 3 - distance + height, :]
        )
    return (along_x, along_y)


def tendency(padded, source):
    along_x, along_y = gradients(padded)
    diverge = along_x[1] + along_y[2]
    forcing = jnp.stack([-diverge, -along_x[3], -along_y[3], source - diverge])
    return forcing - mean_flow * along_x


def spectral_index(flat, length):
    second = length // 16
    wave = flat // second + 16 * (flat % second)
    return jnp.where(wave < length // 2, wave, wave - length).astype(jnp.float32)


def twiddles(rows_count, cols_count, modulus, sign):
    products = jnp.arange(rows_count)[:, None] * jnp.arange(cols_count)[None, :] % modulus
    angles = 2.0 * math.pi / modulus * products.astype(jnp.float32)
    return (jnp.cos(angles), sign * jnp.sin(angles))


def mix_rows(real_part, imag_part, cosine, sine):
    exact = lax.Precision.HIGHEST
    cos_real = jnp.einsum("ka,...ab->...kb", cosine, real_part, precision=exact)
    cos_imag = jnp.einsum("ka,...ab->...kb", cosine, imag_part, precision=exact)
    sin_real = jnp.einsum("ka,...ab->...kb", sine, real_part, precision=exact)
    sin_imag = jnp.einsum("ka,...ab->...kb", sine, imag_part, precision=exact)
    return (cos_real - sin_imag, cos_imag + sin_real)


def mix_cols(real_part, imag_part, cosine, sine):
    exact = lax.Precision.HIGHEST
    cos_real = jnp.einsum("...kb,bc->...kc", real_part, cosine, precision=exact)
    cos_imag = jnp.einsum("...kb,bc->...kc", imag_part, cosine, precision=exact)
    sin_real = jnp.einsum("...kb,bc->...kc", real_part, sine, precision=exact)
    sin_imag = jnp.einsum("...kb,bc->...kc", imag_part, sine, precision=exact)
    return (cos_real - sin_imag, cos_imag + sin_real)


def rotate(real_part, imag_part, cosine, sine):
    return (real_part * cosine - imag_part * sine, real_part * sine + imag_part * cosine)


def discrete(real_part, imag_part, sign):
    length = real_part.shape[-1]
    second = length // 16
    initial = real_part.shape
    folded = initial[:-1] + (16, second)
    real_part = real_part.reshape(folded)
    imag_part = imag_part.reshape(folded)
    small_cos, small_sin = twiddles(16, 16, 16, sign)
    large_cos, large_sin = twiddles(second, second, second, sign)
    turn_cos, turn_sin = twiddles(16, second, length, sign)
    if sign < 0:
        real_part, imag_part = mix_rows(real_part, imag_part, small_cos, small_sin)
        real_part, imag_part = rotate(real_part, imag_part, turn_cos, turn_sin)
        real_part, imag_part = mix_cols(real_part, imag_part, large_cos, large_sin)
    else:
        real_part, imag_part = mix_cols(real_part, imag_part, large_cos, large_sin)
        real_part, imag_part = rotate(real_part, imag_part, turn_cos, turn_sin)
        real_part, imag_part = mix_rows(real_part, imag_part, small_cos, small_sin)
        real_part = real_part / length
        imag_part = imag_part / length
    return (real_part.reshape(initial), imag_part.reshape(initial))


def transform(stacked, sign, kind):
    if kind == "real_in":
        real_part = stacked
        imag_part = jnp.zeros_like(stacked)
    else:
        half = stacked.shape[0] // 2
        real_part = stacked[:half]
        imag_part = stacked[half:]
    real_out, imag_out = discrete(real_part, imag_part, sign)
    if kind == "real_out":
        return real_out
    return jnp.concatenate([real_out, imag_out], axis=0)


def project(stacked, wave_x, wave_y):
    coef_xx = wave_x * wave_x
    coef_xy = 2.0 * wave_x * wave_y
    coef_yy = wave_y * wave_y
    denominator = wave_x * wave_x + wave_y * wave_y
    positive = denominator > 0
    safe = jnp.where(positive, denominator, 1.0)

    def combine(parts):
        numerator = -(coef_xx * parts[0] + coef_xy * parts[1] + coef_yy * parts[2])
        return jnp.where(positive, numerator / safe, 0.0)

    return jnp.stack([combine(stacked[:3]), combine(stacked[3:])])


def refine(stacked, weights):
    result = jnp.zeros(stacked.shape[:-1] + (2 * stacked.shape[-1],), jnp.float32)
    for offset in range(4):
        result = (
            result
            + jnp.repeat(jnp.roll(stacked, 1 - offset, axis=-1), 2, axis=-1) * weights[offset]
        )
    return result


def lines_x(stacked, action):
    gathered = action(lax.all_to_all(stacked, "gx", split_axis=2, concat_axis=3, tiled=True))
    return lax.all_to_all(gathered, "gx", split_axis=3, concat_axis=2, tiled=True)


def lines_y(stacked, action):
    turned = jnp.swapaxes(stacked, 2, 3)
    gathered = action(lax.all_to_all(turned, "gy", split_axis=2, concat_axis=3, tiled=True))
    returned = lax.all_to_all(gathered, "gy", split_axis=3, concat_axis=2, tiled=True)
    return jnp.swapaxes(returned, 2, 3)


def expand(fields):
    return extended(fields, (("gx", 3), ("gy", 2)), 3)


def shards(velocity, weights_x, weights_y, acoustic, wall_mask):
    acoustic = acoustic.astype(jnp.float32)
    flow_x = velocity[0]
    flow_y = velocity[1]
    tensor = jnp.stack([flow_x * flow_x, flow_x * flow_y, flow_y * flow_y])
    count_gx = lax.axis_size("gx")
    count_gy = lax.axis_size("gy")
    place_x = lax.axis_index("gx")
    place_y = lax.axis_index("gy")
    local_y = tensor.shape[2]
    local_x = tensor.shape[3]
    length_x = local_x * count_gx
    length_y = local_y * count_gy

    def forward_real(portion):
        return transform(portion, -1, "real_in")

    def finish_x(portion):
        return refine(transform(portion, 1, "real_out"), weights_x)

    spectra = lines_x(tensor, forward_real)
    share_x = local_x // count_gy
    line_x = spectral_index(place_x * local_x + place_y * share_x + jnp.arange(share_x), length_x)[
        :, None
    ]
    line_y = spectral_index(jnp.arange(length_y), length_y)[None, :]

    def solve_y(portion):
        solved = project(transform(portion, -1, "complex"), line_x, line_y)
        return refine(transform(solved, 1, "complex"), weights_y)

    pressure = lines_y(spectra, solve_y)
    source = lines_x(pressure, finish_x)[0]
    open_cells = (1 - wall_mask).astype(jnp.float32)
    first_rate = tendency(expand(acoustic), source)
    middle = open_cells * (acoustic + time_step * first_rate)
    second_rate = tendency(expand(middle), source)
    return (open_cells * (acoustic + 0.5 * time_step * (first_rate + second_rate))).astype(
        jnp.bfloat16
    )


def solution(mesh):
    in_specs = (P(None, None, "gy", "gx"), P(), P(), P(None, None, "gy", "gx"), P(None, "gy", "gx"))
    out_specs = P(None, None, "gy", "gx")

    def chosen(velocity, weights_x, weights_y, acoustic, wall_mask):
        sizes = (mesh.shape["gx"], mesh.shape["gy"], velocity.shape, acoustic.shape)
        plan = fast_shards if fits(*sizes) else shards
        return plan(velocity, weights_x, weights_y, acoustic, wall_mask)

    return jax.shard_map(
        chosen, mesh=mesh, in_specs=in_specs, out_specs=out_specs, check_vma=False
    )
```

profile of v0, /device:TPU:0, one launch (start us, length us, event | category | flops | bytes accessed | tf_op | source)
XLA Modules:
  0.0 101.4 jit_solution(11674411205395703520)
XLA Ops:
  0.0 1.8 %rows.1 = (f32[24,1024]{1,0:T(8,128)}, f32[24,1024]{1,0:T(8,128)}, s32[1]{0:T(128)}) custom-call(s32[1]{0:T(128)} %bitcast.refs_0_.refs_1_, bf16[4,1,512,1024]{3,2,1,0:T(8,128)(2,1)} %refs_4_.8, bf16[4,1,512,1024]{3,2,1,0:T(8,128)(2,1)} %refs_4_.8, s32[1,512,1024]{2,1,0:T(8,128)} %refs_7_.3, s32[1,512,1024]{2,1,0:T(8,128)} %refs_7_.3, ...), custom_call_target="tpu_custom_call" | custom-call | bytes 2097152 | tf_op jit(solution)/shard_map/rows/pallas_call | solution.py:718
  1.9 0.6 pieces.1
  2.5 0.5 collective-permute-start.4
  3.0 2.6 %collective-permute-start.5 = (f32[2,64,512]{2,1,0:T(8,128)S(1)}, f32[2,64,512]{2,1,0:T(8,128)S(1)}, u32[]{:S(2)}, u32[]{:S(2)}) collective-permute-start(f32[2,64,512]{2,1,0:T(8,128)S(1)} %get-tuple-element.53), channel_id=1, source_target_pairs={{0,16},{8,24},{16,0},{24,8},{1,17},{9,25},{17,1},{25,9},{2,18},{10... | collective-permute-start | bytes 786440 | tf_op jit(solution)/shard_map/ppermute | solution.py:737
  5.6 0.1 collective-permute-start.6
  5.7 1.8 %collective-permute-start = (f32[24,1024]{1,0:T(8,128)}, f32[24,1024]{1,0:T(8,128)S(1)}, u32[]{:S(2)}, u32[]{:S(2)}) collective-permute-start(f32[24,1024]{1,0:T(8,128)} %get-tuple-element.34), channel_id=1, source_target_pairs={{0,1},{1,2},{2,3},{3,4},{4,5},{5,6},{6,7},{7,0},{8,9},{9,10},{10,1... | collective-permute-start | bytes 294920 | tf_op jit(solution)/shard_map/ppermute | solution.py:733
  7.4 3.0 %collective-permute-start.1 = (f32[24,1024]{1,0:T(8,128)}, f32[24,1024]{1,0:T(8,128)S(1)}, u32[]{:S(2)}, u32[]{:S(2)}) collective-permute-start(f32[24,1024]{1,0:T(8,128)} %get-tuple-element.35), channel_id=1, source_target_pairs={{0,7},{1,0},{2,1},{3,2},{4,3},{5,4},{6,5},{7,6},{8,15},{9,8},{10,9... | collective-permute-start | bytes 294920 | tf_op jit(solution)/shard_map/ppermute | solution.py:733
  10.5 3.6 %collective-permute-done.refs_7_.refs_3_.refs_8_ = f32[24,1024]{1,0:T(8,128)S(1)} collective-permute-done((f32[24,1024]{1,0:T(8,128)}, f32[24,1024]{1,0:T(8,128)S(1)}, u32[]{:S(2)}, u32[]{:S(2)}) %collective-permute-start) | collective-permute-done | bytes 98336 | tf_op jit(solution)/shard_map/ppermute | solution.py:733
  14.1 0.4 collective-permute-done.1.refs_8_.refs_4_.refs_9_
  14.5 0.0 collective-permute-done.4.refs_2_
  14.5 0.0 collective-permute-done.5.refs_3_
  14.5 3.3 %collective-permute-done.6.refs_4_ = f32[2,64,512]{2,1,0:T(8,128)S(1)} collective-permute-done((f32[2,64,512]{2,1,0:T(8,128)S(1)}, f32[2,64,512]{2,1,0:T(8,128)S(1)}, u32[]{:S(2)}, u32[]{:S(2)}) %collective-permute-start.6) | collective-permute-done | bytes 262176 | tf_op jit(solution)/shard_map/ppermute | solution.py:737
  17.9 2.1 %forward_x.1 = (f32[32,64,128]{2,1,0:T(8,128)}, f32[8,128]{1,0:T(8,128)S(1)}) custom-call(s32[1]{0:T(128)} %bitcast.refs_0_.refs_1_, f32[2,64,512]{2,1,0:T(8,128)S(1)} %get-tuple-element.51.refs_1_, f32[2,64,512]{2,1,0:T(8,128)S(1)} %collective-permute-done.4.refs_2_, f32[2,64,512]{2,1,0:T(8,128)S(1)} %collective-permute-done.5.refs_3_, ...), custom_call_target="tpu_custom_call" | custom-call | flops 1000000000 | bytes 4194304 | tf_op jit(solution)/shard_map/forward_x/pallas_call | solution.py:718
  19.9 5.9 %all-to-all-start = ((f32[32,64,128]{2,1,0:T(8,128)}), f32[32,64,128]{2,1,0:T(8,128)S(1)}, u32[]{:S(2)}, u32[]{:S(2)}) async-start(f32[32,64,128]{2,1,0:T(8,128)} %get-tuple-element.55), calls=%async_computation | async-start | bytes 2097152 | tf_op jit(solution)/shard_map/all_to_all | solution.py:769
  25.9 0.6 add_convert_fusion.refs_0_
  26.5 3.0 %columns.1 = (f32[48,640]{1,0:T(8,128)}, f32[48,640]{1,0:T(8,128)}) custom-call(f32[4]{0:T(128)} %add_convert_fusion.refs_0_, bf16[4,1,512,1024]{3,2,1,0:T(8,128)(2,1)} %refs_4_.8, bf16[4,1,512,1024]{3,2,1,0:T(8,128)(2,1)} %refs_4_.8, s32[1,512,1024]{2,1,0:T(8,128)} %refs_7_.3, s32[1,512,1024]{2,1,0:T(8,128)} %refs_7_.3, f32[2,1,256,512]{3,2,1,0:T(8,128)} %refs_1_.7, ...), custom_call_target="tpu_custom_call" | custom-call | bytes 8388608 | tf_op jit(solution)/shard_map/columns/pallas_call | solution.py:718
  29.5 0.3 collective-permute-start.2
  29.7 1.5 %collective-permute-start.3 = (f32[48,640]{1,0:T(8,128)}, f32[48,640]{1,0:T(8,128)S(1)}, u32[]{:S(2)}, u32[]{:S(2)}) collective-permute-start(f32[48,640]{1,0:T(8,128)} %get-tuple-element.37), channel_id=1, source_target_pairs={{0,24},{8,0},{16,8},{24,16},{1,25},{9,1},{17,9},{25,17},{2,26},{10... | collective-permute-start | bytes 368648 | tf_op jit(solution)/shard_map/ppermute | solution.py:733
  31.2 0.7 pad_add_fusion.refs_0_
  31.9 2.8 %tables.1 = (f32[5,256,256]{2,1,0:T(8,128)}, f32[4,144,240]{2,1,0:T(8,128)}, s32[1]{0:T(128)}) custom-call(s32[2]{0:T(128)} %pad_add_fusion.refs_0_, f32[4,4096]{1,0:T(4,128)} %refs_1_.4, f32[4,4096]{1,0:T(4,128)} %refs_2_.7), custom_call_target="tpu_custom_call" | custom-call | bytes 4194304 | tf_op jit(solution)/shard_map/tables/pallas_call | solution.py:718
  34.7 0.7 constant_dynamic-slice_fusion.refs_3_
  35.4 3.7 %collective-permute-done.2.refs_5_ = f32[48,640]{1,0:T(8,128)S(1)} collective-permute-done((f32[48,640]{1,0:T(8,128)}, f32[48,640]{1,0:T(8,128)S(1)}, u32[]{:S(2)}, u32[]{:S(2)}) %collective-permute-start.2) | collective-permute-done | bytes 122912 | tf_op jit(solution)/shard_map/ppermute | solution.py:733
  39.1 0.0 collective-permute-done.3.refs_6_
  39.1 0.6 copy-done.18
  39.8 0.0 copy-done.19
  39.8 3.8 %sides.1 = (f32[5,640,128]{2,1,0:T(8,128)}, f32[272,640]{1,0:T(8,128)}, s32[1]{0:T(128)}) custom-call(f32[4]{0:T(128)} %add_convert_fusion.refs_0_, s32[1]{0:T(128)} %get-tuple-element.33.refs_1_, f32[2,1,256,512]{3,2,1,0:T(8,128)} %refs_1_.7, f32[24,1024]{1,0:T(8,128)} %copy-done.2, f32[24,1024]{1,0:T(8,128)} %copy-done.4, f32[48,640]{1,0:T(8,128)} %copy-done.18, ...), custom_call_target="tpu_custom_call" | custom-call | bytes 8388608 | tf_op jit(solution)/shard_map/sides/pallas_call | solution.py:718
  43.6 8.5 %all-to-all-done.refs_1_ = f32[32,64,128]{2,1,0:T(8,128)S(1)} async-done(((f32[32,64,128]{2,1,0:T(8,128)}), f32[32,64,128]{2,1,0:T(8,128)S(1)}, u32[]{:S(2)}, u32[]{:S(2)}) %all-to-all-start) | async-done | bytes 1048608 | tf_op jit(solution)/shard_map/all_to_all | solution.py:769
  52.1 0.0 copy-done.12
  52.1 4.8 %solve_y.1 = f32[32,40,128]{2,1,0:T(8,128)} custom-call(s32[1]{0:T(128)} %get-tuple-element.49.refs_0_, f32[32,64,128]{2,1,0:T(8,128)S(1)} %all-to-all-done.refs_1_, f32[8,128]{1,0:T(8,128)S(1)} %get-tuple-element.56.refs_2_, f32[1,128]{1,0:T(1,128)S(1)} %constant_dynamic-slice_fusion.refs_3_, bf16[1024,256]{1,0:T(8,128)(2,1)S(1)} %copy-done.12, ...), custom_call_target="tpu_custom_call" | custom-call | flops 4000000000 | bytes 6291456 | tf_op jit(solution)/shard_map/solve_y/pallas_call | solution.py:718
  56.9 3.6 %all-to-all-start.1 = ((f32[32,40,128]{2,1,0:T(8,128)}), f32[32,40,128]{2,1,0:T(8,128)S(1)}, u32[]{:S(2)}, u32[]{:S(2)}) async-start(f32[32,40,128]{2,1,0:T(8,128)} %solve_y.1), calls=%async_computation.1 | async-start | bytes 1310720 | tf_op jit(solution)/shard_map/all_to_all | solution.py:792
  60.5 0.0 copy-start.10
  60.6 13.4 %quiet_step.2 = (f32[3,512,1024]{2,1,0:T(8,128)}, bf16[4,1,512,1024]{3,2,1,0:T(8,128)(2,1)}, bf16[4,144,1152]{2,1,0:T(8,128)(2,1)}, s32[1]{0:T(128)}) custom-call(f32[4]{0:T(128)} %add_convert_fusion.refs_0_, s32[1]{0:T(128)} %bitcast.refs_0_.refs_1_, bf16[4,1,512,1024]{3,2,1,0:T(8,128)(2,1)} %refs_4_.8, bf16[4,1,512,1024]{3,2,1,0:T(8,128)(2,1)} %refs_4_.8, ...), custom_call_target="tpu_custom_call" | custom-call | flops 8999999488 | bytes 37748736 | tf_op jit(solution)/shard_map/quiet_step/pallas_call | solution.py:718
  74.0 0.0 copy-start.1
  74.0 0.0 copy-start.3
  74.0 0.0 copy-start.7
  74.0 0.0 copy-start.8
  74.1 4.4 %all-to-all-done.1.refs_1_ = f32[32,40,128]{2,1,0:T(8,128)S(1)} async-done(((f32[32,40,128]{2,1,0:T(8,128)}), f32[32,40,128]{2,1,0:T(8,128)S(1)}, u32[]{:S(2)}, u32[]{:S(2)}) %all-to-all-start.1) | async-done | bytes 655392 | tf_op jit(solution)/shard_map/all_to_all | solution.py:792
  78.5 1.6 %inverse_x.1 = (f32[72,640]{1,0:T(8,128)S(1)}, f32[72,640]{1,0:T(8,128)S(1)}, f32[72,640]{1,0:T(8,128)S(1)}, f32[72,640]{1,0:T(8,128)S(1)}) custom-call(s32[1]{0:T(128)} %get-tuple-element.48.refs_0_, f32[32,40,128]{2,1,0:T(8,128)S(1)} %all-to-all-done.1.refs_1_, bf16[1536,512]{1,0:T(8,128)(2,1)S(1)} %copy-done.10, f32[8,256]{1,0:T(8,128)S(1)} %copy-done.14), custom_call_target="tpu_custom_call" | custom-call | flops 1000000000 | bytes 4194304 | tf_op jit(solution)/shard_map/inverse_x/pallas_call | solution.py:718
  80.1 0.7 copy-done.6
  80.7 0.1 collective-permute-start.7
  80.8 1.6 %collective-permute-start.8 = (f32[72,640]{1,0:T(8,128)S(1)}, f32[72,640]{1,0:T(8,128)S(1)}, u32[]{:S(2)}, u32[]{:S(2)}) collective-permute-start(f32[72,640]{1,0:T(8,128)S(1)} %get-tuple-element.59), channel_id=1, source_target_pairs={{0,16},{8,24},{16,0},{24,8},{1,17},{9,25},{17,1},{25,9},{2,18},{10... | collective-permute-start | bytes 552968 | tf_op jit(solution)/shard_map/ppermute | solution.py:737
  82.4 0.2 collective-permute-start.9
  82.6 6.6 %quiet_step.3 = (f32[3,512,1024]{2,1,0:T(8,128)}, bf16[4,1,512,1024]{3,2,1,0:T(8,128)(2,1)}, bf16[4,144,1152]{2,1,0:T(8,128)(2,1)}, s32[1]{0:T(128)}) custom-call(f32[4]{0:T(128)S(1)} %copy-done.9, s32[1]{0:T(128)} %bitcast.refs_0_.refs_1_, bf16[4,1,512,1024]{3,2,1,0:T(8,128)(2,1)} %refs_4_.8, ...), custom_call_target="tpu_custom_call", output_to_operand_aliasing={{0}: (14, {}), {1}: (15, {}), {2}: (16, {})} | custom-call | flops 3000000000 | bytes 12582912 | tf_op jit(solution)/shard_map/quiet_step/pallas_call | solution.py:718
  89.2 0.0 collective-permute-done.7.refs_9_
  89.2 0.0 collective-permute-done.8.refs_10_
  89.3 2.0 %collective-permute-done.9.refs_11_ = f32[72,640]{1,0:T(8,128)S(1)} collective-permute-done((f32[72,640]{1,0:T(8,128)S(1)}, f32[72,640]{1,0:T(8,128)S(1)}, u32[]{:S(2)}, u32[]{:S(2)}) %collective-permute-start.9) | collective-permute-done | bytes 184352 | tf_op jit(solution)/shard_map/ppermute | solution.py:737
  91.3 0.7 copy-done.17
  91.9 9.3 %source_step.1 = bf16[4,1,512,1024]{3,2,1,0:T(8,128)(2,1)} custom-call(s32[1]{0:T(128)} %bitcast.refs_0_.refs_1_, f32[272,640]{1,0:T(8,128)} %get-tuple-element.38.refs_1_, bf16[4,144,1152]{2,1,0:T(8,128)(2,1)} %get-tuple-element.43.refs_2_, f32[5,256,256]{2,1,0:T(8,128)} %get-tuple-element.44.refs_3_, ...), custom_call_target="tpu_custom_call", output_to_operand_aliasing={{}: (7, {})} | custom-call | flops 4000000000 | bytes 16777216 | tf_op jit(solution)/shard_map/source_step/pallas_call | solution.py:718
  (30 shorter events, 0.1 us)
Async XLA Ops:
  0.0 1.9 %copy-start = (f32[2,1,256,512]{3,2,1,0:T(8,128)S(1)}, f32[2,1,256,512]{3,2,1,0:T(8,128)}, u32[]{:S(2)}) copy-start(f32[2,1,256,512]{3,2,1,0:T(8,128)} %refs_1_.7) | copy-start | bytes 3145732
  0.0 17.8 %copy-start.11 = (bf16[1536,512]{1,0:T(8,128)(2,1)S(1)}, bf16[1536,512]{1,0:T(8,128)(2,1)}, u32[]{:S(2)}) copy-start(bf16[1536,512]{1,0:T(8,128)(2,1)} %constant.39.clone.refs_5_) | copy-start | bytes 4718596
  0.0 17.8 %copy-start.14 = (f32[8,256]{1,0:T(8,128)S(1)}, f32[8,256]{1,0:T(8,128)}, u32[]{:S(2)}) copy-start(f32[8,256]{1,0:T(8,128)} %constant.40.clone.refs_6_.refs_3_) | copy-start | bytes 24580
  2.5 12.0 %collective-permute-start.4 = (f32[2,64,512]{2,1,0:T(8,128)S(1)}, f32[2,64,512]{2,1,0:T(8,128)S(1)}, u32[]{:S(2)}, u32[]{:S(2)}) collective-permute-start(f32[2,64,512]{2,1,0:T(8,128)S(1)} %get-tuple-element.52), channel_id=1, source_target_pairs={{0,8},{8,0},{16,24},{24,16},{1,9},{9,1},{17,25},{25,17},{2,10},{10... | collective-permute-start | bytes 786440 | tf_op jit(solution)/shard_map/ppermute | solution.py:737
  3.0 11.5 %collective-permute-start.5 = (f32[2,64,512]{2,1,0:T(8,128)S(1)}, f32[2,64,512]{2,1,0:T(8,128)S(1)}, u32[]{:S(2)}, u32[]{:S(2)}) collective-permute-start(f32[2,64,512]{2,1,0:T(8,128)S(1)} %get-tuple-element.53), channel_id=1, source_target_pairs={{0,16},{8,24},{16,0},{24,8},{1,17},{9,25},{17,1},{25,9},{2,18},{10... | collective-permute-start | bytes 786440 | tf_op jit(solution)/shard_map/ppermute | solution.py:737
  5.6 12.3 %collective-permute-start.6 = (f32[2,64,512]{2,1,0:T(8,128)S(1)}, f32[2,64,512]{2,1,0:T(8,128)S(1)}, u32[]{:S(2)}, u32[]{:S(2)}) collective-permute-start(f32[2,64,512]{2,1,0:T(8,128)S(1)} %get-tuple-element.54), channel_id=1, source_target_pairs={{0,24},{8,16},{16,8},{24,0},{1,25},{9,17},{17,9},{25,1},{2,26},{10... | collective-permute-start | bytes 786440 | tf_op jit(solution)/shard_map/ppermute | solution.py:737
  5.7 8.4 %collective-permute-start = (f32[24,1024]{1,0:T(8,128)}, f32[24,1024]{1,0:T(8,128)S(1)}, u32[]{:S(2)}, u32[]{:S(2)}) collective-permute-start(f32[24,1024]{1,0:T(8,128)} %get-tuple-element.34), channel_id=1, source_target_pairs={{0,1},{1,2},{2,3},{3,4},{4,5},{5,6},{6,7},{7,0},{8,9},{9,10},{10,1... | collective-permute-start | bytes 294920 | tf_op jit(solution)/shard_map/ppermute | solution.py:733
  7.4 7.1 %collective-permute-start.1 = (f32[24,1024]{1,0:T(8,128)}, f32[24,1024]{1,0:T(8,128)S(1)}, u32[]{:S(2)}, u32[]{:S(2)}) collective-permute-start(f32[24,1024]{1,0:T(8,128)} %get-tuple-element.35), channel_id=1, source_target_pairs={{0,7},{1,0},{2,1},{3,2},{4,3},{5,4},{6,5},{7,6},{8,15},{9,8},{10,9... | collective-permute-start | bytes 294920 | tf_op jit(solution)/shard_map/ppermute | solution.py:733
  14.1 5.8 %copy-start.2 = (f32[24,1024]{1,0:T(8,128)}, f32[24,1024]{1,0:T(8,128)S(1)}, u32[]{:S(2)}) copy-start(f32[24,1024]{1,0:T(8,128)S(1)} %collective-permute-done.refs_7_.refs_3_.refs_8_) | copy-start | bytes 294916
  14.5 5.4 %copy-start.4 = (f32[24,1024]{1,0:T(8,128)}, f32[24,1024]{1,0:T(8,128)S(1)}, u32[]{:S(2)}) copy-start(f32[24,1024]{1,0:T(8,128)S(1)} %collective-permute-done.1.refs_8_.refs_4_.refs_9_) | copy-start | bytes 294916
  19.9 32.2 %all-to-all-start = ((f32[32,64,128]{2,1,0:T(8,128)}), f32[32,64,128]{2,1,0:T(8,128)S(1)}, u32[]{:S(2)}, u32[]{:S(2)}) async-start(f32[32,64,128]{2,1,0:T(8,128)} %get-tuple-element.55), calls=%async_computation | async-start | bytes 2097152 | tf_op jit(solution)/shard_map/all_to_all | solution.py:769
  26.5 25.6 %copy-start.12 = (bf16[1024,256]{1,0:T(8,128)(2,1)S(1)}, bf16[1024,256]{1,0:T(8,128)(2,1)}, u32[]{:S(2)}) copy-start(bf16[1024,256]{1,0:T(8,128)(2,1)} %constant.42.clone.refs_4_) | copy-start | bytes 1572868
  26.5 25.6 %copy-start.13 = (bf16[256,48]{1,0:T(8,128)(2,1)S(1)}, bf16[256,48]{1,0:T(8,128)(2,1)}, u32[]{:S(2)}) copy-start(bf16[256,48]{1,0:T(8,128)(2,1)} %constant.43.clone.refs_5_) | copy-start | bytes 73732
  29.5 9.6 %collective-permute-start.2 = (f32[48,640]{1,0:T(8,128)}, f32[48,640]{1,0:T(8,128)S(1)}, u32[]{:S(2)}, u32[]{:S(2)}) collective-permute-start(f32[48,640]{1,0:T(8,128)} %get-tuple-element.36), channel_id=1, source_target_pairs={{0,8},{8,16},{16,24},{24,0},{1,9},{9,17},{17,25},{25,1},{2,10},{10... | collective-permute-start | bytes 368648 | tf_op jit(solution)/shard_map/ppermute | solution.py:733
  29.7 9.4 %collective-permute-start.3 = (f32[48,640]{1,0:T(8,128)}, f32[48,640]{1,0:T(8,128)S(1)}, u32[]{:S(2)}, u32[]{:S(2)}) collective-permute-start(f32[48,640]{1,0:T(8,128)} %get-tuple-element.37), channel_id=1, source_target_pairs={{0,24},{8,0},{16,8},{24,16},{1,25},{9,1},{17,9},{25,17},{2,26},{10... | collective-permute-start | bytes 368648 | tf_op jit(solution)/shard_map/ppermute | solution.py:733
  39.1 0.7 copy-start.18
  39.1 0.7 copy-start.19
  56.9 21.5 %all-to-all-start.1 = ((f32[32,40,128]{2,1,0:T(8,128)}), f32[32,40,128]{2,1,0:T(8,128)S(1)}, u32[]{:S(2)}, u32[]{:S(2)}) async-start(f32[32,40,128]{2,1,0:T(8,128)} %solve_y.1), calls=%async_computation.1 | async-start | bytes 1310720 | tf_op jit(solution)/shard_map/all_to_all | solution.py:792
  60.5 17.9 %copy-start.10 = (bf16[1536,512]{1,0:T(8,128)(2,1)S(1)}, bf16[1536,512]{1,0:T(8,128)(2,1)}, u32[]{:S(2)}) copy-start(bf16[1536,512]{1,0:T(8,128)(2,1)} %constant.44.clone.refs_2_) | copy-start | bytes 4718596
  74.0 8.6 %copy-start.1 = (bf16[512,256]{1,0:T(8,128)(2,1)S(1)}, bf16[512,256]{1,0:T(8,128)(2,1)}, u32[]{:S(2)}) copy-start(bf16[512,256]{1,0:T(8,128)(2,1)} %constant.36.clone.refs_11_.refs_6_) | copy-start | bytes 786436
  74.0 8.6 %copy-start.3 = (f32[24,1024]{1,0:T(8,128)S(1)}, f32[24,1024]{1,0:T(8,128)}, u32[]{:S(2)}) copy-start(f32[24,1024]{1,0:T(8,128)} %copy-done.2) | copy-start | bytes 294916
  74.0 8.6 %copy-start.5 = (f32[24,1024]{1,0:T(8,128)S(1)}, f32[24,1024]{1,0:T(8,128)}, u32[]{:S(2)}) copy-start(f32[24,1024]{1,0:T(8,128)} %copy-done.4) | copy-start | bytes 294916
  74.0 8.6 %copy-start.7 = (bf16[144,144]{1,0:T(8,128)(2,1)S(1)}, bf16[144,144]{1,0:T(8,128)(2,1)}, u32[]{:S(2)}) copy-start(bf16[144,144]{1,0:T(8,128)(2,1)} %constant.37.clone.refs_12_) | copy-start | bytes 124420
  74.0 8.6 %copy-start.8 = (bf16[128,144]{1,0:T(8,128)(2,1)S(1)}, bf16[128,144]{1,0:T(8,128)(2,1)}, u32[]{:S(2)}) copy-start(bf16[128,144]{1,0:T(8,128)(2,1)} %constant.38.clone.refs_13_) | copy-start | bytes 110596
  74.0 8.6 %copy-start.9 = (f32[4]{0:T(128)S(1)}, f32[4]{0:T(128)}, u32[]{:S(2)}) copy-start(f32[4]{0:T(128)} %add_convert_fusion.refs_0_) | copy-start | bytes 52
  80.0 0.7 copy-start.6
  80.7 8.5 %collective-permute-start.7 = (f32[72,640]{1,0:T(8,128)S(1)}, f32[72,640]{1,0:T(8,128)S(1)}, u32[]{:S(2)}, u32[]{:S(2)}) collective-permute-start(f32[72,640]{1,0:T(8,128)S(1)} %get-tuple-element.58), channel_id=1, source_target_pairs={{0,8},{8,0},{16,24},{24,16},{1,9},{9,1},{17,25},{25,17},{2,10},{10... | collective-permute-start | bytes 552968 | tf_op jit(solution)/shard_map/ppermute | solution.py:737
  80.8 8.4 %collective-permute-start.8 = (f32[72,640]{1,0:T(8,128)S(1)}, f32[72,640]{1,0:T(8,128)S(1)}, u32[]{:S(2)}, u32[]{:S(2)}) collective-permute-start(f32[72,640]{1,0:T(8,128)S(1)} %get-tuple-element.59), channel_id=1, source_target_pairs={{0,16},{8,24},{16,0},{24,8},{1,17},{9,25},{17,1},{25,9},{2,18},{10... | collective-permute-start | bytes 552968 | tf_op jit(solution)/shard_map/ppermute | solution.py:737
  82.4 8.9 %collective-permute-start.9 = (f32[72,640]{1,0:T(8,128)S(1)}, f32[72,640]{1,0:T(8,128)S(1)}, u32[]{:S(2)}, u32[]{:S(2)}) collective-permute-start(f32[72,640]{1,0:T(8,128)S(1)} %get-tuple-element.60), channel_id=1, source_target_pairs={{0,24},{8,16},{16,8},{24,0},{1,25},{9,17},{17,9},{25,1},{2,26},{10... | collective-permute-start | bytes 552968 | tf_op jit(solution)/shard_map/ppermute | solution.py:737
  89.2 2.1 %copy-start.15 = (f32[72,640]{1,0:T(8,128)}, f32[72,640]{1,0:T(8,128)S(1)}, u32[]{:S(2)}) copy-start(f32[72,640]{1,0:T(8,128)S(1)} %collective-permute-done.7.refs_9_) | copy-start | bytes 552964
  89.2 2.0 %copy-start.16 = (f32[72,640]{1,0:T(8,128)}, f32[72,640]{1,0:T(8,128)S(1)}, u32[]{:S(2)}) copy-start(f32[72,640]{1,0:T(8,128)S(1)} %collective-permute-done.8.refs_10_) | copy-start | bytes 552964
  91.3 0.7 copy-start.17
where the time goes:
time: 102 us; the launch traced here: 101 us
  Pallas kernels  49.8 us (49%)
  waiting for transfers between devices  26 us (25%)
  starting transfers between devices  21.1 us (21%)
  local copies, waits for them, and re-layouts  2.77 us (3%)
  other arithmetic  1.28 us (1%)
    pallas_call x11, Pallas kernels, call(): pl.pallas_call(body, out_shape=outs, in_specs=in_specs + [pl.BlockSpec(me...  49.8 us
    all_to_all x1, waiting for transfers between devices, pressure_lines(): spectra = lax.all_to_all(spectra, ('gy', 'gx'), 0, 0, tiled=True)  8.48 us
    ppermute x4, waiting for transfers between devices, ring(): lax.ppermute(array, axis, [(i, (i + step) % size) for i in range(size)])  7.72 us
    ppermute x4, starting transfers between devices, ring(): lax.ppermute(array, axis, [(i, (i + step) % size) for i in range(size)])  6.54 us
    all_to_all x1, starting transfers between devices, pressure_lines(): spectra = lax.all_to_all(spectra, ('gy', 'gx'), 0, 0, tiled=True)  5.93 us
    ppermute x6, waiting for transfers between devices, swap(): lax.ppermute(array, axis, [(i, i ^ mask) for i in range(lax.axis_size(axi...  5.37 us
    ppermute x6, starting transfers between devices, swap(): lax.ppermute(array, axis, [(i, i ^ mask) for i in range(lax.axis_size(axi...  5.04 us
    all_to_all x1, waiting for transfers between devices, pressure_lines(): solved = lax.all_to_all(solved, ('gy', 'gx'), 0, 0, tiled=True)  4.4 us
  transfers between devices with their start and end apart: 12, of which 7 were waited for; matrix products, arithmetic and copies ran while one was open for 2% of the time, Pallas kernels for 29%

commit v1 on v0

--- a/solution.py
+++ b/solution.py
@@ -151,9 +151,8 @@
             piece[c] = velocity[c, 0, pl.ds(start, rows), :]
 
 
-def rows_kernel(place, top, low, top_wall, low_wall, top_flow, low_flow, first, last, mark):
+def rows_kernel(top, low, top_wall, low_wall, top_flow, low_flow, first, last):
     small, width = top.shape[2], top_flow.shape[3]
-    mark[0] = place[0]
     first[...] = jnp.zeros(first.shape, F32)
     last[...] = jnp.zeros(last.shape, F32)
     for k, (start, rows) in STRIP.items():
@@ -640,7 +639,7 @@
         )
         for mask, piece in enumerate(lines)
     ]
-    for copy in pieces + copies[:2]:
+    for copy in (*pieces, *copies, *tile_copies(0), *tile_copies(1)):
         copy.start()
     for copy in pieces + copies[:1]:
         copy.wait()
@@ -653,8 +652,6 @@
         after, before = lane_tile(level, (k + 1) % count), lane_tile(level, (k - 1) % count)
         around.append(split(jnp.concatenate([lane_tile(level, k), jnp.where(near, after, before)], axis=1)))
     copies[1].wait()
-    for copy in (copies[2], *tile_copies(0), copies[3], *tile_copies(1)):
-        copy.start()
     for k in range(count):
         lanes = 2 * LANES if k < count - 1 else LANES
         value = split(exact_dot(around[k], split(matrix[k][:, :lanes])))
@@ -824,28 +821,9 @@
         return pl.BlockSpec(block, lambda i: index)
 
     own = place_x.astype(jnp.int32).reshape(1)
-    first, last, cut = call(
-        rows_kernel,
-        (own, acoustic, acoustic, wall_mask, wall_mask, velocity, velocity),
-        (shaped(STRIP_ROWS, wide),) * 2 + (shaped(1, kind=jnp.int32),),
-        steps=1,
-        specs={
-            0: scalars,
-            1: at((parts, 1, small, wide), 0, 0, 0, 0),
-            2: at((parts, 1, small, wide), 0, 0, tall // small - 1, 0),
-            3: at((1, HALO, wide), 0, 0, 0),
-            4: at((1, HALO, wide), 0, tall // HALO - 1, 0),
-            5: at((1, 1, HALO, local_x), 1, 0, 0, 0),
-            6: at((1, 1, HALO, local_x), 1, 0, local_y // HALO - 1, 0),
-        },
-        out_specs=(at((STRIP_ROWS, wide), 0, 0),) * 2 + (scalars,),
-        moved=2 << 20,
-        megabytes=54,
-        name="rows",
-    )
     sent = call(
         pieces_kernel,
-        (cut, velocity),
+        (own, velocity),
         (shaped(2, local_y // count_x, local_x),) * count_x,
         specs={0: scalars},
         moved=2 << 20,
@@ -853,6 +831,24 @@
         name="pieces",
     )
     moved = [piece if mask == 0 else swap(piece, "gx", mask) for mask, piece in enumerate(sent)]
+    first, last = call(
+        rows_kernel,
+        (acoustic, acoustic, wall_mask, wall_mask, velocity, velocity),
+        (shaped(STRIP_ROWS, wide),) * 2,
+        steps=1,
+        specs={
+            0: at((parts, 1, small, wide), 0, 0, 0, 0),
+            1: at((parts, 1, small, wide), 0, 0, tall // small - 1, 0),
+            2: at((1, HALO, wide), 0, 0, 0),
+            3: at((1, HALO, wide), 0, tall // HALO - 1, 0),
+            4: at((1, 1, HALO, local_x), 1, 0, 0, 0),
+            5: at((1, 1, HALO, local_x), 1, 0, local_y // HALO - 1, 0),
+        },
+        after=moved[1:2],
+        moved=2 << 20,
+        megabytes=50,
+        name="rows",
+    )
     above, below = ring(last, "gy", 1), ring(first, "gy", -1)
     to_right, to_left = call(
         columns_kernel,
@@ -956,7 +952,7 @@
             ),
             after=before,
             aliases={len(operands) + k: k for k in range(len(before))},
-            megabytes=54 if first == 0 else 53,
+            megabytes=54,
             flops=3 * 10**9 * count,
             moved=(12 << 20) * count,
             name="quiet_step",
@@ -993,7 +989,7 @@
         specs={0: scalars, **specs},
         out_specs=anywhere,
         aliases={7: 0},
-        megabytes=55,
+        megabytes=56,
         flops=4 * 10**9,
         moved=16 << 20,
         name="source_step",

time: 102 us -> 99.9 us (0.979)
  local copies, waits for them, and re-layouts: 2.77 us -> 6.79 us
  waiting for transfers between devices: 26 us -> 22.4 us
  Pallas kernels: 49.8 us -> 47.7 us
    unnamed x40 -> x32, local copies, waits for them, and re-layouts: 2.08 us -> 6.09 us
    ppermute x4, waiting for transfers between devices: 7.72 us -> 4.13 us  [ring(): lax.ppermute(array, axis, [(i, (i + step) % size) for i in range(size)])]
    pallas_call x11, Pallas kernels: 49.8 us -> 47.7 us  [call(): pl.pallas_call(body, out_shape=outs, in_specs=in_specs + [pl.BlockSpec(me...]
  transfers between devices with their start and end apart: 12 -> 12, of which waited for: 7 -> 6; matrix products, arithmetic and copies ran while one was open for 2% -> 2% of each run, Pallas kernels for 29% -> 31%
where the time goes in v1:
time: 99.9 us; the launch traced here: 99.3 us
  Pallas kernels  47.7 us (48%)
  waiting for transfers between devices  22.4 us (22%)
  starting transfers between devices  20.8 us (21%)
  local copies, waits for them, and re-layouts  6.79 us (7%)
  other arithmetic  1.25 us (1%)
    pallas_call x11, Pallas kernels, call(): pl.pallas_call(body, out_shape=outs, in_specs=in_specs + [pl.BlockSpec(me...  47.7 us
    all_to_all x1, waiting for transfers between devices, pressure_lines(): spectra = lax.all_to_all(spectra, ('gy', 'gx'), 0, 0, tiled=True)  8.55 us
    ppermute x4, starting transfers between devices, ring(): lax.ppermute(array, axis, [(i, (i + step) % size) for i in range(size)])  6.66 us
    unnamed x32, local copies, waits for them, and re-layouts  6.09 us
    all_to_all x1, starting transfers between devices, pressure_lines(): spectra = lax.all_to_all(spectra, ('gy', 'gx'), 0, 0, tiled=True)  5.52 us
    ppermute x6, waiting for transfers between devices, swap(): lax.ppermute(array, axis, [(i, i ^ mask) for i in range(lax.axis_size(axi...  5.32 us
    ppermute x6, starting transfers between devices, swap(): lax.ppermute(array, axis, [(i, i ^ mask) for i in range(lax.axis_size(axi...  5.03 us
    all_to_all x1, waiting for transfers between devices, pressure_lines(): solved = lax.all_to_all(solved, ('gy', 'gx'), 0, 0, tiled=True)  4.43 us
  transfers between devices with their start and end apart: 12, of which 6 were waited for; matrix products, arithmetic and copies ran while one was open for 2% of the time, Pallas kernels for 31%

profile of v1, /device:TPU:0, one launch (start us, length us, event | category | flops | bytes accessed | tf_op | source)
XLA Modules:
  0.0 99.3 jit_solution(5525782124810256344)
XLA Ops:
  0.0 1.2 %copy-done.1 = f32[2,1,256,512]{3,2,1,0:T(8,128)S(1)} copy-done((f32[2,1,256,512]{3,2,1,0:T(8,128)S(1)}, f32[2,1,256,512]{3,2,1,0:T(8,128)}, u32[]{:S(2)}) %copy-start.1) | copy-done | bytes 1048600
  1.2 0.1 pieces.1
  1.3 0.5 collective-permute-start
  1.8 2.6 %collective-permute-start.5 = (f32[2,64,512]{2,1,0:T(8,128)S(1)}, f32[2,64,512]{2,1,0:T(8,128)S(1)}, u32[]{:S(2)}, u32[]{:S(2)}) collective-permute-start(f32[2,64,512]{2,1,0:T(8,128)S(1)} %get-tuple-element.51), channel_id=1, source_target_pairs={{0,16},{8,24},{16,0},{24,8},{1,17},{9,25},{17,1},{25,9},{2,18},{10... | collective-permute-start | bytes 786440 | tf_op jit(solution)/shard_map/ppermute | solution.py:734
  4.4 0.1 collective-permute-start.6
  4.5 0.0 collective-permute-done.refs_6_.refs_2_
  4.5 1.6 %copy-done = s32[1,512,1024]{2,1,0:T(8,128)S(1)} copy-done((s32[1,512,1024]{2,1,0:T(8,128)S(1)}, s32[1,512,1024]{2,1,0:T(8,128)}, u32[]{:S(2)}) %copy-start) | copy-done | bytes 2097176
  6.0 1.2 %copy-done.2 = f32[2,1,256,512]{3,2,1,0:T(8,128)S(1)} copy-done((f32[2,1,256,512]{3,2,1,0:T(8,128)S(1)}, f32[2,1,256,512]{3,2,1,0:T(8,128)}, u32[]{:S(2)}) %copy-start.2) | copy-done | bytes 1048600
  7.3 1.1 %rows.1 = (f32[24,1024]{1,0:T(8,128)S(1)}, f32[24,1024]{1,0:T(8,128)S(1)}) custom-call(bf16[4,1,512,1024]{3,2,1,0:T(8,128)(2,1)} %refs_4_.8, bf16[4,1,512,1024]{3,2,1,0:T(8,128)(2,1)} %refs_4_.8, s32[1,512,1024]{2,1,0:T(8,128)S(1)} %copy-done, s32[1,512,1024]{2,1,0:T(8,128)S(1)} %copy-done, f32[2,1,256,512]{3,2,1,0:T(8,128)S(1)} %copy-done.2, ...), custom_call_target="tpu_custom_call" | custom-call | bytes 2097152 | tf_op jit(solution)/shard_map/rows/pallas_call | solution.py:715
  8.4 1.8 %collective-permute-start.1 = (f32[24,1024]{1,0:T(8,128)S(1)}, f32[24,1024]{1,0:T(8,128)S(1)}, u32[]{:S(2)}, u32[]{:S(2)}) collective-permute-start(f32[24,1024]{1,0:T(8,128)S(1)} %get-tuple-element.34), channel_id=1, source_target_pairs={{0,1},{1,2},{2,3},{3,4},{4,5},{5,6},{6,7},{7,0},{8,9},{9,10},{10,1... | collective-permute-start | bytes 294920 | tf_op jit(solution)/shard_map/ppermute | solution.py:730
  10.2 3.1 %collective-permute-start.2 = (f32[24,1024]{1,0:T(8,128)S(1)}, f32[24,1024]{1,0:T(8,128)S(1)}, u32[]{:S(2)}, u32[]{:S(2)}) collective-permute-start(f32[24,1024]{1,0:T(8,128)S(1)} %get-tuple-element.35), channel_id=1, source_target_pairs={{0,7},{1,0},{2,1},{3,2},{4,3},{5,4},{6,5},{7,6},{8,15},{9,8},{10,9... | collective-permute-start | bytes 294920 | tf_op jit(solution)/shard_map/ppermute | solution.py:730
  13.3 0.0 collective-permute-done.5.refs_3_
  13.3 3.3 %collective-permute-done.6.refs_4_ = f32[2,64,512]{2,1,0:T(8,128)S(1)} collective-permute-done((f32[2,64,512]{2,1,0:T(8,128)S(1)}, f32[2,64,512]{2,1,0:T(8,128)S(1)}, u32[]{:S(2)}, u32[]{:S(2)}) %collective-permute-start.6) | collective-permute-done | bytes 262176 | tf_op jit(solution)/shard_map/ppermute | solution.py:734
  16.6 0.0 collective-permute-done.1.refs_7_.refs_3_.refs_8_
  16.7 0.4 collective-permute-done.2.refs_8_.refs_4_.refs_9_
  17.1 2.0 %forward_x.1 = (f32[32,64,128]{2,1,0:T(8,128)}, f32[8,128]{1,0:T(8,128)S(1)}) custom-call(s32[1]{0:T(128)} %bitcast.refs_0_.refs_1_, f32[2,64,512]{2,1,0:T(8,128)S(1)} %get-tuple-element.50.refs_1_, f32[2,64,512]{2,1,0:T(8,128)S(1)} %collective-permute-done.refs_6_.refs_2_, f32[2,64,512]{2,1,0:T(8,128)S(1)} %collective-permute-done.5.refs_3_, ...), custom_call_target="tpu_custom_call" | custom-call | flops 1000000000 | bytes 4194304 | tf_op jit(solution)/shard_map/forward_x/pallas_call | solution.py:715
  19.2 5.5 %all-to-all-start = ((f32[32,64,128]{2,1,0:T(8,128)}), f32[32,64,128]{2,1,0:T(8,128)S(1)}, u32[]{:S(2)}, u32[]{:S(2)}) async-start(f32[32,64,128]{2,1,0:T(8,128)} %get-tuple-element.53), calls=%async_computation | async-start | bytes 2097152 | tf_op jit(solution)/shard_map/all_to_all | solution.py:766
  24.7 0.7 add_convert_fusion.refs_0_
  25.4 3.0 %columns.1 = (f32[48,640]{1,0:T(8,128)}, f32[48,640]{1,0:T(8,128)}) custom-call(f32[4]{0:T(128)} %add_convert_fusion.refs_0_, bf16[4,1,512,1024]{3,2,1,0:T(8,128)(2,1)} %refs_4_.8, bf16[4,1,512,1024]{3,2,1,0:T(8,128)(2,1)} %refs_4_.8, s32[1,512,1024]{2,1,0:T(8,128)} %refs_7_.3, s32[1,512,1024]{2,1,0:T(8,128)} %refs_7_.3, f32[2,1,256,512]{3,2,1,0:T(8,128)} %refs_2_.10, ...), custom_call_target="tpu_custom_call" | custom-call | bytes 8388608 | tf_op jit(solution)/shard_map/columns/pallas_call | solution.py:715
  28.3 0.3 collective-permute-start.3
  28.6 1.5 %collective-permute-start.4 = (f32[48,640]{1,0:T(8,128)}, f32[48,640]{1,0:T(8,128)S(1)}, u32[]{:S(2)}, u32[]{:S(2)}) collective-permute-start(f32[48,640]{1,0:T(8,128)} %get-tuple-element.37), channel_id=1, source_target_pairs={{0,24},{8,0},{16,8},{24,16},{1,25},{9,1},{17,9},{25,17},{2,26},{10... | collective-permute-start | bytes 368648 | tf_op jit(solution)/shard_map/ppermute | solution.py:730
  30.1 0.6 pad_add_fusion.refs_0_
  30.7 2.9 %tables.1 = (f32[5,256,256]{2,1,0:T(8,128)}, f32[4,144,240]{2,1,0:T(8,128)}, s32[1]{0:T(128)}) custom-call(s32[2]{0:T(128)} %pad_add_fusion.refs_0_, f32[4,4096]{1,0:T(4,128)} %refs_1_.4, f32[4,4096]{1,0:T(4,128)} %refs_2_.7), custom_call_target="tpu_custom_call" | custom-call | bytes 4194304 | tf_op jit(solution)/shard_map/tables/pallas_call | solution.py:715
  33.5 0.7 constant_dynamic-slice_fusion.refs_3_
  34.2 3.7 %collective-permute-done.3.refs_5_ = f32[48,640]{1,0:T(8,128)S(1)} collective-permute-done((f32[48,640]{1,0:T(8,128)}, f32[48,640]{1,0:T(8,128)S(1)}, u32[]{:S(2)}, u32[]{:S(2)}) %collective-permute-start.3) | collective-permute-done | bytes 122912 | tf_op jit(solution)/shard_map/ppermute | solution.py:730
  37.9 0.0 collective-permute-done.4.refs_6_
  37.9 0.6 copy-done.14
  38.6 0.0 copy-done.15
  38.6 3.8 %sides.1 = (f32[5,640,128]{2,1,0:T(8,128)}, f32[272,640]{1,0:T(8,128)}, s32[1]{0:T(128)}) custom-call(f32[4]{0:T(128)} %add_convert_fusion.refs_0_, s32[1]{0:T(128)} %get-tuple-element.32.refs_1_, f32[2,1,256,512]{3,2,1,0:T(8,128)} %refs_2_.10, f32[24,1024]{1,0:T(8,128)} %copy-done.3, f32[24,1024]{1,0:T(8,128)} %copy-done.4, f32[48,640]{1,0:T(8,128)} %copy-done.14, ...), custom_call_target="tpu_custom_call" | custom-call | bytes 8388608 | tf_op jit(solution)/shard_map/sides/pallas_call | solution.py:715
  42.4 8.5 %all-to-all-done.refs_1_ = f32[32,64,128]{2,1,0:T(8,128)S(1)} async-done(((f32[32,64,128]{2,1,0:T(8,128)}), f32[32,64,128]{2,1,0:T(8,128)S(1)}, u32[]{:S(2)}, u32[]{:S(2)}) %all-to-all-start) | async-done | bytes 1048608 | tf_op jit(solution)/shard_map/all_to_all | solution.py:766
  50.9 0.0 copy-done.8
  50.9 4.9 %solve_y.1 = f32[32,40,128]{2,1,0:T(8,128)} custom-call(s32[1]{0:T(128)} %get-tuple-element.49.refs_0_, f32[32,64,128]{2,1,0:T(8,128)S(1)} %all-to-all-done.refs_1_, f32[8,128]{1,0:T(8,128)S(1)} %get-tuple-element.54.refs_2_, f32[1,128]{1,0:T(1,128)S(1)} %constant_dynamic-slice_fusion.refs_3_, bf16[1024,256]{1,0:T(8,128)(2,1)S(1)} %copy-done.8, ...), custom_call_target="tpu_custom_call" | custom-call | flops 4000000000 | bytes 6291456 | tf_op jit(solution)/shard_map/solve_y/pallas_call | solution.py:715
  55.8 3.6 %all-to-all-start.1 = ((f32[32,40,128]{2,1,0:T(8,128)}), f32[32,40,128]{2,1,0:T(8,128)S(1)}, u32[]{:S(2)}, u32[]{:S(2)}) async-start(f32[32,40,128]{2,1,0:T(8,128)} %solve_y.1), calls=%async_computation.1 | async-start | bytes 1310720 | tf_op jit(solution)/shard_map/all_to_all | solution.py:789
  59.4 0.0 copy-start.6
  59.5 13.5 %quiet_step.2 = (f32[3,512,1024]{2,1,0:T(8,128)}, bf16[4,1,512,1024]{3,2,1,0:T(8,128)(2,1)}, bf16[4,144,1152]{2,1,0:T(8,128)(2,1)}, s32[1]{0:T(128)}) custom-call(f32[4]{0:T(128)} %add_convert_fusion.refs_0_, s32[1]{0:T(128)} %bitcast.refs_0_.refs_1_, bf16[4,1,512,1024]{3,2,1,0:T(8,128)(2,1)} %refs_4_.8, bf16[4,1,512,1024]{3,2,1,0:T(8,128)(2,1)} %refs_4_.8, ...), custom_call_target="tpu_custom_call" | custom-call | flops 8999999488 | bytes 37748736 | tf_op jit(solution)/shard_map/quiet_step/pallas_call | solution.py:715
  72.9 4.4 %all-to-all-done.1.refs_1_ = f32[32,40,128]{2,1,0:T(8,128)S(1)} async-done(((f32[32,40,128]{2,1,0:T(8,128)}), f32[32,40,128]{2,1,0:T(8,128)S(1)}, u32[]{:S(2)}, u32[]{:S(2)}) %all-to-all-start.1) | async-done | bytes 655392 | tf_op jit(solution)/shard_map/all_to_all | solution.py:789
  77.4 1.4 %inverse_x.1 = (f32[72,640]{1,0:T(8,128)S(1)}, f32[72,640]{1,0:T(8,128)S(1)}, f32[72,640]{1,0:T(8,128)S(1)}, f32[72,640]{1,0:T(8,128)S(1)}) custom-call(s32[1]{0:T(128)} %get-tuple-element.48.refs_0_, f32[32,40,128]{2,1,0:T(8,128)S(1)} %all-to-all-done.1.refs_1_, bf16[1536,512]{1,0:T(8,128)(2,1)S(1)} %copy-done.6, f32[8,256]{1,0:T(8,128)S(1)} %copy-done.10), custom_call_target="tpu_custom_call" | custom-call | flops 1000000000 | bytes 4194304 | tf_op jit(solution)/shard_map/inverse_x/pallas_call | solution.py:715
  78.8 0.0 copy-start.5
  78.8 0.7 copy-done.5
  79.5 0.1 collective-permute-start.7
  79.5 1.6 %collective-permute-start.8 = (f32[72,640]{1,0:T(8,128)S(1)}, f32[72,640]{1,0:T(8,128)S(1)}, u32[]{:S(2)}, u32[]{:S(2)}) collective-permute-start(f32[72,640]{1,0:T(8,128)S(1)} %get-tuple-element.57), channel_id=1, source_target_pairs={{0,16},{8,24},{16,0},{24,8},{1,17},{9,25},{17,1},{25,9},{2,18},{10... | collective-permute-start | bytes 552968 | tf_op jit(solution)/shard_map/ppermute | solution.py:734
  81.1 0.2 collective-permute-start.9
  81.3 6.6 %quiet_step.3 = (f32[3,512,1024]{2,1,0:T(8,128)}, bf16[4,1,512,1024]{3,2,1,0:T(8,128)(2,1)}, bf16[4,144,1152]{2,1,0:T(8,128)(2,1)}, s32[1]{0:T(128)}) custom-call(f32[4]{0:T(128)} %add_convert_fusion.refs_0_, s32[1]{0:T(128)} %bitcast.refs_0_.refs_1_, ...), custom_call_target="tpu_custom_call", output_to_operand_aliasing={{0}: (14, {}), {1}: (15, {}), {2}: (16, {})} | custom-call | flops 3000000000 | bytes 12582912 | tf_op jit(solution)/shard_map/quiet_step/pallas_call | solution.py:715
  88.0 0.0 collective-permute-done.7.refs_9_
  88.0 0.0 collective-permute-done.8.refs_10_
  88.0 2.0 %collective-permute-done.9.refs_11_ = f32[72,640]{1,0:T(8,128)S(1)} collective-permute-done((f32[72,640]{1,0:T(8,128)S(1)}, f32[72,640]{1,0:T(8,128)S(1)}, u32[]{:S(2)}, u32[]{:S(2)}) %collective-permute-start.9) | collective-permute-done | bytes 184352 | tf_op jit(solution)/shard_map/ppermute | solution.py:734
  90.0 0.7 copy-done.13
  90.7 8.4 %source_step.1 = bf16[4,1,512,1024]{3,2,1,0:T(8,128)(2,1)} custom-call(s32[1]{0:T(128)} %bitcast.refs_0_.refs_1_, f32[272,640]{1,0:T(8,128)} %get-tuple-element.38.refs_1_, bf16[4,144,1152]{2,1,0:T(8,128)(2,1)} %get-tuple-element.43.refs_2_, f32[5,256,256]{2,1,0:T(8,128)} %get-tuple-element.44.refs_3_, ...), custom_call_target="tpu_custom_call", output_to_operand_aliasing={{}: (7, {})} | custom-call | flops 4000000000 | bytes 16777216 | tf_op jit(solution)/shard_map/source_step/pallas_call | solution.py:715
  (22 shorter events, 0.0 us)
Async XLA Ops:
  0.0 1.2 %copy-start.1 = (f32[2,1,256,512]{3,2,1,0:T(8,128)S(1)}, f32[2,1,256,512]{3,2,1,0:T(8,128)}, u32[]{:S(2)}) copy-start(f32[2,1,256,512]{3,2,1,0:T(8,128)} %refs_2_.10) | copy-start | bytes 3145732
  1.3 3.2 %collective-permute-start = (f32[2,64,512]{2,1,0:T(8,128)S(1)}, f32[2,64,512]{2,1,0:T(8,128)S(1)}, u32[]{:S(2)}, u32[]{:S(2)}) collective-permute-start(f32[2,64,512]{2,1,0:T(8,128)S(1)} %get-tuple-element.33), channel_id=1, source_target_pairs={{0,8},{8,0},{16,24},{24,16},{1,9},{9,1},{17,25},{25,17},{2,10},{10... | collective-permute-start | bytes 786440 | tf_op jit(solution)/shard_map/ppermute | solution.py:734
  1.8 11.5 %collective-permute-start.5 = (f32[2,64,512]{2,1,0:T(8,128)S(1)}, f32[2,64,512]{2,1,0:T(8,128)S(1)}, u32[]{:S(2)}, u32[]{:S(2)}) collective-permute-start(f32[2,64,512]{2,1,0:T(8,128)S(1)} %get-tuple-element.51), channel_id=1, source_target_pairs={{0,16},{8,24},{16,0},{24,8},{1,17},{9,25},{17,1},{25,9},{2,18},{10... | collective-permute-start | bytes 786440 | tf_op jit(solution)/shard_map/ppermute | solution.py:734
  4.4 12.3 %collective-permute-start.6 = (f32[2,64,512]{2,1,0:T(8,128)S(1)}, f32[2,64,512]{2,1,0:T(8,128)S(1)}, u32[]{:S(2)}, u32[]{:S(2)}) collective-permute-start(f32[2,64,512]{2,1,0:T(8,128)S(1)} %get-tuple-element.52), channel_id=1, source_target_pairs={{0,24},{8,16},{16,8},{24,0},{1,25},{9,17},{17,9},{25,1},{2,26},{10... | collective-permute-start | bytes 786440 | tf_op jit(solution)/shard_map/ppermute | solution.py:734
  4.5 1.6 %copy-start = (s32[1,512,1024]{2,1,0:T(8,128)S(1)}, s32[1,512,1024]{2,1,0:T(8,128)}, u32[]{:S(2)}) copy-start(s32[1,512,1024]{2,1,0:T(8,128)} %refs_7_.3) | copy-start | bytes 6291460
  6.0 1.2 %copy-start.2 = (f32[2,1,256,512]{3,2,1,0:T(8,128)S(1)}, f32[2,1,256,512]{3,2,1,0:T(8,128)}, u32[]{:S(2)}) copy-start(f32[2,1,256,512]{3,2,1,0:T(8,128)} %refs_2_.10) | copy-start | bytes 3145732
  7.3 9.8 %copy-start.7 = (bf16[1536,512]{1,0:T(8,128)(2,1)S(1)}, bf16[1536,512]{1,0:T(8,128)(2,1)}, u32[]{:S(2)}) copy-start(bf16[1536,512]{1,0:T(8,128)(2,1)} %constant.39.clone.refs_5_) | copy-start | bytes 4718596
  7.3 9.8 %copy-start.10 = (f32[8,256]{1,0:T(8,128)S(1)}, f32[8,256]{1,0:T(8,128)}, u32[]{:S(2)}) copy-start(f32[8,256]{1,0:T(8,128)} %constant.40.clone.refs_6_.refs_3_) | copy-start | bytes 24580
  8.4 8.3 %collective-permute-start.1 = (f32[24,1024]{1,0:T(8,128)S(1)}, f32[24,1024]{1,0:T(8,128)S(1)}, u32[]{:S(2)}, u32[]{:S(2)}) collective-permute-start(f32[24,1024]{1,0:T(8,128)S(1)} %get-tuple-element.34), channel_id=1, source_target_pairs={{0,1},{1,2},{2,3},{3,4},{4,5},{5,6},{6,7},{7,0},{8,9},{9,10},{10,1... | collective-permute-start | bytes 294920 | tf_op jit(solution)/shard_map/ppermute | solution.py:730
  10.2 6.9 %collective-permute-start.2 = (f32[24,1024]{1,0:T(8,128)S(1)}, f32[24,1024]{1,0:T(8,128)S(1)}, u32[]{:S(2)}, u32[]{:S(2)}) collective-permute-start(f32[24,1024]{1,0:T(8,128)S(1)} %get-tuple-element.35), channel_id=1, source_target_pairs={{0,7},{1,0},{2,1},{3,2},{4,3},{5,4},{6,5},{7,6},{8,15},{9,8},{10,9... | collective-permute-start | bytes 294920 | tf_op jit(solution)/shard_map/ppermute | solution.py:730
  16.7 2.5 %copy-start.3 = (f32[24,1024]{1,0:T(8,128)}, f32[24,1024]{1,0:T(8,128)S(1)}, u32[]{:S(2)}) copy-start(f32[24,1024]{1,0:T(8,128)S(1)} %collective-permute-done.1.refs_7_.refs_3_.refs_8_) | copy-start | bytes 294916
  17.1 2.1 %copy-start.4 = (f32[24,1024]{1,0:T(8,128)}, f32[24,1024]{1,0:T(8,128)S(1)}, u32[]{:S(2)}) copy-start(f32[24,1024]{1,0:T(8,128)S(1)} %collective-permute-done.2.refs_8_.refs_4_.refs_9_) | copy-start | bytes 294916
  19.2 31.8 %all-to-all-start = ((f32[32,64,128]{2,1,0:T(8,128)}), f32[32,64,128]{2,1,0:T(8,128)S(1)}, u32[]{:S(2)}, u32[]{:S(2)}) async-start(f32[32,64,128]{2,1,0:T(8,128)} %get-tuple-element.53), calls=%async_computation | async-start | bytes 2097152 | tf_op jit(solution)/shard_map/all_to_all | solution.py:766
  25.4 25.6 %copy-start.8 = (bf16[1024,256]{1,0:T(8,128)(2,1)S(1)}, bf16[1024,256]{1,0:T(8,128)(2,1)}, u32[]{:S(2)}) copy-start(bf16[1024,256]{1,0:T(8,128)(2,1)} %constant.42.clone.refs_4_) | copy-start | bytes 1572868
  25.4 25.6 %copy-start.9 = (bf16[256,48]{1,0:T(8,128)(2,1)S(1)}, bf16[256,48]{1,0:T(8,128)(2,1)}, u32[]{:S(2)}) copy-start(bf16[256,48]{1,0:T(8,128)(2,1)} %constant.43.clone.refs_5_) | copy-start | bytes 73732
  28.3 9.6 %collective-permute-start.3 = (f32[48,640]{1,0:T(8,128)}, f32[48,640]{1,0:T(8,128)S(1)}, u32[]{:S(2)}, u32[]{:S(2)}) collective-permute-start(f32[48,640]{1,0:T(8,128)} %get-tuple-element.36), channel_id=1, source_target_pairs={{0,8},{8,16},{16,24},{24,0},{1,9},{9,17},{17,25},{25,1},{2,10},{10... | collective-permute-start | bytes 368648 | tf_op jit(solution)/shard_map/ppermute | solution.py:730
  28.6 9.3 %collective-permute-start.4 = (f32[48,640]{1,0:T(8,128)}, f32[48,640]{1,0:T(8,128)S(1)}, u32[]{:S(2)}, u32[]{:S(2)}) collective-permute-start(f32[48,640]{1,0:T(8,128)} %get-tuple-element.37), channel_id=1, source_target_pairs={{0,24},{8,0},{16,8},{24,16},{1,25},{9,1},{17,9},{25,17},{2,26},{10... | collective-permute-start | bytes 368648 | tf_op jit(solution)/shard_map/ppermute | solution.py:730
  37.9 0.6 copy-start.14
  37.9 0.7 copy-start.15
  55.8 21.5 %all-to-all-start.1 = ((f32[32,40,128]{2,1,0:T(8,128)}), f32[32,40,128]{2,1,0:T(8,128)S(1)}, u32[]{:S(2)}, u32[]{:S(2)}) async-start(f32[32,40,128]{2,1,0:T(8,128)} %solve_y.1), calls=%async_computation.1 | async-start | bytes 1310720 | tf_op jit(solution)/shard_map/all_to_all | solution.py:789
  59.4 17.9 %copy-start.6 = (bf16[1536,512]{1,0:T(8,128)(2,1)S(1)}, bf16[1536,512]{1,0:T(8,128)(2,1)}, u32[]{:S(2)}) copy-start(bf16[1536,512]{1,0:T(8,128)(2,1)} %constant.44.clone.refs_2_) | copy-start | bytes 4718596
  78.8 0.7 copy-start.5
  79.5 8.5 %collective-permute-start.7 = (f32[72,640]{1,0:T(8,128)S(1)}, f32[72,640]{1,0:T(8,128)S(1)}, u32[]{:S(2)}, u32[]{:S(2)}) collective-permute-start(f32[72,640]{1,0:T(8,128)S(1)} %get-tuple-element.56), channel_id=1, source_target_pairs={{0,8},{8,0},{16,24},{24,16},{1,9},{9,1},{17,25},{25,17},{2,10},{10... | collective-permute-start | bytes 552968 | tf_op jit(solution)/shard_map/ppermute | solution.py:734
  79.5 8.5 %collective-permute-start.8 = (f32[72,640]{1,0:T(8,128)S(1)}, f32[72,640]{1,0:T(8,128)S(1)}, u32[]{:S(2)}, u32[]{:S(2)}) collective-permute-start(f32[72,640]{1,0:T(8,128)S(1)} %get-tuple-element.57), channel_id=1, source_target_pairs={{0,16},{8,24},{16,0},{24,8},{1,17},{9,25},{17,1},{25,9},{2,18},{10... | collective-permute-start | bytes 552968 | tf_op jit(solution)/shard_map/ppermute | solution.py:734
  81.1 8.9 %collective-permute-start.9 = (f32[72,640]{1,0:T(8,128)S(1)}, f32[72,640]{1,0:T(8,128)S(1)}, u32[]{:S(2)}, u32[]{:S(2)}) collective-permute-start(f32[72,640]{1,0:T(8,128)S(1)} %get-tuple-element.58), channel_id=1, source_target_pairs={{0,24},{8,16},{16,8},{24,0},{1,25},{9,17},{17,9},{25,1},{2,26},{10... | collective-permute-start | bytes 552968 | tf_op jit(solution)/shard_map/ppermute | solution.py:734
  88.0 2.0 %copy-start.11 = (f32[72,640]{1,0:T(8,128)}, f32[72,640]{1,0:T(8,128)S(1)}, u32[]{:S(2)}) copy-start(f32[72,640]{1,0:T(8,128)S(1)} %collective-permute-done.7.refs_9_) | copy-start | bytes 552964
  88.0 2.0 %copy-start.12 = (f32[72,640]{1,0:T(8,128)}, f32[72,640]{1,0:T(8,128)S(1)}, u32[]{:S(2)}) copy-start(f32[72,640]{1,0:T(8,128)S(1)} %collective-permute-done.8.refs_10_) | copy-start | bytes 552964
  90.0 0.7 copy-start.13

commit v2 on v1

--- a/solution.py
+++ b/solution.py
@@ -143,10 +143,11 @@
     return full, (high[:, :base], low[:, :base]), (high[:, base:], low[:, base:])
 
 
-def pieces_kernel(place, velocity, *pieces):
+def pieces_kernel(velocity, *pieces):
     rows = pieces[0].shape[1]
+    place = lax.axis_index("gx")
     for mask, piece in enumerate(pieces):
-        start = pl.multiple_of((place[0] ^ mask) * rows, 8)
+        start = pl.multiple_of((place ^ mask) * rows, 8)
         for c in range(2):
             piece[c] = velocity[c, 0, pl.ds(start, rows), :]
 
@@ -230,11 +231,12 @@
     squares[HALO + rows :, local:] = tile[rows : rows + HALO]
 
 
-def forward_x_kernel(place, *refs):
+def forward_x_kernel(*refs):
     *pieces, tables, turns, out, total, lines, made, sent = refs
     count, _, rows, local = lines.shape
+    place = lax.axis_index("gx")
     for mask, piece in enumerate(pieces):
-        lines[place[0] ^ mask] = piece[...]
+        lines[place ^ mask] = piece[...]
     base = turns.shape[1]
     per = local // base
     u = [lines[t // per, 0, :, (t % per) * base : (t % per + 1) * base] for t in range(RADIX)]
@@ -563,13 +565,13 @@
             density[0, 0] = value.astype(BF16)
         else:
             calm[k - 1] = value
-    shown_open[0] = opened.astype(BF16)
+    shown_open[0] = (time_step * opened).astype(BF16)
     mark[0] = place[0]
 
 
 def tables_kernel(place, weights_x, weights_y, rise_x, rise_y, mark):
     mark[0] = place[0]
-    tiles, reach_x, lanes = rise_x.shape
+    _, tiles, reach_x, lanes = rise_x.shape
     wide, length_x = (tiles - 1) * lanes, weights_x.shape[1]
     first = place[0] * wide
     half = LANES // 2
@@ -592,28 +594,32 @@
         value = jnp.zeros(fine.shape, F32)
         for t in range(4):
             value = jnp.where(cells == (target + t) % reach_x, own[t : t + 1, :], value)
-        rise_x[k] = value
+        rise_x[0, k], rise_x[1, k] = split(value)
     steps, high, reach = rise_y.shape
     tall = steps * TILE
     first = place[1] * tall
     own = [weights(weights_y, first + k * LANES, LANES) for k in range(-1, tall // LANES + 1)]
     own = jnp.concatenate([jnp.concatenate(own, axis=1), jnp.zeros((4, tall + 2 * LANES), F32)], axis=0).T
-    cells = lax.broadcasted_iota(jnp.int32, (high, reach), 1) % (reach // 3)
+    cells = lax.broadcasted_iota(jnp.int32, (high, reach), 1)
+    last = cells >= reach // 3 * 2
+    cells = cells % (reach // 3)
     target = lax.broadcasted_iota(jnp.int32, (high, reach), 0) // 2 + (HALO // 2 - 1)
     for k in range(steps):
         start = LANES - HALO + k * TILE
         value = jnp.zeros((high, reach), F32)
         for t in range(4):
             value = jnp.where(cells == target + t, own[start : start + high, t : t + 1], value)
-        rise_y[k] = value
-
-
-def source_kernel(place, squares, opened, rise_x, rise_y, quiet, across, _, *refs):
+        upper, lower = split(value)
+        rise_y[k] = jnp.where(last, lower, upper)
+
+
+def source_kernel(squares, opened, rise_x, rise_y, quiet, across, _, *refs):
     *lines, out, squared, cells_open, matrix, rows_matrix, calm, band, held, raised, forced, done, fetched, kept = refs
     steps = done.shape[0]
     tile, width = calm.shape[2:]
     high = tile + 2 * HALO
     rows = lines[0].shape[0]
+    place = lax.axis_index("gx")
 
     def tile_copies(k):
         part = quiet.at[:, pl.ds(k * tile, tile), :]
@@ -634,7 +640,7 @@
     pieces = [
         pltpu.make_async_copy(
             piece,
-            held.at[pl.ds(pl.multiple_of((place[0] ^ mask) * rows, 8), rows), :],
+            held.at[pl.ds(pl.multiple_of((place ^ mask) * rows, 8), rows), :],
             fetched.at[4 + len(arrays) + mask],
         )
         for mask, piece in enumerate(lines)
@@ -654,23 +660,20 @@
     copies[1].wait()
     for k in range(count):
         lanes = 2 * LANES if k < count - 1 else LANES
-        value = split(exact_dot(around[k], split(matrix[k][:, :lanes])))
+        value = split(exact_dot(around[k], [matrix[part, k, :, :lanes] for part in range(2)]))
         for part in range(2):
             raised[part, :, 2 * k * LANES : 2 * k * LANES + lanes] = value[part]
     for copy in copies[2:]:
         copy.wait()
 
     reach = rows_matrix.shape[2] // 3
-    third = lane_index((high, 3 * reach)) >= 2 * reach
     for k in range(steps):
         start = k * (tile // 2)
         window = [raised[part, start : start + reach, :] for part in (0, 1, 0)]
-        weights = split(rows_matrix[k])
-        weights = jnp.where(third, weights[1], weights[0])
         calm_here, open_here = tile_copies(k)
         open_here.wait()
-        free = time_step * cells_open[k % 2].astype(F32)
-        value = free * dot(weights, jnp.concatenate(window, axis=0))
+        free = cells_open[k % 2].astype(F32)
+        value = free * dot(rows_matrix[k], jnp.concatenate(window, axis=0))
         forced[k % 2] = value
         inner = value[HALO : HALO + tile]
         shown = (0.5 / 60.0) * free[HALO : HALO + tile, :width]
@@ -738,7 +741,7 @@
     return jax.ShapeDtypeStruct(shape, kind)
 
 
-def pressure_lines(pieces, place_x, gathered, spread, stepped):
+def pressure_lines(pieces, gathered, spread, stepped):
     _, rows, local_x = pieces[0].shape
     count_x, count_y = lax.axis_size("gx"), lax.axis_size("gy")
     count = count_x * count_y
@@ -749,14 +752,13 @@
     turns[0:3], turns[3:6] = cos_turn, sin_turn
     spectra, total = call(
         forward_x_kernel,
-        (place_x, *pieces, np.concatenate([beside(full), beside(zero, middle)]), turns),
+        (*pieces, np.concatenate([beside(full), beside(zero, middle)]), turns),
         (shaped(count, rows, LANES), shaped(8, LANES)),
         (
             pltpu.VMEM((count_x, 2, rows, local_x), F32),
             pltpu.VMEM((count, rows, LANES), F32),
             pltpu.SemaphoreType.DMA((5,)),
         ),
-        specs=scalars,
         out_specs=(pl.BlockSpec(memory_space=pl.ANY), pl.BlockSpec(memory_space=pltpu.VMEM)),
         after=gathered,
         flops=10**9,
@@ -823,9 +825,8 @@
     own = place_x.astype(jnp.int32).reshape(1)
     sent = call(
         pieces_kernel,
-        (own, velocity),
+        (velocity,),
         (shaped(2, local_y // count_x, local_x),) * count_x,
-        specs={0: scalars},
         moved=2 << 20,
         megabytes=8,
         name="pieces",
@@ -875,8 +876,8 @@
         tables_kernel,
         (jnp.stack([place_x, place_y]).astype(jnp.int32), weights_x, weights_y),
         (
-            shaped(tiles, 2 * LANES, 2 * LANES),
-            shaped(steps, high, 3 * (high // 2 + HALO)),
+            shaped(2, tiles, 2 * LANES, 2 * LANES, kind=BF16),
+            shaped(steps, high, 3 * (high // 2 + HALO), kind=BF16),
             shaped(1, kind=jnp.int32),
         ),
         specs={0: scalars},
@@ -952,7 +953,7 @@
             ),
             after=before,
             aliases={len(operands) + k: k for k in range(len(before))},
-            megabytes=54,
+            megabytes=54 if first == 0 else 50,
             flops=3 * 10**9 * count,
             moved=(12 << 20) * count,
             name="quiet_step",
@@ -963,15 +964,15 @@
     if early < steps:
         *begun, _ = quiet_tiles(early, steps - early, begun)
     quiet, final, opened = begun
-    lines = pressure_lines(moved, own, (above, below), beside, stepped)
-    operands = (own, squares, opened, rise_x, rise_y, quiet, across, final, *lines)
+    lines = pressure_lines(moved, (above, below), beside, stepped)
+    operands = (squares, opened, rise_x, rise_y, quiet, across, final, *lines)
     anywhere = pl.BlockSpec(memory_space=pl.ANY)
-    specs = {k: anywhere for k in range(1, len(operands))}
+    specs = {k: anywhere for k in range(len(operands))}
     scratch = (
         pltpu.VMEM(squares.shape, F32),
         pltpu.VMEM((2,) + opened.shape[1:], BF16),
-        pltpu.VMEM(rise_x.shape, F32),
-        pltpu.VMEM(rise_y.shape, F32),
+        pltpu.VMEM(rise_x.shape, BF16),
+        pltpu.VMEM(rise_y.shape, BF16),
         pltpu.VMEM((2, parts - 1, TILE, wide), F32),
         pltpu.VMEM(across.shape, BF16),
         pltpu.VMEM((local_y + 2 * MARGIN, local_x + LANES), F32),
@@ -986,9 +987,9 @@
         operands,
         shaped(*acoustic.shape, kind=BF16),
         scratch,
-        specs={0: scalars, **specs},
+        specs=specs,
         out_specs=anywhere,
-        aliases={7: 0},
+        aliases={6: 0},
         megabytes=56,
         flops=4 * 10**9,
         moved=16 << 20,

time: 99.9 us -> 103 us (1.031)
  local copies, waits for them, and re-layouts: 6.79 us -> 9.34 us
    unnamed x32 -> x50, local copies, waits for them, and re-layouts: 6.09 us -> 8.64 us
  transfers between devices with their start and end apart: 12 -> 12, of which waited for: 6 -> 6; matrix products, arithmetic and copies ran while one was open for 2% -> 2% of each run, Pallas kernels for 31% -> 30%
where the time goes in v2:
time: 103 us; the launch traced here: 102 us
  Pallas kernels  48.1 us (47%)
  waiting for transfers between devices  21.8 us (21%)
  starting transfers between devices  21.1 us (20%)
  local copies, waits for them, and re-layouts  9.34 us (9%)
  other arithmetic  1.23 us (1%)
    pallas_call x11, Pallas kernels, call(): pl.pallas_call(body, out_shape=outs, in_specs=in_specs + [pl.BlockSpec(me...  48.1 us
    unnamed x50, local copies, waits for them, and re-layouts  8.64 us
    all_to_all x1, waiting for transfers between devices, pressure_lines(): spectra = lax.all_to_all(spectra, ('gy', 'gx'), 0, 0, tiled=True)  8.53 us
    ppermute x4, starting transfers between devices, ring(): lax.ppermute(array, axis, [(i, (i + step) % size) for i in range(size)])  6.66 us
    all_to_all x1, starting transfers between devices, pressure_lines(): spectra = lax.all_to_all(spectra, ('gy', 'gx'), 0, 0, tiled=True)  5.52 us
    ppermute x6, starting transfers between devices, swap(): lax.ppermute(array, axis, [(i, i ^ mask) for i in range(lax.axis_size(axi...  5.01 us
    ppermute x6, waiting for transfers between devices, swap(): lax.ppermute(array, axis, [(i, i ^ mask) for i in range(lax.axis_size(axi...  4.96 us
    all_to_all x1, waiting for transfers between devices, pressure_lines(): solved = lax.all_to_all(solved, ('gy', 'gx'), 0, 0, tiled=True)  4.26 us
  transfers between devices with their start and end apart: 12, of which 6 were waited for; matrix products, arithmetic and copies ran while one was open for 2% of the time, Pallas kernels for 30%

profile of v2, /device:TPU:0, one launch (start us, length us, event | category | flops | bytes accessed | tf_op | source)
XLA Modules:
  0.0 101.9 jit_solution(6905468977666409486)
XLA Ops:
  0.0 1.2 %copy-done.1 = f32[2,1,256,512]{3,2,1,0:T(8,128)S(1)} copy-done((f32[2,1,256,512]{3,2,1,0:T(8,128)S(1)}, f32[2,1,256,512]{3,2,1,0:T(8,128)}, u32[]{:S(2)}) %copy-start.1) | copy-done | bytes 1048600
  1.2 0.1 pieces.1
  1.3 0.5 collective-permute-start
  1.8 2.6 %collective-permute-start.5 = (f32[2,64,512]{2,1,0:T(8,128)S(1)}, f32[2,64,512]{2,1,0:T(8,128)S(1)}, u32[]{:S(2)}, u32[]{:S(2)}) collective-permute-start(f32[2,64,512]{2,1,0:T(8,128)S(1)} %get-tuple-element.51), channel_id=1, source_target_pairs={{0,16},{8,24},{16,0},{24,8},{1,17},{9,25},{17,1},{25,9},{2,18},{10... | collective-permute-start | bytes 786440 | tf_op jit(solution)/shard_map/ppermute | solution.py:737
  4.4 0.1 collective-permute-start.6
  4.5 0.0 collective-permute-done.refs_6_.refs_1_
  4.5 1.6 %copy-done = s32[1,512,1024]{2,1,0:T(8,128)S(1)} copy-done((s32[1,512,1024]{2,1,0:T(8,128)S(1)}, s32[1,512,1024]{2,1,0:T(8,128)}, u32[]{:S(2)}) %copy-start) | copy-done | bytes 2097176
  6.0 1.2 %copy-done.2 = f32[2,1,256,512]{3,2,1,0:T(8,128)S(1)} copy-done((f32[2,1,256,512]{3,2,1,0:T(8,128)S(1)}, f32[2,1,256,512]{3,2,1,0:T(8,128)}, u32[]{:S(2)}) %copy-start.2) | copy-done | bytes 1048600
  7.3 1.1 %rows.1 = (f32[24,1024]{1,0:T(8,128)S(1)}, f32[24,1024]{1,0:T(8,128)S(1)}) custom-call(bf16[4,1,512,1024]{3,2,1,0:T(8,128)(2,1)} %refs_4_.9, bf16[4,1,512,1024]{3,2,1,0:T(8,128)(2,1)} %refs_4_.9, s32[1,512,1024]{2,1,0:T(8,128)S(1)} %copy-done, s32[1,512,1024]{2,1,0:T(8,128)S(1)} %copy-done, f32[2,1,256,512]{3,2,1,0:T(8,128)S(1)} %copy-done.2, ...), custom_call_target="tpu_custom_call" | custom-call | bytes 2097152 | tf_op jit(solution)/shard_map/rows/pallas_call | solution.py:718
  8.4 1.8 %collective-permute-start.1 = (f32[24,1024]{1,0:T(8,128)S(1)}, f32[24,1024]{1,0:T(8,128)S(1)}, u32[]{:S(2)}, u32[]{:S(2)}) collective-permute-start(f32[24,1024]{1,0:T(8,128)S(1)} %get-tuple-element.34), channel_id=1, source_target_pairs={{0,1},{1,2},{2,3},{3,4},{4,5},{5,6},{6,7},{7,0},{8,9},{9,10},{10,1... | collective-permute-start | bytes 294920 | tf_op jit(solution)/shard_map/ppermute | solution.py:733
  10.2 3.1 %collective-permute-start.2 = (f32[24,1024]{1,0:T(8,128)S(1)}, f32[24,1024]{1,0:T(8,128)S(1)}, u32[]{:S(2)}, u32[]{:S(2)}) collective-permute-start(f32[24,1024]{1,0:T(8,128)S(1)} %get-tuple-element.35), channel_id=1, source_target_pairs={{0,7},{1,0},{2,1},{3,2},{4,3},{5,4},{6,5},{7,6},{8,15},{9,8},{10,9... | collective-permute-start | bytes 294920 | tf_op jit(solution)/shard_map/ppermute | solution.py:733
  13.3 0.0 collective-permute-done.5.refs_2_
  13.3 3.3 %collective-permute-done.6.refs_3_ = f32[2,64,512]{2,1,0:T(8,128)S(1)} collective-permute-done((f32[2,64,512]{2,1,0:T(8,128)S(1)}, f32[2,64,512]{2,1,0:T(8,128)S(1)}, u32[]{:S(2)}, u32[]{:S(2)}) %collective-permute-start.6) | collective-permute-done | bytes 262176 | tf_op jit(solution)/shard_map/ppermute | solution.py:737
  16.6 0.0 collective-permute-done.1.refs_7_.refs_3_.refs_8_.refs_6_
  16.7 0.4 collective-permute-done.2.refs_8_.refs_4_.refs_9_.refs_7_
  17.1 2.1 %forward_x.1 = (f32[32,64,128]{2,1,0:T(8,128)}, f32[8,128]{1,0:T(8,128)S(1)}) custom-call(f32[2,64,512]{2,1,0:T(8,128)S(1)} %get-tuple-element.50.refs_0_, f32[2,64,512]{2,1,0:T(8,128)S(1)} %collective-permute-done.refs_6_.refs_1_, f32[2,64,512]{2,1,0:T(8,128)S(1)} %collective-permute-done.5.refs_2_, f32[2,64,512]{2,1,0:T(8,128)S(1)} %collective-permute-done.6.refs_3_, ...), custom_call_target="tpu_custom_call" | custom-call | flops 1000000000 | bytes 4194304 | tf_op jit(solution)/shard_map/forward_x/pallas_call | solution.py:718
  19.2 5.5 %all-to-all-start = ((f32[32,64,128]{2,1,0:T(8,128)}), f32[32,64,128]{2,1,0:T(8,128)S(1)}, u32[]{:S(2)}, u32[]{:S(2)}) async-start(f32[32,64,128]{2,1,0:T(8,128)} %get-tuple-element.53), calls=%async_computation | async-start | bytes 2097152 | tf_op jit(solution)/shard_map/all_to_all | solution.py:768
  24.7 0.7 add_convert_fusion.refs_0_
  25.4 3.0 %columns.1 = (f32[48,640]{1,0:T(8,128)}, f32[48,640]{1,0:T(8,128)}) custom-call(f32[4]{0:T(128)} %add_convert_fusion.refs_0_, bf16[4,1,512,1024]{3,2,1,0:T(8,128)(2,1)} %refs_4_.9, bf16[4,1,512,1024]{3,2,1,0:T(8,128)(2,1)} %refs_4_.9, s32[1,512,1024]{2,1,0:T(8,128)} %refs_7_.3, s32[1,512,1024]{2,1,0:T(8,128)} %refs_7_.3, f32[2,1,256,512]{3,2,1,0:T(8,128)} %refs_2_.10, ...), custom_call_target="tpu_custom_call" | custom-call | bytes 8388608 | tf_op jit(solution)/shard_map/columns/pallas_call | solution.py:718
  28.4 0.3 collective-permute-start.3
  28.6 1.5 %collective-permute-start.4 = (f32[48,640]{1,0:T(8,128)}, f32[48,640]{1,0:T(8,128)S(1)}, u32[]{:S(2)}, u32[]{:S(2)}) collective-permute-start(f32[48,640]{1,0:T(8,128)} %get-tuple-element.37), channel_id=1, source_target_pairs={{0,24},{8,0},{16,8},{24,16},{1,25},{9,1},{17,9},{25,17},{2,26},{10... | collective-permute-start | bytes 368648 | tf_op jit(solution)/shard_map/ppermute | solution.py:733
  30.1 0.6 pad_add_fusion.refs_0_
  30.7 3.0 %tables.1 = (bf16[2,5,256,256]{3,2,1,0:T(8,128)(2,1)}, bf16[4,144,240]{2,1,0:T(8,128)(2,1)}, s32[1]{0:T(128)}) custom-call(s32[2]{0:T(128)} %pad_add_fusion.refs_0_, f32[4,4096]{1,0:T(4,128)} %refs_1_.3, f32[4,4096]{1,0:T(4,128)} %refs_2_.7), custom_call_target="tpu_custom_call" | custom-call | bytes 4194304 | tf_op jit(solution)/shard_map/tables/pallas_call | solution.py:718
  33.7 0.7 constant_dynamic-slice_fusion.refs_3_
  34.4 3.6 %collective-permute-done.3.refs_5_ = f32[48,640]{1,0:T(8,128)S(1)} collective-permute-done((f32[48,640]{1,0:T(8,128)}, f32[48,640]{1,0:T(8,128)S(1)}, u32[]{:S(2)}, u32[]{:S(2)}) %collective-permute-start.3) | collective-permute-done | bytes 122912 | tf_op jit(solution)/shard_map/ppermute | solution.py:733
  37.9 0.0 collective-permute-done.4.refs_6_
  37.9 0.6 copy-done.23
  38.6 0.1 copy-done.24
  38.6 3.8 %sides.1 = (f32[5,640,128]{2,1,0:T(8,128)}, f32[272,640]{1,0:T(8,128)}, s32[1]{0:T(128)}) custom-call(f32[4]{0:T(128)} %add_convert_fusion.refs_0_, s32[1]{0:T(128)} %get-tuple-element.32.refs_1_, f32[2,1,256,512]{3,2,1,0:T(8,128)} %refs_2_.10, f32[24,1024]{1,0:T(8,128)} %copy-done.7, f32[24,1024]{1,0:T(8,128)} %copy-done.9, f32[48,640]{1,0:T(8,128)} %copy-done.23, ...), custom_call_target="tpu_custom_call" | custom-call | bytes 8388608 | tf_op jit(solution)/shard_map/sides/pallas_call | solution.py:718
  42.4 8.5 %all-to-all-done.refs_1_ = f32[32,64,128]{2,1,0:T(8,128)S(1)} async-done(((f32[32,64,128]{2,1,0:T(8,128)}), f32[32,64,128]{2,1,0:T(8,128)S(1)}, u32[]{:S(2)}, u32[]{:S(2)}) %all-to-all-start) | async-done | bytes 1048608 | tf_op jit(solution)/shard_map/all_to_all | solution.py:768
  50.9 4.9 %solve_y.1 = f32[32,40,128]{2,1,0:T(8,128)} custom-call(s32[1]{0:T(128)} %get-tuple-element.49.refs_0_, f32[32,64,128]{2,1,0:T(8,128)S(1)} %all-to-all-done.refs_1_, f32[8,128]{1,0:T(8,128)S(1)} %get-tuple-element.54.refs_2_, f32[1,128]{1,0:T(1,128)S(1)} %constant_dynamic-slice_fusion.refs_3_, bf16[1024,256]{1,0:T(8,128)(2,1)S(1)} %copy-done.17, ...), custom_call_target="tpu_custom_call" | custom-call | flops 4000000000 | bytes 6291456 | tf_op jit(solution)/shard_map/solve_y/pallas_call | solution.py:718
  55.8 3.9 %all-to-all-start.1 = ((f32[32,40,128]{2,1,0:T(8,128)}), f32[32,40,128]{2,1,0:T(8,128)}, u32[]{:S(2)}, u32[]{:S(2)}) async-start(f32[32,40,128]{2,1,0:T(8,128)} %solve_y.1), calls=%async_computation.1 | async-start | bytes 1310720 | tf_op jit(solution)/shard_map/all_to_all | solution.py:791
  59.8 13.4 %quiet_step.2 = (f32[3,512,1024]{2,1,0:T(8,128)}, bf16[4,1,512,1024]{3,2,1,0:T(8,128)(2,1)}, bf16[4,144,1152]{2,1,0:T(8,128)(2,1)}, s32[1]{0:T(128)}) custom-call(f32[4]{0:T(128)} %add_convert_fusion.refs_0_, s32[1]{0:T(128)} %bitcast.4.refs_1_, bf16[4,1,512,1024]{3,2,1,0:T(8,128)(2,1)} %refs_4_.9, bf16[4,1,512,1024]{3,2,1,0:T(8,128)(2,1)} %refs_4_.9, ...), custom_call_target="tpu_custom_call" | custom-call | flops 8999999488 | bytes 37748736 | tf_op jit(solution)/shard_map/quiet_step/pallas_call | solution.py:718
  73.2 0.0 copy-start.6
  73.2 0.0 copy-start.12
  73.2 4.3 %all-to-all-done.1.refs_1_ = f32[32,40,128]{2,1,0:T(8,128)} async-done(((f32[32,40,128]{2,1,0:T(8,128)}), f32[32,40,128]{2,1,0:T(8,128)}, u32[]{:S(2)}, u32[]{:S(2)}) %all-to-all-start.1) | async-done | bytes 655392 | tf_op jit(solution)/shard_map/all_to_all | solution.py:791
  77.5 1.4 %copy-done.15 = bf16[1536,512]{1,0:T(8,128)(2,1)S(1)} copy-done((bf16[1536,512]{1,0:T(8,128)(2,1)S(1)}, bf16[1536,512]{1,0:T(8,128)(2,1)}, u32[]{:S(2)}) %copy-start.15) | copy-done | bytes 1572888
  78.9 2.6 %inverse_x.1 = (f32[72,640]{1,0:T(8,128)S(1)}, f32[72,640]{1,0:T(8,128)S(1)}, f32[72,640]{1,0:T(8,128)S(1)}, f32[72,640]{1,0:T(8,128)S(1)}) custom-call(s32[1]{0:T(128)} %get-tuple-element.48.refs_0_, f32[32,40,128]{2,1,0:T(8,128)} %all-to-all-done.1.refs_1_, bf16[1536,512]{1,0:T(8,128)(2,1)S(1)} %copy-done.15, f32[8,256]{1,0:T(8,128)S(1)} %copy-done.19), custom_call_target="tpu_custom_call" | custom-call | flops 1000000000 | bytes 4194304 | tf_op jit(solution)/shard_map/inverse_x/pallas_call | solution.py:718
  81.5 0.7 copy-done.11
  82.2 0.1 collective-permute-start.7
  82.3 1.6 %collective-permute-start.8 = (f32[72,640]{1,0:T(8,128)S(1)}, f32[72,640]{1,0:T(8,128)S(1)}, u32[]{:S(2)}, u32[]{:S(2)}) collective-permute-start(f32[72,640]{1,0:T(8,128)S(1)} %get-tuple-element.57), channel_id=1, source_target_pairs={{0,16},{8,24},{16,0},{24,8},{1,17},{9,25},{17,1},{25,9},{2,18},{10... | collective-permute-start | bytes 552968 | tf_op jit(solution)/shard_map/ppermute | solution.py:737
  83.9 0.2 collective-permute-start.9
  84.1 5.9 %quiet_step.3 = (f32[3,512,1024]{2,1,0:T(8,128)}, bf16[4,1,512,1024]{3,2,1,0:T(8,128)(2,1)}, bf16[4,144,1152]{2,1,0:T(8,128)(2,1)S(1)}, s32[1]{0:T(128)}) custom-call(f32[4]{0:T(128)S(1)} %copy-done.14, s32[1]{0:T(128)} %bitcast.4.refs_1_, bf16[4,1,512,1024]{3,2,1,0:T(8,128)(2,1)} %refs_4_.9, ...), custom_call_target="tpu_custom_call", output_to_operand_aliasing={{0}: (14, {}), {1}: (15, {}), {2}: (16, {})} | custom-call | flops 3000000000 | bytes 12582912 | tf_op jit(solution)/shard_map/quiet_step/pallas_call | solution.py:718
  90.0 1.1 %copy-done.4 = bf16[4,144,1152]{2,1,0:T(8,128)(2,1)} copy-done((bf16[4,144,1152]{2,1,0:T(8,128)(2,1)}, bf16[4,144,1152]{2,1,0:T(8,128)(2,1)S(1)}, u32[]{:S(2)}) %copy-start.4) | copy-done | bytes 1327128
  91.1 0.0 collective-permute-done.7.refs_8_
  91.1 1.6 %collective-permute-done.9.refs_10_ = f32[72,640]{1,0:T(8,128)S(1)} collective-permute-done((f32[72,640]{1,0:T(8,128)S(1)}, f32[72,640]{1,0:T(8,128)S(1)}, u32[]{:S(2)}, u32[]{:S(2)}) %collective-permute-start.9) | collective-permute-done | bytes 184352 | tf_op jit(solution)/shard_map/ppermute | solution.py:737
  92.7 0.7 copy-done.22
  93.4 8.3 %source_step.1 = bf16[4,1,512,1024]{3,2,1,0:T(8,128)(2,1)} custom-call(f32[272,640]{1,0:T(8,128)} %get-tuple-element.38.refs_0_, bf16[4,144,1152]{2,1,0:T(8,128)(2,1)} %copy-done.4, bf16[2,5,256,256]{3,2,1,0:T(8,128)(2,1)} %get-tuple-element.44.refs_2_, bf16[4,144,240]{2,1,0:T(8,128)(2,1)} %get-tuple-element.45.refs_3_, ...), custom_call_target="tpu_custom_call", output_to_operand_aliasing={{}: (6, {})} | custom-call | flops 4000000000 | bytes 16777216 | tf_op jit(solution)/shard_map/source_step/pallas_call | solution.py:718
  (40 shorter events, 0.1 us)
Async XLA Ops:
  0.0 1.2 %copy-start.1 = (f32[2,1,256,512]{3,2,1,0:T(8,128)S(1)}, f32[2,1,256,512]{3,2,1,0:T(8,128)}, u32[]{:S(2)}) copy-start(f32[2,1,256,512]{3,2,1,0:T(8,128)} %refs_2_.10) | copy-start | bytes 3145732
  1.3 3.2 %collective-permute-start = (f32[2,64,512]{2,1,0:T(8,128)S(1)}, f32[2,64,512]{2,1,0:T(8,128)S(1)}, u32[]{:S(2)}, u32[]{:S(2)}) collective-permute-start(f32[2,64,512]{2,1,0:T(8,128)S(1)} %get-tuple-element.33), channel_id=1, source_target_pairs={{0,8},{8,0},{16,24},{24,16},{1,9},{9,1},{17,25},{25,17},{2,10},{10... | collective-permute-start | bytes 786440 | tf_op jit(solution)/shard_map/ppermute | solution.py:737
  1.8 11.5 %collective-permute-start.5 = (f32[2,64,512]{2,1,0:T(8,128)S(1)}, f32[2,64,512]{2,1,0:T(8,128)S(1)}, u32[]{:S(2)}, u32[]{:S(2)}) collective-permute-start(f32[2,64,512]{2,1,0:T(8,128)S(1)} %get-tuple-element.51), channel_id=1, source_target_pairs={{0,16},{8,24},{16,0},{24,8},{1,17},{9,25},{17,1},{25,9},{2,18},{10... | collective-permute-start | bytes 786440 | tf_op jit(solution)/shard_map/ppermute | solution.py:737
  4.4 12.3 %collective-permute-start.6 = (f32[2,64,512]{2,1,0:T(8,128)S(1)}, f32[2,64,512]{2,1,0:T(8,128)S(1)}, u32[]{:S(2)}, u32[]{:S(2)}) collective-permute-start(f32[2,64,512]{2,1,0:T(8,128)S(1)} %get-tuple-element.52), channel_id=1, source_target_pairs={{0,24},{8,16},{16,8},{24,0},{1,25},{9,17},{17,9},{25,1},{2,26},{10... | collective-permute-start | bytes 786440 | tf_op jit(solution)/shard_map/ppermute | solution.py:737
  4.5 1.6 %copy-start = (s32[1,512,1024]{2,1,0:T(8,128)S(1)}, s32[1,512,1024]{2,1,0:T(8,128)}, u32[]{:S(2)}) copy-start(s32[1,512,1024]{2,1,0:T(8,128)} %refs_7_.3) | copy-start | bytes 6291460
  6.0 1.2 %copy-start.2 = (f32[2,1,256,512]{3,2,1,0:T(8,128)S(1)}, f32[2,1,256,512]{3,2,1,0:T(8,128)}, u32[]{:S(2)}) copy-start(f32[2,1,256,512]{3,2,1,0:T(8,128)} %refs_2_.10) | copy-start | bytes 3145732
  7.3 9.8 %copy-start.16 = (bf16[1536,512]{1,0:T(8,128)(2,1)S(1)}, bf16[1536,512]{1,0:T(8,128)(2,1)}, u32[]{:S(2)}) copy-start(bf16[1536,512]{1,0:T(8,128)(2,1)} %constant.39.clone.refs_4_) | copy-start | bytes 4718596
  7.3 9.8 %copy-start.19 = (f32[8,256]{1,0:T(8,128)S(1)}, f32[8,256]{1,0:T(8,128)}, u32[]{:S(2)}) copy-start(f32[8,256]{1,0:T(8,128)} %constant.40.clone.refs_5_.refs_3_) | copy-start | bytes 24580
  8.4 8.3 %collective-permute-start.1 = (f32[24,1024]{1,0:T(8,128)S(1)}, f32[24,1024]{1,0:T(8,128)S(1)}, u32[]{:S(2)}, u32[]{:S(2)}) collective-permute-start(f32[24,1024]{1,0:T(8,128)S(1)} %get-tuple-element.34), channel_id=1, source_target_pairs={{0,1},{1,2},{2,3},{3,4},{4,5},{5,6},{6,7},{7,0},{8,9},{9,10},{10,1... | collective-permute-start | bytes 294920 | tf_op jit(solution)/shard_map/ppermute | solution.py:733
  10.2 6.9 %collective-permute-start.2 = (f32[24,1024]{1,0:T(8,128)S(1)}, f32[24,1024]{1,0:T(8,128)S(1)}, u32[]{:S(2)}, u32[]{:S(2)}) collective-permute-start(f32[24,1024]{1,0:T(8,128)S(1)} %get-tuple-element.35), channel_id=1, source_target_pairs={{0,7},{1,0},{2,1},{3,2},{4,3},{5,4},{6,5},{7,6},{8,15},{9,8},{10,9... | collective-permute-start | bytes 294920 | tf_op jit(solution)/shard_map/ppermute | solution.py:733
  16.7 2.5 %copy-start.7 = (f32[24,1024]{1,0:T(8,128)}, f32[24,1024]{1,0:T(8,128)S(1)}, u32[]{:S(2)}) copy-start(f32[24,1024]{1,0:T(8,128)S(1)} %collective-permute-done.1.refs_7_.refs_3_.refs_8_.refs_6_) | copy-start | bytes 294916
  17.1 2.1 %copy-start.9 = (f32[24,1024]{1,0:T(8,128)}, f32[24,1024]{1,0:T(8,128)S(1)}, u32[]{:S(2)}) copy-start(f32[24,1024]{1,0:T(8,128)S(1)} %collective-permute-done.2.refs_8_.refs_4_.refs_9_.refs_7_) | copy-start | bytes 294916
  19.2 31.8 %all-to-all-start = ((f32[32,64,128]{2,1,0:T(8,128)}), f32[32,64,128]{2,1,0:T(8,128)S(1)}, u32[]{:S(2)}, u32[]{:S(2)}) async-start(f32[32,64,128]{2,1,0:T(8,128)} %get-tuple-element.53), calls=%async_computation | async-start | bytes 2097152 | tf_op jit(solution)/shard_map/all_to_all | solution.py:768
  25.4 25.6 %copy-start.17 = (bf16[1024,256]{1,0:T(8,128)(2,1)S(1)}, bf16[1024,256]{1,0:T(8,128)(2,1)}, u32[]{:S(2)}) copy-start(bf16[1024,256]{1,0:T(8,128)(2,1)} %constant.42.clone.refs_4_) | copy-start | bytes 1572868
  25.4 25.6 %copy-start.18 = (bf16[256,48]{1,0:T(8,128)(2,1)S(1)}, bf16[256,48]{1,0:T(8,128)(2,1)}, u32[]{:S(2)}) copy-start(bf16[256,48]{1,0:T(8,128)(2,1)} %constant.43.clone.refs_5_) | copy-start | bytes 73732
  28.4 9.6 %collective-permute-start.3 = (f32[48,640]{1,0:T(8,128)}, f32[48,640]{1,0:T(8,128)S(1)}, u32[]{:S(2)}, u32[]{:S(2)}) collective-permute-start(f32[48,640]{1,0:T(8,128)} %get-tuple-element.36), channel_id=1, source_target_pairs={{0,8},{8,16},{16,24},{24,0},{1,9},{9,17},{17,25},{25,1},{2,10},{10... | collective-permute-start | bytes 368648 | tf_op jit(solution)/shard_map/ppermute | solution.py:733
  28.6 9.3 %collective-permute-start.4 = (f32[48,640]{1,0:T(8,128)}, f32[48,640]{1,0:T(8,128)S(1)}, u32[]{:S(2)}, u32[]{:S(2)}) collective-permute-start(f32[48,640]{1,0:T(8,128)} %get-tuple-element.37), channel_id=1, source_target_pairs={{0,24},{8,0},{16,8},{24,16},{1,25},{9,1},{17,9},{25,17},{2,26},{10... | collective-permute-start | bytes 368648 | tf_op jit(solution)/shard_map/ppermute | solution.py:733
  37.9 0.6 copy-start.23
  37.9 0.7 copy-start.24
  55.8 21.7 %all-to-all-start.1 = ((f32[32,40,128]{2,1,0:T(8,128)}), f32[32,40,128]{2,1,0:T(8,128)}, u32[]{:S(2)}, u32[]{:S(2)}) async-start(f32[32,40,128]{2,1,0:T(8,128)} %solve_y.1), calls=%async_computation.1 | async-start | bytes 1310720 | tf_op jit(solution)/shard_map/all_to_all | solution.py:791
  73.1 10.9 %copy-start.3 = (bf16[4,144,1152]{2,1,0:T(8,128)(2,1)S(1)}, bf16[4,144,1152]{2,1,0:T(8,128)(2,1)}, u32[]{:S(2)}) copy-start(bf16[4,144,1152]{2,1,0:T(8,128)(2,1)} %get-tuple-element.42.refs_16_) | copy-start | bytes 3981316
  73.2 10.9 %copy-start.5 = (f32[5,640,128]{2,1,0:T(8,128)S(1)}, f32[5,640,128]{2,1,0:T(8,128)}, u32[]{:S(2)}) copy-start(f32[5,640,128]{2,1,0:T(8,128)} %get-tuple-element.39.refs_10_) | copy-start | bytes 4915204
  73.2 10.9 %copy-start.6 = (bf16[512,256]{1,0:T(8,128)(2,1)S(1)}, bf16[512,256]{1,0:T(8,128)(2,1)}, u32[]{:S(2)}) copy-start(bf16[512,256]{1,0:T(8,128)(2,1)} %constant.36.clone.refs_11_.refs_5_) | copy-start | bytes 786436
  73.2 10.9 %copy-start.8 = (f32[24,1024]{1,0:T(8,128)S(1)}, f32[24,1024]{1,0:T(8,128)}, u32[]{:S(2)}) copy-start(f32[24,1024]{1,0:T(8,128)} %copy-done.7) | copy-start | bytes 294916
  73.2 10.9 %copy-start.10 = (f32[24,1024]{1,0:T(8,128)S(1)}, f32[24,1024]{1,0:T(8,128)}, u32[]{:S(2)}) copy-start(f32[24,1024]{1,0:T(8,128)} %copy-done.9) | copy-start | bytes 294916
  73.2 10.9 %copy-start.12 = (bf16[144,144]{1,0:T(8,128)(2,1)S(1)}, bf16[144,144]{1,0:T(8,128)(2,1)}, u32[]{:S(2)}) copy-start(bf16[144,144]{1,0:T(8,128)(2,1)} %constant.37.clone.refs_12_) | copy-start | bytes 124420
  73.2 10.9 %copy-start.14 = (f32[4]{0:T(128)S(1)}, f32[4]{0:T(128)}, u32[]{:S(2)}) copy-start(f32[4]{0:T(128)} %add_convert_fusion.refs_0_) | copy-start | bytes 52
  77.5 6.6 %copy-start.13 = (bf16[128,144]{1,0:T(8,128)(2,1)S(1)}, bf16[128,144]{1,0:T(8,128)(2,1)}, u32[]{:S(2)}) copy-start(bf16[128,144]{1,0:T(8,128)(2,1)} %constant.38.clone.refs_13_) | copy-start | bytes 110596
  77.5 1.4 %copy-start.15 = (bf16[1536,512]{1,0:T(8,128)(2,1)S(1)}, bf16[1536,512]{1,0:T(8,128)(2,1)}, u32[]{:S(2)}) copy-start(bf16[1536,512]{1,0:T(8,128)(2,1)} %constant.44.clone.refs_2_) | copy-start | bytes 4718596
  81.5 0.7 copy-start.11
  82.2 8.9 %collective-permute-start.7 = (f32[72,640]{1,0:T(8,128)S(1)}, f32[72,640]{1,0:T(8,128)S(1)}, u32[]{:S(2)}, u32[]{:S(2)}) collective-permute-start(f32[72,640]{1,0:T(8,128)S(1)} %get-tuple-element.56), channel_id=1, source_target_pairs={{0,8},{8,0},{16,24},{24,16},{1,9},{9,1},{17,25},{25,17},{2,10},{10... | collective-permute-start | bytes 552968 | tf_op jit(solution)/shard_map/ppermute | solution.py:737
  82.3 8.8 %collective-permute-start.8 = (f32[72,640]{1,0:T(8,128)S(1)}, f32[72,640]{1,0:T(8,128)S(1)}, u32[]{:S(2)}, u32[]{:S(2)}) collective-permute-start(f32[72,640]{1,0:T(8,128)S(1)} %get-tuple-element.57), channel_id=1, source_target_pairs={{0,16},{8,24},{16,0},{24,8},{1,17},{9,25},{17,1},{25,9},{2,18},{10... | collective-permute-start | bytes 552968 | tf_op jit(solution)/shard_map/ppermute | solution.py:737
  83.9 8.9 %collective-permute-start.9 = (f32[72,640]{1,0:T(8,128)S(1)}, f32[72,640]{1,0:T(8,128)S(1)}, u32[]{:S(2)}, u32[]{:S(2)}) collective-permute-start(f32[72,640]{1,0:T(8,128)S(1)} %get-tuple-element.58), channel_id=1, source_target_pairs={{0,24},{8,16},{16,8},{24,0},{1,25},{9,17},{17,9},{25,1},{2,26},{10... | collective-permute-start | bytes 552968 | tf_op jit(solution)/shard_map/ppermute | solution.py:737
  90.0 1.1 %copy-start.4 = (bf16[4,144,1152]{2,1,0:T(8,128)(2,1)}, bf16[4,144,1152]{2,1,0:T(8,128)(2,1)S(1)}, u32[]{:S(2)}) copy-start(bf16[4,144,1152]{2,1,0:T(8,128)(2,1)S(1)} %get-tuple-element.43.refs_1_) | copy-start | bytes 3981316
  91.1 1.7 %copy-start.20 = (f32[72,640]{1,0:T(8,128)}, f32[72,640]{1,0:T(8,128)S(1)}, u32[]{:S(2)}) copy-start(f32[72,640]{1,0:T(8,128)S(1)} %collective-permute-done.7.refs_8_) | copy-start | bytes 552964
  91.1 1.6 %copy-start.21 = (f32[72,640]{1,0:T(8,128)}, f32[72,640]{1,0:T(8,128)S(1)}, u32[]{:S(2)}) copy-start(f32[72,640]{1,0:T(8,128)S(1)} %collective-permute-done.8.refs_9_) | copy-start | bytes 552964
  92.7 0.7 copy-start.22

commit v3 on v2

--- a/solution.py
+++ b/solution.py
@@ -345,7 +345,8 @@
     kx = wave[0:1, :]
     first = lanes % 64 < 32
     edge = jnp.float32(length // 2)
-    alone = jnp.where(first, kx * kx, 0.0)
+    square_kx = kx * kx
+    alone = jnp.where(first, square_kx, 0.0)
     slope = jnp.where(first | (kx == -edge), 0.0, jnp.broadcast_to(kx, lanes.shape))
     q = lax.broadcasted_iota(jnp.int32, lanes.shape, 0)
     low_ky = RADIX * (q - jnp.where(q < base // 2, 0, base)).astype(F32)
@@ -358,7 +359,9 @@
         if r == 0:
             corner = jnp.where((kx == -edge) & ~first, edge * edge, 0.0)
             symbol = jnp.where(ky == -edge, jnp.where(first, alone, corner), symbol)
-        terms.append(symbol * pl.reciprocal(kx * kx + ky * ky) * spectrum)
+        square = square_kx + ky * ky
+        guess = pl.reciprocal(square, approx=True)
+        terms.append(symbol * (guess * (2.0 - square * guess)) * spectrum)
     pairs = [
         jnp.where(first, low + spin(low, -32), high + spin(high, 32))
         for low, high in zip(terms[:4], terms[4:])
@@ -485,13 +488,6 @@
     return jnp.concatenate(pieces, axis=1)
 
 
-def slope_y(read):
-    value = read(3) - read(-3)
-    for index in (0, 1):
-        value = value + whole_weights[index] * (read(index + 1) - read(-index - 1))
-    return value
-
-
 def edged(k, side, center, up, down, above, below, sides, has, first=0):
     step = pl.program_id(0) + first
     tile, width = center.shape
@@ -613,8 +609,8 @@
         rise_y[k] = jnp.where(last, lower, upper)
 
 
-def source_kernel(squares, opened, rise_x, rise_y, quiet, across, _, *refs):
-    *lines, out, squared, cells_open, matrix, rows_matrix, calm, band, held, raised, forced, done, fetched, kept = refs
+def source_kernel(squares, opened, rise_x, rise_y, quiet, across, along, _, *refs):
+    *lines, out, squared, cells_open, matrix, rows_matrix, calm, band, column, held, raised, done, fetched, kept = refs
     steps = done.shape[0]
     tile, width = calm.shape[2:]
     high = tile + 2 * HALO
@@ -632,7 +628,7 @@
         part = out.at[1:, 0, pl.ds(k * tile, tile), :]
         return pltpu.make_async_copy(done.at[k], part, kept.at[k])
 
-    arrays = ((squares, squared), (rise_x, matrix), (rise_y, rows_matrix), (across, band))
+    arrays = ((squares, squared), (rise_x, matrix), (rise_y, rows_matrix), (across, band), (along, column))
     copies = [
         pltpu.make_async_copy(source, target, fetched.at[4 + k])
         for k, (source, target) in enumerate(arrays)
@@ -674,11 +670,10 @@
         open_here.wait()
         free = cells_open[k % 2].astype(F32)
         value = free * dot(rows_matrix[k], jnp.concatenate(window, axis=0))
-        forced[k % 2] = value
         inner = value[HALO : HALO + tile]
         shown = (0.5 / 60.0) * free[HALO : HALO + tile, :width]
         x = shown * slopes_x(split(inner), band, False)
-        y = shown * slope_y(lambda d: forced[k % 2, HALO + d : HALO + d + tile, :width])
+        y = shown * sum(dot(column[...], part) for part in split(value[:, :width]))
         calm_here.wait()
         still = calm.at[k % 2]
         done[k, 0] = (still[0] - x).astype(BF16)
@@ -953,7 +948,7 @@
             ),
             after=before,
             aliases={len(operands) + k: k for k in range(len(before))},
-            megabytes=54 if first == 0 else 50,
+            megabytes=54,
             flops=3 * 10**9 * count,
             moved=(12 << 20) * count,
             name="quiet_step",
@@ -965,7 +960,7 @@
         *begun, _ = quiet_tiles(early, steps - early, begun)
     quiet, final, opened = begun
     lines = pressure_lines(moved, (above, below), beside, stepped)
-    operands = (squares, opened, rise_x, rise_y, quiet, across, final, *lines)
+    operands = (squares, opened, rise_x, rise_y, quiet, across, along_inner, final, *lines)
     anywhere = pl.BlockSpec(memory_space=pl.ANY)
     specs = {k: anywhere for k in range(len(operands))}
     scratch = (
@@ -975,11 +970,11 @@
         pltpu.VMEM(rise_y.shape, BF16),
         pltpu.VMEM((2, parts - 1, TILE, wide), F32),
         pltpu.VMEM(across.shape, BF16),
+        pltpu.VMEM(along_inner.shape, BF16),
         pltpu.VMEM((local_y + 2 * MARGIN, local_x + LANES), F32),
         pltpu.VMEM((2, local_y + 2 * HALO, full), BF16),
-        pltpu.VMEM((2, high, full), F32),
         pltpu.VMEM((steps, parts - 1, TILE, wide), BF16),
-        pltpu.SemaphoreType.DMA((8 + count_x,)),
+        pltpu.SemaphoreType.DMA((9 + count_x,)),
         pltpu.SemaphoreType.DMA((steps,)),
     )
     return call(
@@ -989,7 +984,7 @@
         scratch,
         specs=specs,
         out_specs=anywhere,
-        aliases={6: 0},
+        aliases={7: 0},
         megabytes=56,
         flops=4 * 10**9,
         moved=16 << 20,

time: 103 us -> 100 us (0.971)
  local copies, waits for them, and re-layouts: 9.34 us -> 6.79 us
    unnamed x50 -> x32, local copies, waits for them, and re-layouts: 8.64 us -> 6.09 us
  transfers between devices with their start and end apart: 12 -> 12, of which waited for: 6 -> 6; matrix products, arithmetic and copies ran while one was open for 2% -> 2% of each run, Pallas kernels for 30% -> 31%
where the time goes in v3:
time: 100 us; the launch traced here: 99.5 us
  Pallas kernels  48 us (48%)
  waiting for transfers between devices  22.1 us (22%)
  starting transfers between devices  21 us (21%)
  local copies, waits for them, and re-layouts  6.79 us (7%)
  other arithmetic  1.17 us (1%)
    pallas_call x11, Pallas kernels, call(): pl.pallas_call(body, out_shape=outs, in_specs=in_specs + [pl.BlockSpec(me...  48 us
    all_to_all x1, waiting for transfers between devices, pressure_lines(): spectra = lax.all_to_all(spectra, ('gy', 'gx'), 0, 0, tiled=True)  8.56 us
    ppermute x4, starting transfers between devices, ring(): lax.ppermute(array, axis, [(i, (i + step) % size) for i in range(size)])  6.66 us
    unnamed x32, local copies, waits for them, and re-layouts  6.09 us
    all_to_all x1, starting transfers between devices, pressure_lines(): spectra = lax.all_to_all(spectra, ('gy', 'gx'), 0, 0, tiled=True)  5.52 us
    ppermute x6, waiting for transfers between devices, swap(): lax.ppermute(array, axis, [(i, i ^ mask) for i in range(lax.axis_size(axi...  5.31 us
    ppermute x6, starting transfers between devices, swap(): lax.ppermute(array, axis, [(i, i ^ mask) for i in range(lax.axis_size(axi...  5.03 us
    all_to_all x1, waiting for transfers between devices, pressure_lines(): solved = lax.all_to_all(solved, ('gy', 'gx'), 0, 0, tiled=True)  4.24 us
  transfers between devices with their start and end apart: 12, of which 6 were waited for; matrix products, arithmetic and copies ran while one was open for 2% of the time, Pallas kernels for 31%

profile of v3, /device:TPU:0, one launch (start us, length us, event | category | flops | bytes accessed | tf_op | source)
XLA Modules:
  0.0 99.5 jit_solution(9720935822754843757)
XLA Ops:
  0.0 1.2 %copy-done.1 = f32[2,1,256,512]{3,2,1,0:T(8,128)S(1)} copy-done((f32[2,1,256,512]{3,2,1,0:T(8,128)S(1)}, f32[2,1,256,512]{3,2,1,0:T(8,128)}, u32[]{:S(2)}) %copy-start.1) | copy-done | bytes 1048600
  1.2 0.1 pieces.1
  1.3 0.5 collective-permute-start
  1.8 2.6 %collective-permute-start.5 = (f32[2,64,512]{2,1,0:T(8,128)S(1)}, f32[2,64,512]{2,1,0:T(8,128)S(1)}, u32[]{:S(2)}, u32[]{:S(2)}) collective-permute-start(f32[2,64,512]{2,1,0:T(8,128)S(1)} %get-tuple-element.51), channel_id=1, source_target_pairs={{0,16},{8,24},{16,0},{24,8},{1,17},{9,25},{17,1},{25,9},{2,18},{10... | collective-permute-start | bytes 786440 | tf_op jit(solution)/shard_map/ppermute | solution.py:732
  4.4 0.1 collective-permute-start.6
  4.5 0.0 collective-permute-done.refs_6_.refs_1_
  4.5 1.6 %copy-done = s32[1,512,1024]{2,1,0:T(8,128)S(1)} copy-done((s32[1,512,1024]{2,1,0:T(8,128)S(1)}, s32[1,512,1024]{2,1,0:T(8,128)}, u32[]{:S(2)}) %copy-start) | copy-done | bytes 2097176
  6.0 1.2 %copy-done.2 = f32[2,1,256,512]{3,2,1,0:T(8,128)S(1)} copy-done((f32[2,1,256,512]{3,2,1,0:T(8,128)S(1)}, f32[2,1,256,512]{3,2,1,0:T(8,128)}, u32[]{:S(2)}) %copy-start.2) | copy-done | bytes 1048600
  7.3 1.1 %rows.1 = (f32[24,1024]{1,0:T(8,128)S(1)}, f32[24,1024]{1,0:T(8,128)S(1)}) custom-call(bf16[4,1,512,1024]{3,2,1,0:T(8,128)(2,1)} %refs_4_.9, bf16[4,1,512,1024]{3,2,1,0:T(8,128)(2,1)} %refs_4_.9, s32[1,512,1024]{2,1,0:T(8,128)S(1)} %copy-done, s32[1,512,1024]{2,1,0:T(8,128)S(1)} %copy-done, f32[2,1,256,512]{3,2,1,0:T(8,128)S(1)} %copy-done.2, ...), custom_call_target="tpu_custom_call" | custom-call | bytes 2097152 | tf_op jit(solution)/shard_map/rows/pallas_call | solution.py:713
  8.4 1.8 %collective-permute-start.1 = (f32[24,1024]{1,0:T(8,128)S(1)}, f32[24,1024]{1,0:T(8,128)S(1)}, u32[]{:S(2)}, u32[]{:S(2)}) collective-permute-start(f32[24,1024]{1,0:T(8,128)S(1)} %get-tuple-element.34), channel_id=1, source_target_pairs={{0,1},{1,2},{2,3},{3,4},{4,5},{5,6},{6,7},{7,0},{8,9},{9,10},{10,1... | collective-permute-start | bytes 294920 | tf_op jit(solution)/shard_map/ppermute | solution.py:728
  10.2 3.1 %collective-permute-start.2 = (f32[24,1024]{1,0:T(8,128)S(1)}, f32[24,1024]{1,0:T(8,128)S(1)}, u32[]{:S(2)}, u32[]{:S(2)}) collective-permute-start(f32[24,1024]{1,0:T(8,128)S(1)} %get-tuple-element.35), channel_id=1, source_target_pairs={{0,7},{1,0},{2,1},{3,2},{4,3},{5,4},{6,5},{7,6},{8,15},{9,8},{10,9... | collective-permute-start | bytes 294920 | tf_op jit(solution)/shard_map/ppermute | solution.py:728
  13.3 0.0 collective-permute-done.5.refs_2_
  13.3 3.3 %collective-permute-done.6.refs_3_ = f32[2,64,512]{2,1,0:T(8,128)S(1)} collective-permute-done((f32[2,64,512]{2,1,0:T(8,128)S(1)}, f32[2,64,512]{2,1,0:T(8,128)S(1)}, u32[]{:S(2)}, u32[]{:S(2)}) %collective-permute-start.6) | collective-permute-done | bytes 262176 | tf_op jit(solution)/shard_map/ppermute | solution.py:732
  16.6 0.0 collective-permute-done.1.refs_7_.refs_3_.refs_8_.refs_6_
  16.7 0.4 collective-permute-done.2.refs_8_.refs_4_.refs_9_.refs_7_
  17.1 2.0 %forward_x.1 = (f32[32,64,128]{2,1,0:T(8,128)}, f32[8,128]{1,0:T(8,128)S(1)}) custom-call(f32[2,64,512]{2,1,0:T(8,128)S(1)} %get-tuple-element.50.refs_0_, f32[2,64,512]{2,1,0:T(8,128)S(1)} %collective-permute-done.refs_6_.refs_1_, f32[2,64,512]{2,1,0:T(8,128)S(1)} %collective-permute-done.5.refs_2_, f32[2,64,512]{2,1,0:T(8,128)S(1)} %collective-permute-done.6.refs_3_, ...), custom_call_target="tpu_custom_call" | custom-call | flops 1000000000 | bytes 4194304 | tf_op jit(solution)/shard_map/forward_x/pallas_call | solution.py:713
  19.2 5.5 %all-to-all-start = ((f32[32,64,128]{2,1,0:T(8,128)}), f32[32,64,128]{2,1,0:T(8,128)S(1)}, u32[]{:S(2)}, u32[]{:S(2)}) async-start(f32[32,64,128]{2,1,0:T(8,128)} %get-tuple-element.53), calls=%async_computation | async-start | bytes 2097152 | tf_op jit(solution)/shard_map/all_to_all | solution.py:763
  24.7 0.6 add_convert_fusion.refs_0_
  25.3 3.0 %columns.1 = (f32[48,640]{1,0:T(8,128)}, f32[48,640]{1,0:T(8,128)}) custom-call(f32[4]{0:T(128)} %add_convert_fusion.refs_0_, bf16[4,1,512,1024]{3,2,1,0:T(8,128)(2,1)} %refs_4_.9, bf16[4,1,512,1024]{3,2,1,0:T(8,128)(2,1)} %refs_4_.9, s32[1,512,1024]{2,1,0:T(8,128)} %refs_7_.3, s32[1,512,1024]{2,1,0:T(8,128)} %refs_7_.3, f32[2,1,256,512]{3,2,1,0:T(8,128)} %refs_2_.10, ...), custom_call_target="tpu_custom_call" | custom-call | bytes 8388608 | tf_op jit(solution)/shard_map/columns/pallas_call | solution.py:713
  28.3 0.3 collective-permute-start.3
  28.5 1.5 %collective-permute-start.4 = (f32[48,640]{1,0:T(8,128)}, f32[48,640]{1,0:T(8,128)S(1)}, u32[]{:S(2)}, u32[]{:S(2)}) collective-permute-start(f32[48,640]{1,0:T(8,128)} %get-tuple-element.37), channel_id=1, source_target_pairs={{0,24},{8,0},{16,8},{24,16},{1,25},{9,1},{17,9},{25,17},{2,26},{10... | collective-permute-start | bytes 368648 | tf_op jit(solution)/shard_map/ppermute | solution.py:728
  30.0 0.6 pad_add_fusion.refs_0_
  30.6 3.0 %tables.1 = (bf16[2,5,256,256]{3,2,1,0:T(8,128)(2,1)}, bf16[4,144,240]{2,1,0:T(8,128)(2,1)}, s32[1]{0:T(128)}) custom-call(s32[2]{0:T(128)} %pad_add_fusion.refs_0_, f32[4,4096]{1,0:T(4,128)} %refs_1_.3, f32[4,4096]{1,0:T(4,128)} %refs_2_.7), custom_call_target="tpu_custom_call" | custom-call | bytes 4194304 | tf_op jit(solution)/shard_map/tables/pallas_call | solution.py:713
  33.6 0.7 constant_dynamic-slice_fusion.refs_3_
  34.3 3.6 %collective-permute-done.3.refs_5_ = f32[48,640]{1,0:T(8,128)S(1)} collective-permute-done((f32[48,640]{1,0:T(8,128)}, f32[48,640]{1,0:T(8,128)S(1)}, u32[]{:S(2)}, u32[]{:S(2)}) %collective-permute-start.3) | collective-permute-done | bytes 122912 | tf_op jit(solution)/shard_map/ppermute | solution.py:728
  37.9 0.0 collective-permute-done.4.refs_6_
  37.9 0.6 copy-done.14
  38.6 0.0 copy-done.15
  38.6 3.8 %sides.1 = (f32[5,640,128]{2,1,0:T(8,128)}, f32[272,640]{1,0:T(8,128)}, s32[1]{0:T(128)}) custom-call(f32[4]{0:T(128)} %add_convert_fusion.refs_0_, s32[1]{0:T(128)} %get-tuple-element.32.refs_1_, f32[2,1,256,512]{3,2,1,0:T(8,128)} %refs_2_.10, f32[24,1024]{1,0:T(8,128)} %copy-done.3, f32[24,1024]{1,0:T(8,128)} %copy-done.4, f32[48,640]{1,0:T(8,128)} %copy-done.14, ...), custom_call_target="tpu_custom_call" | custom-call | bytes 8388608 | tf_op jit(solution)/shard_map/sides/pallas_call | solution.py:713
  42.4 8.6 %all-to-all-done.refs_1_ = f32[32,64,128]{2,1,0:T(8,128)S(1)} async-done(((f32[32,64,128]{2,1,0:T(8,128)}), f32[32,64,128]{2,1,0:T(8,128)S(1)}, u32[]{:S(2)}, u32[]{:S(2)}) %all-to-all-start) | async-done | bytes 1048608 | tf_op jit(solution)/shard_map/all_to_all | solution.py:763
  50.9 0.0 copy-done.8
  50.9 4.9 %solve_y.1 = f32[32,40,128]{2,1,0:T(8,128)} custom-call(s32[1]{0:T(128)} %get-tuple-element.49.refs_0_, f32[32,64,128]{2,1,0:T(8,128)S(1)} %all-to-all-done.refs_1_, f32[8,128]{1,0:T(8,128)S(1)} %get-tuple-element.54.refs_2_, f32[1,128]{1,0:T(1,128)S(1)} %constant_dynamic-slice_fusion.refs_3_, bf16[1024,256]{1,0:T(8,128)(2,1)S(1)} %copy-done.8, ...), custom_call_target="tpu_custom_call" | custom-call | flops 4000000000 | bytes 6291456 | tf_op jit(solution)/shard_map/solve_y/pallas_call | solution.py:713
  55.8 3.8 %all-to-all-start.1 = ((f32[32,40,128]{2,1,0:T(8,128)}), f32[32,40,128]{2,1,0:T(8,128)S(1)}, u32[]{:S(2)}, u32[]{:S(2)}) async-start(f32[32,40,128]{2,1,0:T(8,128)} %solve_y.1), calls=%async_computation.1 | async-start | bytes 1310720 | tf_op jit(solution)/shard_map/all_to_all | solution.py:786
  59.6 0.0 copy-start.6
  59.6 13.5 %quiet_step.2 = (f32[3,512,1024]{2,1,0:T(8,128)}, bf16[4,1,512,1024]{3,2,1,0:T(8,128)(2,1)}, bf16[4,144,1152]{2,1,0:T(8,128)(2,1)}, s32[1]{0:T(128)}) custom-call(f32[4]{0:T(128)} %add_convert_fusion.refs_0_, s32[1]{0:T(128)} %bitcast.4.refs_1_, bf16[4,1,512,1024]{3,2,1,0:T(8,128)(2,1)} %refs_4_.9, bf16[4,1,512,1024]{3,2,1,0:T(8,128)(2,1)} %refs_4_.9, ...), custom_call_target="tpu_custom_call" | custom-call | flops 8999999488 | bytes 37748736 | tf_op jit(solution)/shard_map/quiet_step/pallas_call | solution.py:713
  73.1 4.2 %all-to-all-done.1.refs_1_ = f32[32,40,128]{2,1,0:T(8,128)S(1)} async-done(((f32[32,40,128]{2,1,0:T(8,128)}), f32[32,40,128]{2,1,0:T(8,128)S(1)}, u32[]{:S(2)}, u32[]{:S(2)}) %all-to-all-start.1) | async-done | bytes 655392 | tf_op jit(solution)/shard_map/all_to_all | solution.py:786
  77.4 1.5 %inverse_x.1 = (f32[72,640]{1,0:T(8,128)S(1)}, f32[72,640]{1,0:T(8,128)S(1)}, f32[72,640]{1,0:T(8,128)S(1)}, f32[72,640]{1,0:T(8,128)S(1)}) custom-call(s32[1]{0:T(128)} %get-tuple-element.48.refs_0_, f32[32,40,128]{2,1,0:T(8,128)S(1)} %all-to-all-done.1.refs_1_, bf16[1536,512]{1,0:T(8,128)(2,1)S(1)} %copy-done.6, f32[8,256]{1,0:T(8,128)S(1)} %copy-done.10), custom_call_target="tpu_custom_call" | custom-call | flops 1000000000 | bytes 4194304 | tf_op jit(solution)/shard_map/inverse_x/pallas_call | solution.py:713
  78.9 0.7 copy-done.5
  79.5 0.1 collective-permute-start.7
  79.6 1.6 %collective-permute-start.8 = (f32[72,640]{1,0:T(8,128)S(1)}, f32[72,640]{1,0:T(8,128)S(1)}, u32[]{:S(2)}, u32[]{:S(2)}) collective-permute-start(f32[72,640]{1,0:T(8,128)S(1)} %get-tuple-element.57), channel_id=1, source_target_pairs={{0,16},{8,24},{16,0},{24,8},{1,17},{9,25},{17,1},{25,9},{2,18},{10... | collective-permute-start | bytes 552968 | tf_op jit(solution)/shard_map/ppermute | solution.py:732
  81.2 0.2 collective-permute-start.9
  81.4 6.7 %quiet_step.3 = (f32[3,512,1024]{2,1,0:T(8,128)}, bf16[4,1,512,1024]{3,2,1,0:T(8,128)(2,1)}, bf16[4,144,1152]{2,1,0:T(8,128)(2,1)}, s32[1]{0:T(128)}) custom-call(f32[4]{0:T(128)} %add_convert_fusion.refs_0_, s32[1]{0:T(128)} %bitcast.4.refs_1_, bf16[4,1,512,1024]{3,2,1,0:T(8,128)(2,1)} %refs_4_.9, ...), custom_call_target="tpu_custom_call", output_to_operand_aliasing={{0}: (14, {}), {1}: (15, {}), {2}: (16, {})} | custom-call | flops 3000000000 | bytes 12582912 | tf_op jit(solution)/shard_map/quiet_step/pallas_call | solution.py:713
  88.1 0.0 collective-permute-done.7.refs_9_
  88.1 0.0 copy-start.11
  88.1 0.0 collective-permute-done.8.refs_10_
  88.1 2.0 %collective-permute-done.9.refs_11_ = f32[72,640]{1,0:T(8,128)S(1)} collective-permute-done((f32[72,640]{1,0:T(8,128)S(1)}, f32[72,640]{1,0:T(8,128)S(1)}, u32[]{:S(2)}, u32[]{:S(2)}) %collective-permute-start.9) | collective-permute-done | bytes 184352 | tf_op jit(solution)/shard_map/ppermute | solution.py:732
  90.1 0.7 copy-done.13
  90.8 8.6 %source_step.1 = bf16[4,1,512,1024]{3,2,1,0:T(8,128)(2,1)} custom-call(f32[272,640]{1,0:T(8,128)} %get-tuple-element.38.refs_0_, bf16[4,144,1152]{2,1,0:T(8,128)(2,1)} %get-tuple-element.43.refs_1_, bf16[2,5,256,256]{3,2,1,0:T(8,128)(2,1)} %get-tuple-element.44.refs_2_, ...), custom_call_target="tpu_custom_call", output_to_operand_aliasing={{}: (7, {})} | custom-call | flops 4000000000 | bytes 16777216 | tf_op jit(solution)/shard_map/source_step/pallas_call | solution.py:713
  (22 shorter events, 0.0 us)
Async XLA Ops:
  0.0 1.2 %copy-start.1 = (f32[2,1,256,512]{3,2,1,0:T(8,128)S(1)}, f32[2,1,256,512]{3,2,1,0:T(8,128)}, u32[]{:S(2)}) copy-start(f32[2,1,256,512]{3,2,1,0:T(8,128)} %refs_2_.10) | copy-start | bytes 3145732
  1.3 3.2 %collective-permute-start = (f32[2,64,512]{2,1,0:T(8,128)S(1)}, f32[2,64,512]{2,1,0:T(8,128)S(1)}, u32[]{:S(2)}, u32[]{:S(2)}) collective-permute-start(f32[2,64,512]{2,1,0:T(8,128)S(1)} %get-tuple-element.33), channel_id=1, source_target_pairs={{0,8},{8,0},{16,24},{24,16},{1,9},{9,1},{17,25},{25,17},{2,10},{10... | collective-permute-start | bytes 786440 | tf_op jit(solution)/shard_map/ppermute | solution.py:732
  1.8 11.5 %collective-permute-start.5 = (f32[2,64,512]{2,1,0:T(8,128)S(1)}, f32[2,64,512]{2,1,0:T(8,128)S(1)}, u32[]{:S(2)}, u32[]{:S(2)}) collective-permute-start(f32[2,64,512]{2,1,0:T(8,128)S(1)} %get-tuple-element.51), channel_id=1, source_target_pairs={{0,16},{8,24},{16,0},{24,8},{1,17},{9,25},{17,1},{25,9},{2,18},{10... | collective-permute-start | bytes 786440 | tf_op jit(solution)/shard_map/ppermute | solution.py:732
  4.4 12.3 %collective-permute-start.6 = (f32[2,64,512]{2,1,0:T(8,128)S(1)}, f32[2,64,512]{2,1,0:T(8,128)S(1)}, u32[]{:S(2)}, u32[]{:S(2)}) collective-permute-start(f32[2,64,512]{2,1,0:T(8,128)S(1)} %get-tuple-element.52), channel_id=1, source_target_pairs={{0,24},{8,16},{16,8},{24,0},{1,25},{9,17},{17,9},{25,1},{2,26},{10... | collective-permute-start | bytes 786440 | tf_op jit(solution)/shard_map/ppermute | solution.py:732
  4.5 1.6 %copy-start = (s32[1,512,1024]{2,1,0:T(8,128)S(1)}, s32[1,512,1024]{2,1,0:T(8,128)}, u32[]{:S(2)}) copy-start(s32[1,512,1024]{2,1,0:T(8,128)} %refs_7_.3) | copy-start | bytes 6291460
  6.0 1.2 %copy-start.2 = (f32[2,1,256,512]{3,2,1,0:T(8,128)S(1)}, f32[2,1,256,512]{3,2,1,0:T(8,128)}, u32[]{:S(2)}) copy-start(f32[2,1,256,512]{3,2,1,0:T(8,128)} %refs_2_.10) | copy-start | bytes 3145732
  7.3 9.8 %copy-start.7 = (bf16[1536,512]{1,0:T(8,128)(2,1)S(1)}, bf16[1536,512]{1,0:T(8,128)(2,1)}, u32[]{:S(2)}) copy-start(bf16[1536,512]{1,0:T(8,128)(2,1)} %constant.39.clone.refs_4_) | copy-start | bytes 4718596
  7.3 9.8 %copy-start.10 = (f32[8,256]{1,0:T(8,128)S(1)}, f32[8,256]{1,0:T(8,128)}, u32[]{:S(2)}) copy-start(f32[8,256]{1,0:T(8,128)} %constant.40.clone.refs_5_.refs_3_) | copy-start | bytes 24580
  8.4 8.3 %collective-permute-start.1 = (f32[24,1024]{1,0:T(8,128)S(1)}, f32[24,1024]{1,0:T(8,128)S(1)}, u32[]{:S(2)}, u32[]{:S(2)}) collective-permute-start(f32[24,1024]{1,0:T(8,128)S(1)} %get-tuple-element.34), channel_id=1, source_target_pairs={{0,1},{1,2},{2,3},{3,4},{4,5},{5,6},{6,7},{7,0},{8,9},{9,10},{10,1... | collective-permute-start | bytes 294920 | tf_op jit(solution)/shard_map/ppermute | solution.py:728
  10.2 6.9 %collective-permute-start.2 = (f32[24,1024]{1,0:T(8,128)S(1)}, f32[24,1024]{1,0:T(8,128)S(1)}, u32[]{:S(2)}, u32[]{:S(2)}) collective-permute-start(f32[24,1024]{1,0:T(8,128)S(1)} %get-tuple-element.35), channel_id=1, source_target_pairs={{0,7},{1,0},{2,1},{3,2},{4,3},{5,4},{6,5},{7,6},{8,15},{9,8},{10,9... | collective-permute-start | bytes 294920 | tf_op jit(solution)/shard_map/ppermute | solution.py:728
  16.7 2.5 %copy-start.3 = (f32[24,1024]{1,0:T(8,128)}, f32[24,1024]{1,0:T(8,128)S(1)}, u32[]{:S(2)}) copy-start(f32[24,1024]{1,0:T(8,128)S(1)} %collective-permute-done.1.refs_7_.refs_3_.refs_8_.refs_6_) | copy-start | bytes 294916
  17.1 2.1 %copy-start.4 = (f32[24,1024]{1,0:T(8,128)}, f32[24,1024]{1,0:T(8,128)S(1)}, u32[]{:S(2)}) copy-start(f32[24,1024]{1,0:T(8,128)S(1)} %collective-permute-done.2.refs_8_.refs_4_.refs_9_.refs_7_) | copy-start | bytes 294916
  19.2 31.8 %all-to-all-start = ((f32[32,64,128]{2,1,0:T(8,128)}), f32[32,64,128]{2,1,0:T(8,128)S(1)}, u32[]{:S(2)}, u32[]{:S(2)}) async-start(f32[32,64,128]{2,1,0:T(8,128)} %get-tuple-element.53), calls=%async_computation | async-start | bytes 2097152 | tf_op jit(solution)/shard_map/all_to_all | solution.py:763
  25.3 25.6 %copy-start.8 = (bf16[1024,256]{1,0:T(8,128)(2,1)S(1)}, bf16[1024,256]{1,0:T(8,128)(2,1)}, u32[]{:S(2)}) copy-start(bf16[1024,256]{1,0:T(8,128)(2,1)} %constant.42.clone.refs_4_) | copy-start | bytes 1572868
  25.3 25.6 %copy-start.9 = (bf16[256,48]{1,0:T(8,128)(2,1)S(1)}, bf16[256,48]{1,0:T(8,128)(2,1)}, u32[]{:S(2)}) copy-start(bf16[256,48]{1,0:T(8,128)(2,1)} %constant.43.clone.refs_5_) | copy-start | bytes 73732
  28.3 9.6 %collective-permute-start.3 = (f32[48,640]{1,0:T(8,128)}, f32[48,640]{1,0:T(8,128)S(1)}, u32[]{:S(2)}, u32[]{:S(2)}) collective-permute-start(f32[48,640]{1,0:T(8,128)} %get-tuple-element.36), channel_id=1, source_target_pairs={{0,8},{8,16},{16,24},{24,0},{1,9},{9,17},{17,25},{25,1},{2,10},{10... | collective-permute-start | bytes 368648 | tf_op jit(solution)/shard_map/ppermute | solution.py:728
  28.5 9.4 %collective-permute-start.4 = (f32[48,640]{1,0:T(8,128)}, f32[48,640]{1,0:T(8,128)S(1)}, u32[]{:S(2)}, u32[]{:S(2)}) collective-permute-start(f32[48,640]{1,0:T(8,128)} %get-tuple-element.37), channel_id=1, source_target_pairs={{0,24},{8,0},{16,8},{24,16},{1,25},{9,1},{17,9},{25,17},{2,26},{10... | collective-permute-start | bytes 368648 | tf_op jit(solution)/shard_map/ppermute | solution.py:728
  37.9 0.6 copy-start.14
  37.9 0.7 copy-start.15
  55.8 21.6 %all-to-all-start.1 = ((f32[32,40,128]{2,1,0:T(8,128)}), f32[32,40,128]{2,1,0:T(8,128)S(1)}, u32[]{:S(2)}, u32[]{:S(2)}) async-start(f32[32,40,128]{2,1,0:T(8,128)} %solve_y.1), calls=%async_computation.1 | async-start | bytes 1310720 | tf_op jit(solution)/shard_map/all_to_all | solution.py:786
  59.6 17.7 %copy-start.6 = (bf16[1536,512]{1,0:T(8,128)(2,1)S(1)}, bf16[1536,512]{1,0:T(8,128)(2,1)}, u32[]{:S(2)}) copy-start(bf16[1536,512]{1,0:T(8,128)(2,1)} %constant.44.clone.refs_2_) | copy-start | bytes 4718596
  78.9 0.7 copy-start.5
  79.5 8.5 %collective-permute-start.7 = (f32[72,640]{1,0:T(8,128)S(1)}, f32[72,640]{1,0:T(8,128)S(1)}, u32[]{:S(2)}, u32[]{:S(2)}) collective-permute-start(f32[72,640]{1,0:T(8,128)S(1)} %get-tuple-element.56), channel_id=1, source_target_pairs={{0,8},{8,0},{16,24},{24,16},{1,9},{9,1},{17,25},{25,17},{2,10},{10... | collective-permute-start | bytes 552968 | tf_op jit(solution)/shard_map/ppermute | solution.py:732
  79.6 8.5 %collective-permute-start.8 = (f32[72,640]{1,0:T(8,128)S(1)}, f32[72,640]{1,0:T(8,128)S(1)}, u32[]{:S(2)}, u32[]{:S(2)}) collective-permute-start(f32[72,640]{1,0:T(8,128)S(1)} %get-tuple-element.57), channel_id=1, source_target_pairs={{0,16},{8,24},{16,0},{24,8},{1,17},{9,25},{17,1},{25,9},{2,18},{10... | collective-permute-start | bytes 552968 | tf_op jit(solution)/shard_map/ppermute | solution.py:732
  81.2 8.9 %collective-permute-start.9 = (f32[72,640]{1,0:T(8,128)S(1)}, f32[72,640]{1,0:T(8,128)S(1)}, u32[]{:S(2)}, u32[]{:S(2)}) collective-permute-start(f32[72,640]{1,0:T(8,128)S(1)} %get-tuple-element.58), channel_id=1, source_target_pairs={{0,24},{8,16},{16,8},{24,0},{1,25},{9,17},{17,9},{25,1},{2,26},{10... | collective-permute-start | bytes 552968 | tf_op jit(solution)/shard_map/ppermute | solution.py:732
  88.1 2.0 %copy-start.11 = (f32[72,640]{1,0:T(8,128)}, f32[72,640]{1,0:T(8,128)S(1)}, u32[]{:S(2)}) copy-start(f32[72,640]{1,0:T(8,128)S(1)} %collective-permute-done.7.refs_9_) | copy-start | bytes 552964
  88.1 2.0 %copy-start.12 = (f32[72,640]{1,0:T(8,128)}, f32[72,640]{1,0:T(8,128)S(1)}, u32[]{:S(2)}) copy-start(f32[72,640]{1,0:T(8,128)S(1)} %collective-permute-done.8.refs_10_) | copy-start | bytes 552964
  90.1 0.7 copy-start.13

commit v4 on v3

--- a/solution.py
+++ b/solution.py
@@ -311,7 +311,7 @@
     ]
 
 
-def solve_y_kernel(count_x, _, lines, total, wave, both, turns, out, held, spread, made, sent):
+def solve_y_kernel(count_x, lines, total, wave, both, turns, out, held, spread, made, sent):
     count, rows, _ = lines.shape
     base = turns.shape[0]
     length = count * rows
@@ -414,9 +414,11 @@
 
 
 def inverse_x_kernel(
-    kept, scale, place, lines, tables, turns, *refs
+    kept, scale, lines, tables, turns, *refs
 ):
-    *outs, held = refs
+    kept_out, *outs, held, own, sent = refs
+    outs = [own] + outs
+    place = lax.axis_index("gx")
     count, half, _ = lines.shape
     base = turns.shape[1]
     length = RADIX * base
@@ -464,13 +466,17 @@
     targets, local = len(outs), outs[0].shape[1] - LANES
     right = lane_index((kept, LANES)) < 64
     for mask, out in enumerate(outs):
-        start = pl.multiple_of((place[0] ^ mask) * local, LANES)
+        start = pl.multiple_of((place ^ mask) * local, LANES)
         after = pl.multiple_of(jnp.where(start + local == length, 0, start + local), LANES)
         before = pl.multiple_of(jnp.where(start == 0, length, start) - LANES, LANES)
         out[:, :local] = held[:, pl.ds(start, local)]
         out[:, local:] = jnp.where(
             right, held[:, pl.ds(after, LANES)], held[:, pl.ds(before, LANES)]
         )
+        if mask == 0:
+            copy = pltpu.make_async_copy(own, kept_out, sent)
+            copy.start()
+    copy.wait()
 
 
 def slopes_x(parts, band, with_edge):
@@ -565,36 +571,41 @@
     mark[0] = place[0]
 
 
-def tables_kernel(place, weights_x, weights_y, rise_x, rise_y, mark):
-    mark[0] = place[0]
-    _, tiles, reach_x, lanes = rise_x.shape
-    wide, length_x = (tiles - 1) * lanes, weights_x.shape[1]
-    first = place[0] * wide
+def own_weights(ref, start, size):
+    length = ref.shape[1]
+    start = jnp.where(start < 0, start + length, jnp.where(start >= length, start - length, start))
+    return ref[:, pl.ds(pl.multiple_of(start, LANES), size)]
+
+
+def columns_table(ref, place, tiles):
+    lanes = 2 * LANES
+    wide = (tiles - 1) * lanes
+    first = place * wide
     half = LANES // 2
-
-    def weights(ref, start, size):
-        length = ref.shape[1]
-        start = jnp.where(start < 0, start + length, jnp.where(start >= length, start - length, start))
-        return ref[:, pl.ds(pl.multiple_of(start, LANES), size)]
-
-    cells = lax.broadcasted_iota(jnp.int32, (reach_x, lanes), 0)
-    fine = lax.broadcasted_iota(jnp.int32, (reach_x, lanes), 1)
-    right, left = weights(weights_x, first + wide, LANES), weights(weights_x, first - LANES, LANES)
+    cells = lax.broadcasted_iota(jnp.int32, (lanes, lanes), 0)
+    fine = lax.broadcasted_iota(jnp.int32, (lanes, lanes), 1)
+    right, left = own_weights(ref, first + wide, LANES), own_weights(ref, first - LANES, LANES)
     edge = jnp.where(lane_index(right.shape) < half, right, left)
     edge = jnp.concatenate([edge, edge], axis=1)
+    tables = []
     for k in range(tiles):
-        own = weights(weights_x, first + k * lanes, lanes) if k < tiles - 1 else edge
+        own = own_weights(ref, first + k * lanes, lanes) if k < tiles - 1 else edge
         target = fine // 2 - 1
         if k == tiles - 1:
             target = jnp.where(fine < half, target, target + half)
         value = jnp.zeros(fine.shape, F32)
         for t in range(4):
-            value = jnp.where(cells == (target + t) % reach_x, own[t : t + 1, :], value)
-        rise_x[0, k], rise_x[1, k] = split(value)
+            value = jnp.where(cells == (target + t) % lanes, own[t : t + 1, :], value)
+        tables.append(split(value))
+    return tables
+
+
+def tables_kernel(place, weights_y, rise_y, mark):
+    mark[0] = place[0]
     steps, high, reach = rise_y.shape
     tall = steps * TILE
     first = place[1] * tall
-    own = [weights(weights_y, first + k * LANES, LANES) for k in range(-1, tall // LANES + 1)]
+    own = [own_weights(weights_y, first + k * LANES, LANES) for k in range(-1, tall // LANES + 1)]
     own = jnp.concatenate([jnp.concatenate(own, axis=1), jnp.zeros((4, tall + 2 * LANES), F32)], axis=0).T
     cells = lax.broadcasted_iota(jnp.int32, (high, reach), 1)
     last = cells >= reach // 3 * 2
@@ -609,8 +620,8 @@
         rise_y[k] = jnp.where(last, lower, upper)
 
 
-def source_kernel(squares, opened, rise_x, rise_y, quiet, across, along, _, *refs):
-    *lines, out, squared, cells_open, matrix, rows_matrix, calm, band, column, held, raised, done, fetched, kept = refs
+def source_kernel(weights_x, squares, opened, rise_y, quiet, across, along, _, *refs):
+    *lines, out, squared, cells_open, rows_matrix, calm, band, column, held, raised, done, fetched, kept = refs
     steps = done.shape[0]
     tile, width = calm.shape[2:]
     high = tile + 2 * HALO
@@ -628,7 +639,7 @@
         part = out.at[1:, 0, pl.ds(k * tile, tile), :]
         return pltpu.make_async_copy(done.at[k], part, kept.at[k])
 
-    arrays = ((squares, squared), (rise_x, matrix), (rise_y, rows_matrix), (across, band), (along, column))
+    arrays = ((squares, squared), (rise_y, rows_matrix), (across, band), (along, column))
     copies = [
         pltpu.make_async_copy(source, target, fetched.at[4 + k])
         for k, (source, target) in enumerate(arrays)
@@ -643,23 +654,23 @@
     ]
     for copy in (*pieces, *copies, *tile_copies(0), *tile_copies(1)):
         copy.start()
+    count = squares.shape[1] // LANES
+    matrix = columns_table(weights_x, place, count)
     for copy in pieces + copies[:1]:
         copy.wait()
 
     level = held[MARGIN - HALO : MARGIN - HALO + squared.shape[0], :] - squared[...]
-    count = level.shape[1] // LANES
     near = lane_index((level.shape[0], LANES)) < 64
     around = []
     for k in range(count):
         after, before = lane_tile(level, (k + 1) % count), lane_tile(level, (k - 1) % count)
         around.append(split(jnp.concatenate([lane_tile(level, k), jnp.where(near, after, before)], axis=1)))
-    copies[1].wait()
     for k in range(count):
         lanes = 2 * LANES if k < count - 1 else LANES
-        value = split(exact_dot(around[k], [matrix[part, k, :, :lanes] for part in range(2)]))
+        value = split(exact_dot(around[k], [part[:, :lanes] for part in matrix[k]]))
         for part in range(2):
             raised[part, :, 2 * k * LANES : 2 * k * LANES + lanes] = value[part]
-    for copy in copies[2:]:
+    for copy in copies[1:]:
         copy.wait()
 
     reach = rows_matrix.shape[2] // 3
@@ -740,7 +751,6 @@
     _, rows, local_x = pieces[0].shape
     count_x, count_y = lax.axis_size("gx"), lax.axis_size("gy")
     count = count_x * count_y
-    scalars = {0: pl.BlockSpec(memory_space=pltpu.SMEM)}
     length_x, length_y = local_x * count_x, rows * count
     full, zero, middle, cos_turn, sin_turn = x_tables(length_x)
     turns = np.zeros((8, cos_turn.shape[1]), np.float32)
@@ -761,7 +771,7 @@
         name="forward_x",
     )
     spectra = lax.all_to_all(spectra, ("gy", "gx"), 0, 0, tiled=True)
-    place = lax.axis_index("gy") * count_x + lax.axis_index("gx")
+    place = lax.axis_index("gy") * count_x + spread[0]
     waves = jnp.asarray(wave_table(length_x, count))
     wave = lax.dynamic_slice(waves, (place, 0), (1, LANES))
     both, turns_y = y_tables(length_y)
@@ -769,7 +779,7 @@
     half = (kept // 2 + 8) // 8 * 8
     solved = call(
         functools.partial(solve_y_kernel, count_x),
-        (spread, spectra, total, wave, beside(both), turns_y),
+        (spectra, total, wave, beside(both), turns_y),
         shaped(count, half, LANES),
         (
             pltpu.VMEM((length_y + 2 * MARGIN, LANES), F32),
@@ -777,7 +787,6 @@
             pltpu.VMEM((count, half, LANES), F32),
             pltpu.SemaphoreType.DMA((count // RADIX,)),
         ),
-        specs=scalars,
         out_specs=pl.BlockSpec(memory_space=pl.ANY),
         flops=4 * 10**9,
         moved=6 << 20,
@@ -789,12 +798,18 @@
     tables = np.concatenate(
         [beside(full.T), beside(back, 2.0 * middle.T)]
     )
+    again = jnp.asarray(np.tile(turns, (count_x, 1, 1)))
+    again = lax.dynamic_slice(again, (stepped[0], 0, 0), (1,) + turns.shape)
     pressed = call(
         functools.partial(inverse_x_kernel, kept, 1.0 / (length_x * length_y)),
-        (stepped, solved, tables, turns),
+        (solved, tables, again[0]),
         (shaped(kept, local_x + LANES),) * count_x,
-        (pltpu.VMEM((kept, length_x), F32),),
-        specs=scalars,
+        (
+            pltpu.VMEM((kept, length_x), F32),
+            pltpu.VMEM((kept, local_x + LANES), F32),
+            pltpu.SemaphoreType.DMA(()),
+        ),
+        out_specs=(pl.BlockSpec(memory_space=pl.ANY),) + (pl.BlockSpec(memory_space=pltpu.VMEM),) * (count_x - 1),
         flops=10**9,
         moved=4 << 20,
         name="inverse_x",
@@ -865,19 +880,13 @@
         name="columns",
     )
     from_left, from_right = ring(to_right, "gx", 1), ring(to_left, "gx", -1)
-    local_memory = pl.BlockSpec(memory_space=pltpu.VMEM)
-    tiles = wide // (2 * LANES) + 1
-    rise_x, rise_y, listed = call(
+    rise_y, listed = call(
         tables_kernel,
-        (jnp.stack([place_x, place_y]).astype(jnp.int32), weights_x, weights_y),
-        (
-            shaped(2, tiles, 2 * LANES, 2 * LANES, kind=BF16),
-            shaped(steps, high, 3 * (high // 2 + HALO), kind=BF16),
-            shaped(1, kind=jnp.int32),
-        ),
+        (jnp.stack([place_x, place_y]).astype(jnp.int32), weights_y),
+        (shaped(steps, high, 3 * (high // 2 + HALO), kind=BF16), shaped(1, kind=jnp.int32)),
         specs={0: scalars},
-        out_specs=(local_memory, local_memory, scalars),
-        moved=4 << 20,
+        out_specs=(pl.BlockSpec(memory_space=pltpu.VMEM), scalars),
+        moved=2 << 20,
         megabytes=54,
         name="tables",
     )
@@ -960,13 +969,12 @@
         *begun, _ = quiet_tiles(early, steps - early, begun)
     quiet, final, opened = begun
     lines = pressure_lines(moved, (above, below), beside, stepped)
-    operands = (squares, opened, rise_x, rise_y, quiet, across, along_inner, final, *lines)
+    operands = (weights_x, squares, opened, rise_y, quiet, across, along_inner, final, *lines)
     anywhere = pl.BlockSpec(memory_space=pl.ANY)
-    specs = {k: anywhere for k in range(len(operands))}
+    specs = {k: anywhere for k in range(1, len(operands))}
     scratch = (
         pltpu.VMEM(squares.shape, F32),
         pltpu.VMEM((2,) + opened.shape[1:], BF16),
-        pltpu.VMEM(rise_x.shape, BF16),
         pltpu.VMEM(rise_y.shape, BF16),
         pltpu.VMEM((2, parts - 1, TILE, wide), F32),
         pltpu.VMEM(across.shape, BF16),
@@ -974,7 +982,7 @@
         pltpu.VMEM((local_y + 2 * MARGIN, local_x + LANES), F32),
         pltpu.VMEM((2, local_y + 2 * HALO, full), BF16),
         pltpu.VMEM((steps, parts - 1, TILE, wide), BF16),
-        pltpu.SemaphoreType.DMA((9 + count_x,)),
+        pltpu.SemaphoreType.DMA((8 + count_x,)),
         pltpu.SemaphoreType.DMA((steps,)),
     )
     return call(

time: 100 us -> 100 us (level)
  between operations: 0.33 us -> 2.96 us
  waiting for transfers between devices: 22.1 us -> 19.7 us
    all_to_all x1, waiting for transfers between devices: 4.24 us -> 1.66 us  [pressure_lines(): solved = lax.all_to_all(solved, ('gy', 'gx'), 0, 0, tiled=True)]
    ppermute x4, waiting for transfers between devices: 4.03 us -> 5.48 us  [ring(): lax.ppermute(array, axis, [(i, (i + step) % size) for i in range(size)])]
    all_to_all x1, waiting for transfers between devices: 8.56 us -> 7.27 us  [pressure_lines(): spectra = lax.all_to_all(spectra, ('gy', 'gx'), 0, 0, tiled=True)]
  transfers between devices with their start and end apart: 12 -> 12, of which waited for: 6 -> 6; matrix products, arithmetic and copies ran while one was open for 2% -> 3% of each run, Pallas kernels for 31% -> 30%
where the time goes in v4:
time: 100 us; the launch traced here: 99.4 us
  Pallas kernels  47.2 us (47%)
  starting transfers between devices  20.8 us (21%)
  waiting for transfers between devices  19.7 us (20%)
  local copies, waits for them, and re-layouts  7.53 us (8%)
  between operations  2.96 us (3%)
  other arithmetic  1.23 us (1%)
    pallas_call x11, Pallas kernels, call(): pl.pallas_call(body, out_shape=outs, in_specs=in_specs + [pl.BlockSpec(me...  47.2 us
    all_to_all x1, waiting for transfers between devices, pressure_lines(): spectra = lax.all_to_all(spectra, ('gy', 'gx'), 0, 0, tiled=True)  7.27 us
    ppermute x4, starting transfers between devices, ring(): lax.ppermute(array, axis, [(i, (i + step) % size) for i in range(size)])  6.66 us
    unnamed x32, local copies, waits for them, and re-layouts  6.12 us
    all_to_all x1, starting transfers between devices, pressure_lines(): spectra = lax.all_to_all(spectra, ('gy', 'gx'), 0, 0, tiled=True)  5.52 us
    ppermute x4, waiting for transfers between devices, ring(): lax.ppermute(array, axis, [(i, (i + step) % size) for i in range(size)])  5.48 us
    ppermute x6, waiting for transfers between devices, swap(): lax.ppermute(array, axis, [(i, i ^ mask) for i in range(lax.axis_size(axi...  5.29 us
    ppermute x6, starting transfers between devices, swap(): lax.ppermute(array, axis, [(i, i ^ mask) for i in range(lax.axis_size(axi...  5.01 us
  transfers between devices with their start and end apart: 12, of which 6 were waited for; matrix products, arithmetic and copies ran while one was open for 3% of the time, Pallas kernels for 30%

profile of v4, /device:TPU:0, one launch (start us, length us, event | category | flops | bytes accessed | tf_op | source)
XLA Modules:
  0.0 99.4 jit_solution(12614544642662697358)
XLA Ops:
  0.0 1.2 %copy-done.1 = f32[2,1,256,512]{3,2,1,0:T(8,128)S(1)} copy-done((f32[2,1,256,512]{3,2,1,0:T(8,128)S(1)}, f32[2,1,256,512]{3,2,1,0:T(8,128)}, u32[]{:S(2)}) %copy-start.1) | copy-done | bytes 1048600
  1.2 0.1 pieces.1
  1.3 0.5 collective-permute-start
  1.8 2.6 %collective-permute-start.5 = (f32[2,64,512]{2,1,0:T(8,128)S(1)}, f32[2,64,512]{2,1,0:T(8,128)S(1)}, u32[]{:S(2)}, u32[]{:S(2)}) collective-permute-start(f32[2,64,512]{2,1,0:T(8,128)S(1)} %get-tuple-element.47), channel_id=1, source_target_pairs={{0,16},{8,24},{16,0},{24,8},{1,17},{9,25},{17,1},{25,9},{2,18},{10... | collective-permute-start | bytes 786440 | tf_op jit(solution)/shard_map/ppermute | solution.py:743
  4.4 0.1 collective-permute-start.6
  4.5 0.0 collective-permute-done.refs_6_.refs_1_
  4.5 1.6 %copy-done = s32[1,512,1024]{2,1,0:T(8,128)S(1)} copy-done((s32[1,512,1024]{2,1,0:T(8,128)S(1)}, s32[1,512,1024]{2,1,0:T(8,128)}, u32[]{:S(2)}) %copy-start) | copy-done | bytes 2097176
  6.0 1.2 %copy-done.2 = f32[2,1,256,512]{3,2,1,0:T(8,128)S(1)} copy-done((f32[2,1,256,512]{3,2,1,0:T(8,128)S(1)}, f32[2,1,256,512]{3,2,1,0:T(8,128)}, u32[]{:S(2)}) %copy-start.2) | copy-done | bytes 1048600
  7.3 1.1 %rows.1 = (f32[24,1024]{1,0:T(8,128)S(1)}, f32[24,1024]{1,0:T(8,128)S(1)}) custom-call(bf16[4,1,512,1024]{3,2,1,0:T(8,128)(2,1)} %refs_4_.9, bf16[4,1,512,1024]{3,2,1,0:T(8,128)(2,1)} %refs_4_.9, s32[1,512,1024]{2,1,0:T(8,128)S(1)} %copy-done, s32[1,512,1024]{2,1,0:T(8,128)S(1)} %copy-done, f32[2,1,256,512]{3,2,1,0:T(8,128)S(1)} %copy-done.2, ...), custom_call_target="tpu_custom_call" | custom-call | bytes 2097152 | tf_op jit(solution)/shard_map/rows/pallas_call | solution.py:724
  8.4 1.8 %collective-permute-start.1 = (f32[24,1024]{1,0:T(8,128)S(1)}, f32[24,1024]{1,0:T(8,128)S(1)}, u32[]{:S(2)}, u32[]{:S(2)}) collective-permute-start(f32[24,1024]{1,0:T(8,128)S(1)} %get-tuple-element.33), channel_id=1, source_target_pairs={{0,1},{1,2},{2,3},{3,4},{4,5},{5,6},{6,7},{7,0},{8,9},{9,10},{10,1... | collective-permute-start | bytes 294920 | tf_op jit(solution)/shard_map/ppermute | solution.py:739
  10.2 3.1 %collective-permute-start.2 = (f32[24,1024]{1,0:T(8,128)S(1)}, f32[24,1024]{1,0:T(8,128)S(1)}, u32[]{:S(2)}, u32[]{:S(2)}) collective-permute-start(f32[24,1024]{1,0:T(8,128)S(1)} %get-tuple-element.34), channel_id=1, source_target_pairs={{0,7},{1,0},{2,1},{3,2},{4,3},{5,4},{6,5},{7,6},{8,15},{9,8},{10,9... | collective-permute-start | bytes 294920 | tf_op jit(solution)/shard_map/ppermute | solution.py:739
  13.3 0.0 collective-permute-done.5.refs_2_
  13.3 3.3 %collective-permute-done.6.refs_3_ = f32[2,64,512]{2,1,0:T(8,128)S(1)} collective-permute-done((f32[2,64,512]{2,1,0:T(8,128)S(1)}, f32[2,64,512]{2,1,0:T(8,128)S(1)}, u32[]{:S(2)}, u32[]{:S(2)}) %collective-permute-start.6) | collective-permute-done | bytes 262176 | tf_op jit(solution)/shard_map/ppermute | solution.py:743
  16.6 0.0 collective-permute-done.1.refs_7_.refs_3_.refs_8_.refs_6_
  16.7 0.4 collective-permute-done.2.refs_8_.refs_4_.refs_9_.refs_7_
  17.1 2.0 %forward_x.1 = (f32[32,64,128]{2,1,0:T(8,128)}, f32[8,128]{1,0:T(8,128)S(1)}) custom-call(f32[2,64,512]{2,1,0:T(8,128)S(1)} %get-tuple-element.46.refs_0_, f32[2,64,512]{2,1,0:T(8,128)S(1)} %collective-permute-done.refs_6_.refs_1_, f32[2,64,512]{2,1,0:T(8,128)S(1)} %collective-permute-done.5.refs_2_, f32[2,64,512]{2,1,0:T(8,128)S(1)} %collective-permute-done.6.refs_3_, ...), custom_call_target="tpu_custom_call" | custom-call | flops 1000000000 | bytes 4194304 | tf_op jit(solution)/shard_map/forward_x/pallas_call | solution.py:724
  19.1 5.5 %all-to-all-start = ((f32[32,64,128]{2,1,0:T(8,128)}), f32[32,64,128]{2,1,0:T(8,128)S(1)}, u32[]{:S(2)}, u32[]{:S(2)}) async-start(f32[32,64,128]{2,1,0:T(8,128)} %get-tuple-element.49), calls=%async_computation | async-start | bytes 2097152 | tf_op jit(solution)/shard_map/all_to_all | solution.py:773
  24.7 0.6 add_convert_fusion.refs_0_
  25.3 0.0 copy-done.3
  25.3 3.0 %columns.1 = (f32[48,640]{1,0:T(8,128)}, f32[48,640]{1,0:T(8,128)}) custom-call(f32[4]{0:T(128)} %add_convert_fusion.refs_0_, bf16[4,1,512,1024]{3,2,1,0:T(8,128)(2,1)} %refs_4_.9, bf16[4,1,512,1024]{3,2,1,0:T(8,128)(2,1)} %refs_4_.9, s32[1,512,1024]{2,1,0:T(8,128)} %refs_7_.3, s32[1,512,1024]{2,1,0:T(8,128)} %refs_7_.3, f32[2,1,256,512]{3,2,1,0:T(8,128)} %refs_2_.7, ...), custom_call_target="tpu_custom_call" | custom-call | bytes 8388608 | tf_op jit(solution)/shard_map/columns/pallas_call | solution.py:724
  28.3 0.3 collective-permute-start.3
  28.6 1.5 %collective-permute-start.4 = (f32[48,640]{1,0:T(8,128)}, f32[48,640]{1,0:T(8,128)S(1)}, u32[]{:S(2)}, u32[]{:S(2)}) collective-permute-start(f32[48,640]{1,0:T(8,128)} %get-tuple-element.36), channel_id=1, source_target_pairs={{0,24},{8,0},{16,8},{24,16},{1,25},{9,1},{17,9},{25,17},{2,26},{10... | collective-permute-start | bytes 368648 | tf_op jit(solution)/shard_map/ppermute | solution.py:739
  30.1 0.6 pad_add_fusion.refs_0_
  30.7 2.2 %tables.1 = (bf16[4,144,240]{2,1,0:T(8,128)(2,1)}, s32[1]{0:T(128)}) custom-call(s32[2]{0:T(128)} %pad_add_fusion.refs_0_, f32[4,4096]{1,0:T(4,128)} %refs_1_.4), custom_call_target="tpu_custom_call" | custom-call | bytes 2097152 | tf_op jit(solution)/shard_map/tables/pallas_call | solution.py:724
  32.9 5.0 %collective-permute-done.3.refs_5_ = f32[48,640]{1,0:T(8,128)S(1)} collective-permute-done((f32[48,640]{1,0:T(8,128)}, f32[48,640]{1,0:T(8,128)S(1)}, u32[]{:S(2)}, u32[]{:S(2)}) %collective-permute-start.3) | collective-permute-done | bytes 122912 | tf_op jit(solution)/shard_map/ppermute | solution.py:739
  37.9 0.0 collective-permute-done.4.refs_6_
  37.9 0.6 copy-done.14
  38.6 0.0 copy-done.15
  38.6 3.8 %sides.1 = (f32[5,640,128]{2,1,0:T(8,128)}, f32[272,640]{1,0:T(8,128)}, s32[1]{0:T(128)}) custom-call(f32[4]{0:T(128)} %add_convert_fusion.refs_0_, s32[1]{0:T(128)} %get-tuple-element.31.refs_1_, f32[2,1,256,512]{3,2,1,0:T(8,128)} %refs_2_.7, f32[24,1024]{1,0:T(8,128)} %copy-done.3, f32[24,1024]{1,0:T(8,128)} %copy-done.4, f32[48,640]{1,0:T(8,128)} %copy-done.14, ...), custom_call_target="tpu_custom_call" | custom-call | bytes 8388608 | tf_op jit(solution)/shard_map/sides/pallas_call | solution.py:724
  42.9 0.7 constant_dynamic-slice_fusion.refs_2_
  43.6 7.3 %all-to-all-done.refs_0_ = f32[32,64,128]{2,1,0:T(8,128)S(1)} async-done(((f32[32,64,128]{2,1,0:T(8,128)}), f32[32,64,128]{2,1,0:T(8,128)S(1)}, u32[]{:S(2)}, u32[]{:S(2)}) %all-to-all-start) | async-done | bytes 1048608 | tf_op jit(solution)/shard_map/all_to_all | solution.py:773
  50.9 4.2 %solve_y.1 = f32[32,40,128]{2,1,0:T(8,128)} custom-call(f32[32,64,128]{2,1,0:T(8,128)S(1)} %all-to-all-done.refs_0_, f32[8,128]{1,0:T(8,128)S(1)} %get-tuple-element.50.refs_1_, f32[1,128]{1,0:T(1,128)S(1)} %constant_dynamic-slice_fusion.refs_2_, bf16[1024,256]{1,0:T(8,128)(2,1)S(1)} %copy-done.8, bf16[256,48]{1,0:T(8,128)(2,1)S(1)} %copy-done.9), custom_call_target="tpu_custom_call" | custom-call | flops 4000000000 | bytes 6291456 | tf_op jit(solution)/shard_map/solve_y/pallas_call | solution.py:724
  55.2 3.6 %all-to-all-start.1 = ((f32[32,40,128]{2,1,0:T(8,128)}), f32[32,40,128]{2,1,0:T(8,128)S(1)}, u32[]{:S(2)}, u32[]{:S(2)}) async-start(f32[32,40,128]{2,1,0:T(8,128)} %solve_y.1), calls=%async_computation.1 | async-start | bytes 1310720 | tf_op jit(solution)/shard_map/all_to_all | solution.py:795
  58.8 0.0 copy-start.6
  58.8 13.5 %quiet_step.2 = (f32[3,512,1024]{2,1,0:T(8,128)}, bf16[4,1,512,1024]{3,2,1,0:T(8,128)(2,1)}, bf16[4,144,1152]{2,1,0:T(8,128)(2,1)}, s32[1]{0:T(128)}) custom-call(f32[4]{0:T(128)} %add_convert_fusion.refs_0_, s32[1]{0:T(128)} %bitcast.4.refs_1_, bf16[4,1,512,1024]{3,2,1,0:T(8,128)(2,1)} %refs_4_.9, bf16[4,1,512,1024]{3,2,1,0:T(8,128)(2,1)} %refs_4_.9, ...), custom_call_target="tpu_custom_call" | custom-call | flops 8999999488 | bytes 37748736 | tf_op jit(solution)/shard_map/quiet_step/pallas_call | solution.py:724
  74.3 0.7 dynamic-slice_bitcast_fusion.refs_2_
  75.0 1.7 %all-to-all-done.1.refs_0_ = f32[32,40,128]{2,1,0:T(8,128)S(1)} async-done(((f32[32,40,128]{2,1,0:T(8,128)}), f32[32,40,128]{2,1,0:T(8,128)S(1)}, u32[]{:S(2)}, u32[]{:S(2)}) %all-to-all-start.1) | async-done | bytes 655392 | tf_op jit(solution)/shard_map/all_to_all | solution.py:795
  76.7 1.3 %inverse_x.1 = (f32[72,640]{1,0:T(8,128)S(1)}, f32[72,640]{1,0:T(8,128)S(1)}, f32[72,640]{1,0:T(8,128)S(1)}, f32[72,640]{1,0:T(8,128)S(1)}) custom-call(f32[32,40,128]{2,1,0:T(8,128)S(1)} %all-to-all-done.1.refs_0_, bf16[1536,512]{1,0:T(8,128)(2,1)S(1)} %copy-done.6, f32[8,256]{1,0:T(8,128)S(1)} %dynamic-slice_bitcast_fusion.refs_2_), custom_call_target="tpu_custom_call" | custom-call | flops 1000000000 | bytes 4194304 | tf_op jit(solution)/shard_map/inverse_x/pallas_call | solution.py:724
  78.1 0.7 copy-done.5
  78.8 0.1 collective-permute-start.7
  78.8 1.6 %collective-permute-start.8 = (f32[72,640]{1,0:T(8,128)S(1)}, f32[72,640]{1,0:T(8,128)S(1)}, u32[]{:S(2)}, u32[]{:S(2)}) collective-permute-start(f32[72,640]{1,0:T(8,128)S(1)} %get-tuple-element.55), channel_id=1, source_target_pairs={{0,16},{8,24},{16,0},{24,8},{1,17},{9,25},{17,1},{25,9},{2,18},{10... | collective-permute-start | bytes 552968 | tf_op jit(solution)/shard_map/ppermute | solution.py:743
  80.4 0.2 collective-permute-start.9
  80.6 6.7 %quiet_step.3 = (f32[3,512,1024]{2,1,0:T(8,128)}, bf16[4,1,512,1024]{3,2,1,0:T(8,128)(2,1)}, bf16[4,144,1152]{2,1,0:T(8,128)(2,1)}, s32[1]{0:T(128)}) custom-call(f32[4]{0:T(128)} %add_convert_fusion.refs_0_, s32[1]{0:T(128)} %bitcast.4.refs_1_, bf16[4,1,512,1024]{3,2,1,0:T(8,128)(2,1)} %refs_4_.9, ...), custom_call_target="tpu_custom_call", output_to_operand_aliasing={{0}: (14, {}), {1}: (15, {}), {2}: (16, {})} | custom-call | flops 3000000000 | bytes 12582912 | tf_op jit(solution)/shard_map/quiet_step/pallas_call | solution.py:724
  87.3 0.0 collective-permute-done.7.refs_9_
  87.3 0.0 collective-permute-done.8.refs_10_
  87.3 2.0 %collective-permute-done.9.refs_11_ = f32[72,640]{1,0:T(8,128)S(1)} collective-permute-done((f32[72,640]{1,0:T(8,128)S(1)}, f32[72,640]{1,0:T(8,128)S(1)}, u32[]{:S(2)}, u32[]{:S(2)}) %collective-permute-start.9) | collective-permute-done | bytes 184352 | tf_op jit(solution)/shard_map/ppermute | solution.py:743
  89.3 0.7 copy-done.13
  90.0 9.3 %source_step.1 = bf16[4,1,512,1024]{3,2,1,0:T(8,128)(2,1)} custom-call(f32[4,4096]{1,0:T(4,128)} %refs_0_.5, f32[272,640]{1,0:T(8,128)} %get-tuple-element.37.refs_1_, bf16[4,144,1152]{2,1,0:T(8,128)(2,1)} %get-tuple-element.42.refs_2_, bf16[4,144,240]{2,1,0:T(8,128)(2,1)} %get-tuple-element.43.refs_3_, ...), custom_call_target="tpu_custom_call", output_to_operand_aliasing={{}: (7, {})} | custom-call | flops 4000000000 | bytes 16777216 | tf_op jit(solution)/shard_map/source_step/pallas_call | solution.py:724
  (23 shorter events, 0.0 us)
Async XLA Ops:
  0.0 1.2 %copy-start.1 = (f32[2,1,256,512]{3,2,1,0:T(8,128)S(1)}, f32[2,1,256,512]{3,2,1,0:T(8,128)}, u32[]{:S(2)}) copy-start(f32[2,1,256,512]{3,2,1,0:T(8,128)} %refs_2_.7) | copy-start | bytes 3145732
  1.3 3.2 %collective-permute-start = (f32[2,64,512]{2,1,0:T(8,128)S(1)}, f32[2,64,512]{2,1,0:T(8,128)S(1)}, u32[]{:S(2)}, u32[]{:S(2)}) collective-permute-start(f32[2,64,512]{2,1,0:T(8,128)S(1)} %get-tuple-element.32), channel_id=1, source_target_pairs={{0,8},{8,0},{16,24},{24,16},{1,9},{9,1},{17,25},{25,17},{2,10},{10... | collective-permute-start | bytes 786440 | tf_op jit(solution)/shard_map/ppermute | solution.py:743
  1.8 11.5 %collective-permute-start.5 = (f32[2,64,512]{2,1,0:T(8,128)S(1)}, f32[2,64,512]{2,1,0:T(8,128)S(1)}, u32[]{:S(2)}, u32[]{:S(2)}) collective-permute-start(f32[2,64,512]{2,1,0:T(8,128)S(1)} %get-tuple-element.47), channel_id=1, source_target_pairs={{0,16},{8,24},{16,0},{24,8},{1,17},{9,25},{17,1},{25,9},{2,18},{10... | collective-permute-start | bytes 786440 | tf_op jit(solution)/shard_map/ppermute | solution.py:743
  4.4 12.3 %collective-permute-start.6 = (f32[2,64,512]{2,1,0:T(8,128)S(1)}, f32[2,64,512]{2,1,0:T(8,128)S(1)}, u32[]{:S(2)}, u32[]{:S(2)}) collective-permute-start(f32[2,64,512]{2,1,0:T(8,128)S(1)} %get-tuple-element.48), channel_id=1, source_target_pairs={{0,24},{8,16},{16,8},{24,0},{1,25},{9,17},{17,9},{25,1},{2,26},{10... | collective-permute-start | bytes 786440 | tf_op jit(solution)/shard_map/ppermute | solution.py:743
  4.5 1.6 %copy-start = (s32[1,512,1024]{2,1,0:T(8,128)S(1)}, s32[1,512,1024]{2,1,0:T(8,128)}, u32[]{:S(2)}) copy-start(s32[1,512,1024]{2,1,0:T(8,128)} %refs_7_.3) | copy-start | bytes 6291460
  6.0 1.2 %copy-start.2 = (f32[2,1,256,512]{3,2,1,0:T(8,128)S(1)}, f32[2,1,256,512]{3,2,1,0:T(8,128)}, u32[]{:S(2)}) copy-start(f32[2,1,256,512]{3,2,1,0:T(8,128)} %refs_2_.7) | copy-start | bytes 3145732
  7.3 9.8 %copy-start.7 = (bf16[1536,512]{1,0:T(8,128)(2,1)S(1)}, bf16[1536,512]{1,0:T(8,128)(2,1)}, u32[]{:S(2)}) copy-start(bf16[1536,512]{1,0:T(8,128)(2,1)} %constant.41.clone.refs_4_) | copy-start | bytes 4718596
  7.3 9.8 %copy-start.10 = (f32[8,256]{1,0:T(8,128)S(1)}, f32[8,256]{1,0:T(8,128)}, u32[]{:S(2)}) copy-start(f32[8,256]{1,0:T(8,128)} %constant.42.clone.refs_5_) | copy-start | bytes 24580
  8.4 8.3 %collective-permute-start.1 = (f32[24,1024]{1,0:T(8,128)S(1)}, f32[24,1024]{1,0:T(8,128)S(1)}, u32[]{:S(2)}, u32[]{:S(2)}) collective-permute-start(f32[24,1024]{1,0:T(8,128)S(1)} %get-tuple-element.33), channel_id=1, source_target_pairs={{0,1},{1,2},{2,3},{3,4},{4,5},{5,6},{6,7},{7,0},{8,9},{9,10},{10,1... | collective-permute-start | bytes 294920 | tf_op jit(solution)/shard_map/ppermute | solution.py:739
  10.2 6.9 %collective-permute-start.2 = (f32[24,1024]{1,0:T(8,128)S(1)}, f32[24,1024]{1,0:T(8,128)S(1)}, u32[]{:S(2)}, u32[]{:S(2)}) collective-permute-start(f32[24,1024]{1,0:T(8,128)S(1)} %get-tuple-element.34), channel_id=1, source_target_pairs={{0,7},{1,0},{2,1},{3,2},{4,3},{5,4},{6,5},{7,6},{8,15},{9,8},{10,9... | collective-permute-start | bytes 294920 | tf_op jit(solution)/shard_map/ppermute | solution.py:739
  16.7 8.7 %copy-start.3 = (f32[24,1024]{1,0:T(8,128)}, f32[24,1024]{1,0:T(8,128)S(1)}, u32[]{:S(2)}) copy-start(f32[24,1024]{1,0:T(8,128)S(1)} %collective-permute-done.1.refs_7_.refs_3_.refs_8_.refs_6_) | copy-start | bytes 294916
  17.1 8.2 %copy-start.4 = (f32[24,1024]{1,0:T(8,128)}, f32[24,1024]{1,0:T(8,128)S(1)}, u32[]{:S(2)}) copy-start(f32[24,1024]{1,0:T(8,128)S(1)} %collective-permute-done.2.refs_8_.refs_4_.refs_9_.refs_7_) | copy-start | bytes 294916
  19.1 31.8 %all-to-all-start = ((f32[32,64,128]{2,1,0:T(8,128)}), f32[32,64,128]{2,1,0:T(8,128)S(1)}, u32[]{:S(2)}, u32[]{:S(2)}) async-start(f32[32,64,128]{2,1,0:T(8,128)} %get-tuple-element.49), calls=%async_computation | async-start | bytes 2097152 | tf_op jit(solution)/shard_map/all_to_all | solution.py:773
  25.3 25.6 %copy-start.8 = (bf16[1024,256]{1,0:T(8,128)(2,1)S(1)}, bf16[1024,256]{1,0:T(8,128)(2,1)}, u32[]{:S(2)}) copy-start(bf16[1024,256]{1,0:T(8,128)(2,1)} %constant.44.clone.refs_3_) | copy-start | bytes 1572868
  25.3 25.6 %copy-start.9 = (bf16[256,48]{1,0:T(8,128)(2,1)S(1)}, bf16[256,48]{1,0:T(8,128)(2,1)}, u32[]{:S(2)}) copy-start(bf16[256,48]{1,0:T(8,128)(2,1)} %constant.45.clone.refs_4_) | copy-start | bytes 73732
  28.3 9.6 %collective-permute-start.3 = (f32[48,640]{1,0:T(8,128)}, f32[48,640]{1,0:T(8,128)S(1)}, u32[]{:S(2)}, u32[]{:S(2)}) collective-permute-start(f32[48,640]{1,0:T(8,128)} %get-tuple-element.35), channel_id=1, source_target_pairs={{0,8},{8,16},{16,24},{24,0},{1,9},{9,17},{17,25},{25,1},{2,10},{10... | collective-permute-start | bytes 368648 | tf_op jit(solution)/shard_map/ppermute | solution.py:739
  28.6 9.3 %collective-permute-start.4 = (f32[48,640]{1,0:T(8,128)}, f32[48,640]{1,0:T(8,128)S(1)}, u32[]{:S(2)}, u32[]{:S(2)}) collective-permute-start(f32[48,640]{1,0:T(8,128)} %get-tuple-element.36), channel_id=1, source_target_pairs={{0,24},{8,0},{16,8},{24,16},{1,25},{9,1},{17,9},{25,17},{2,26},{10... | collective-permute-start | bytes 368648 | tf_op jit(solution)/shard_map/ppermute | solution.py:739
  37.9 0.7 copy-start.14
  37.9 0.7 copy-start.15
  55.2 21.5 %all-to-all-start.1 = ((f32[32,40,128]{2,1,0:T(8,128)}), f32[32,40,128]{2,1,0:T(8,128)S(1)}, u32[]{:S(2)}, u32[]{:S(2)}) async-start(f32[32,40,128]{2,1,0:T(8,128)} %solve_y.1), calls=%async_computation.1 | async-start | bytes 1310720 | tf_op jit(solution)/shard_map/all_to_all | solution.py:795
  58.8 17.9 %copy-start.6 = (bf16[1536,512]{1,0:T(8,128)(2,1)S(1)}, bf16[1536,512]{1,0:T(8,128)(2,1)}, u32[]{:S(2)}) copy-start(bf16[1536,512]{1,0:T(8,128)(2,1)} %constant.47.clone.refs_1_) | copy-start | bytes 4718596
  78.1 0.7 copy-start.5
  78.8 8.5 %collective-permute-start.7 = (f32[72,640]{1,0:T(8,128)S(1)}, f32[72,640]{1,0:T(8,128)S(1)}, u32[]{:S(2)}, u32[]{:S(2)}) collective-permute-start(f32[72,640]{1,0:T(8,128)S(1)} %get-tuple-element.54), channel_id=1, source_target_pairs={{0,8},{8,0},{16,24},{24,16},{1,9},{9,1},{17,25},{25,17},{2,10},{10... | collective-permute-start | bytes 552968 | tf_op jit(solution)/shard_map/ppermute | solution.py:743
  78.8 8.5 %collective-permute-start.8 = (f32[72,640]{1,0:T(8,128)S(1)}, f32[72,640]{1,0:T(8,128)S(1)}, u32[]{:S(2)}, u32[]{:S(2)}) collective-permute-start(f32[72,640]{1,0:T(8,128)S(1)} %get-tuple-element.55), channel_id=1, source_target_pairs={{0,16},{8,24},{16,0},{24,8},{1,17},{9,25},{17,1},{25,9},{2,18},{10... | collective-permute-start | bytes 552968 | tf_op jit(solution)/shard_map/ppermute | solution.py:743
  80.4 8.9 %collective-permute-start.9 = (f32[72,640]{1,0:T(8,128)S(1)}, f32[72,640]{1,0:T(8,128)S(1)}, u32[]{:S(2)}, u32[]{:S(2)}) collective-permute-start(f32[72,640]{1,0:T(8,128)S(1)} %get-tuple-element.56), channel_id=1, source_target_pairs={{0,24},{8,16},{16,8},{24,0},{1,25},{9,17},{17,9},{25,1},{2,26},{10... | collective-permute-start | bytes 552968 | tf_op jit(solution)/shard_map/ppermute | solution.py:743
  87.3 2.0 %copy-start.11 = (f32[72,640]{1,0:T(8,128)}, f32[72,640]{1,0:T(8,128)S(1)}, u32[]{:S(2)}) copy-start(f32[72,640]{1,0:T(8,128)S(1)} %collective-permute-done.7.refs_9_) | copy-start | bytes 552964
  87.3 2.0 %copy-start.12 = (f32[72,640]{1,0:T(8,128)}, f32[72,640]{1,0:T(8,128)S(1)}, u32[]{:S(2)}) copy-start(f32[72,640]{1,0:T(8,128)S(1)} %collective-permute-done.8.refs_10_) | copy-start | bytes 552964
  89.3 0.7 copy-start.13

commit v5 on v2

--- a/solution.py
+++ b/solution.py
@@ -311,7 +311,7 @@
     ]
 
 
-def solve_y_kernel(count_x, _, lines, total, wave, both, turns, out, held, spread, made, sent):
+def solve_y_kernel(count_x, lines, total, wave, both, turns, out, held, spread, made, sent):
     count, rows, _ = lines.shape
     base = turns.shape[0]
     length = count * rows
@@ -345,7 +345,8 @@
     kx = wave[0:1, :]
     first = lanes % 64 < 32
     edge = jnp.float32(length // 2)
-    alone = jnp.where(first, kx * kx, 0.0)
+    square_kx = kx * kx
+    alone = jnp.where(first, square_kx, 0.0)
     slope = jnp.where(first | (kx == -edge), 0.0, jnp.broadcast_to(kx, lanes.shape))
     q = lax.broadcasted_iota(jnp.int32, lanes.shape, 0)
     low_ky = RADIX * (q - jnp.where(q < base // 2, 0, base)).astype(F32)
@@ -358,7 +359,9 @@
         if r == 0:
             corner = jnp.where((kx == -edge) & ~first, edge * edge, 0.0)
             symbol = jnp.where(ky == -edge, jnp.where(first, alone, corner), symbol)
-        terms.append(symbol * pl.reciprocal(kx * kx + ky * ky) * spectrum)
+        square = square_kx + ky * ky
+        guess = pl.reciprocal(square, approx=True)
+        terms.append(symbol * (guess * (2.0 - square * guess)) * spectrum)
     pairs = [
         jnp.where(first, low + spin(low, -32), high + spin(high, 32))
         for low, high in zip(terms[:4], terms[4:])
@@ -411,9 +414,10 @@
 
 
 def inverse_x_kernel(
-    kept, scale, place, lines, tables, turns, *refs
+    kept, scale, lines, tables, turns, *refs
 ):
     *outs, held = refs
+    place = lax.axis_index("gx")
     count, half, _ = lines.shape
     base = turns.shape[1]
     length = RADIX * base
@@ -461,7 +465,7 @@
     targets, local = len(outs), outs[0].shape[1] - LANES
     right = lane_index((kept, LANES)) < 64
     for mask, out in enumerate(outs):
-        start = pl.multiple_of((place[0] ^ mask) * local, LANES)
+        start = pl.multiple_of((place ^ mask) * local, LANES)
         after = pl.multiple_of(jnp.where(start + local == length, 0, start + local), LANES)
         before = pl.multiple_of(jnp.where(start == 0, length, start) - LANES, LANES)
         out[:, :local] = held[:, pl.ds(start, local)]
@@ -745,7 +749,6 @@
     _, rows, local_x = pieces[0].shape
     count_x, count_y = lax.axis_size("gx"), lax.axis_size("gy")
     count = count_x * count_y
-    scalars = {0: pl.BlockSpec(memory_space=pltpu.SMEM)}
     length_x, length_y = local_x * count_x, rows * count
     full, zero, middle, cos_turn, sin_turn = x_tables(length_x)
     turns = np.zeros((8, cos_turn.shape[1]), np.float32)
@@ -766,7 +769,7 @@
         name="forward_x",
     )
     spectra = lax.all_to_all(spectra, ("gy", "gx"), 0, 0, tiled=True)
-    place = lax.axis_index("gy") * count_x + lax.axis_index("gx")
+    place = lax.axis_index("gy") * count_x + spread[0]
     waves = jnp.asarray(wave_table(length_x, count))
     wave = lax.dynamic_slice(waves, (place, 0), (1, LANES))
     both, turns_y = y_tables(length_y)
@@ -774,7 +777,7 @@
     half = (kept // 2 + 8) // 8 * 8
     solved = call(
         functools.partial(solve_y_kernel, count_x),
-        (spread, spectra, total, wave, beside(both), turns_y),
+        (spectra, total, wave, beside(both), turns_y),
         shaped(count, half, LANES),
         (
             pltpu.VMEM((length_y + 2 * MARGIN, LANES), F32),
@@ -782,7 +785,6 @@
             pltpu.VMEM((count, half, LANES), F32),
             pltpu.SemaphoreType.DMA((count // RADIX,)),
         ),
-        specs=scalars,
         out_specs=pl.BlockSpec(memory_space=pl.ANY),
         flops=4 * 10**9,
         moved=6 << 20,
@@ -794,12 +796,13 @@
     tables = np.concatenate(
         [beside(full.T), beside(back, 2.0 * middle.T)]
     )
+    again = jnp.asarray(np.tile(turns, (count_x, 1, 1)))
+    again = lax.dynamic_slice(again, (stepped[0], 0, 0), (1,) + turns.shape)
     pressed = call(
         functools.partial(inverse_x_kernel, kept, 1.0 / (length_x * length_y)),
-        (stepped, solved, tables, turns),
+        (solved, tables, again[0]),
         (shaped(kept, local_x + LANES),) * count_x,
         (pltpu.VMEM((kept, length_x), F32),),
-        specs=scalars,
         flops=10**9,
         moved=4 << 20,
         name="inverse_x",
@@ -953,7 +956,7 @@
             ),
             after=before,
             aliases={len(operands) + k: k for k in range(len(before))},
-            megabytes=54 if first == 0 else 50,
+            megabytes=54,
             flops=3 * 10**9 * count,
             moved=(12 << 20) * count,
             name="quiet_step",

time: 103 us -> 98.7 us (0.958)
  waiting for transfers between devices: 21.8 us -> 18.9 us
  between operations: 0.41 us -> 2.82 us
  local copies, waits for them, and re-layouts: 9.34 us -> 7.5 us
  Pallas kernels: 48.1 us -> 46.6 us
    all_to_all x1, waiting for transfers between devices: 4.26 us -> 1.68 us  [pressure_lines(): solved = lax.all_to_all(solved, ('gy', 'gx'), 0, 0, tiled=True)]
    unnamed x50 -> x32, local copies, waits for them, and re-layouts: 8.64 us -> 6.09 us
    pallas_call x11, Pallas kernels: 48.1 us -> 46.6 us  [call(): pl.pallas_call(body, out_shape=outs, in_specs=in_specs + [pl.BlockSpec(me...]
    all_to_all x1, waiting for transfers between devices: 8.53 us -> 7.23 us  [pressure_lines(): spectra = lax.all_to_all(spectra, ('gy', 'gx'), 0, 0, tiled=True)]
  transfers between devices with their start and end apart: 12 -> 12, of which waited for: 6 -> 6; matrix products, arithmetic and copies ran while one was open for 2% -> 3% of each run, Pallas kernels for 30% -> 32%
where the time goes in v5:
time: 98.7 us; the launch traced here: 98.1 us
  Pallas kernels  46.6 us (47%)
  starting transfers between devices  21 us (21%)
  waiting for transfers between devices  18.9 us (19%)
  local copies, waits for them, and re-layouts  7.5 us (8%)
  between operations  2.82 us (3%)
  other arithmetic  1.17 us (1%)
    pallas_call x11, Pallas kernels, call(): pl.pallas_call(body, out_shape=outs, in_specs=in_specs + [pl.BlockSpec(me...  46.6 us
    all_to_all x1, waiting for transfers between devices, pressure_lines(): spectra = lax.all_to_all(spectra, ('gy', 'gx'), 0, 0, tiled=True)  7.23 us
    ppermute x4, starting transfers between devices, ring(): lax.ppermute(array, axis, [(i, (i + step) % size) for i in range(size)])  6.66 us
    unnamed x32, local copies, waits for them, and re-layouts  6.09 us
    all_to_all x1, starting transfers between devices, pressure_lines(): spectra = lax.all_to_all(spectra, ('gy', 'gx'), 0, 0, tiled=True)  5.52 us
    ppermute x6, waiting for transfers between devices, swap(): lax.ppermute(array, axis, [(i, i ^ mask) for i in range(lax.axis_size(axi...  5.3 us
    ppermute x6, starting transfers between devices, swap(): lax.ppermute(array, axis, [(i, i ^ mask) for i in range(lax.axis_size(axi...  5.01 us
    ppermute x4, waiting for transfers between devices, ring(): lax.ppermute(array, axis, [(i, (i + step) % size) for i in range(size)])  4.73 us
  transfers between devices with their start and end apart: 12, of which 6 were waited for; matrix products, arithmetic and copies ran while one was open for 3% of the time, Pallas kernels for 32%

profile of v5, /device:TPU:0, one launch (start us, length us, event | category | flops | bytes accessed | tf_op | source)
XLA Modules:
  0.0 98.1 jit_solution(17734500102244799160)
XLA Ops:
  0.0 1.2 %copy-done.1 = f32[2,1,256,512]{3,2,1,0:T(8,128)S(1)} copy-done((f32[2,1,256,512]{3,2,1,0:T(8,128)S(1)}, f32[2,1,256,512]{3,2,1,0:T(8,128)}, u32[]{:S(2)}) %copy-start.1) | copy-done | bytes 1048600
  1.2 0.1 pieces.1
  1.3 0.5 collective-permute-start
  1.8 2.6 %collective-permute-start.5 = (f32[2,64,512]{2,1,0:T(8,128)S(1)}, f32[2,64,512]{2,1,0:T(8,128)S(1)}, u32[]{:S(2)}, u32[]{:S(2)}) collective-permute-start(f32[2,64,512]{2,1,0:T(8,128)S(1)} %get-tuple-element.49), channel_id=1, source_target_pairs={{0,16},{8,24},{16,0},{24,8},{1,17},{9,25},{17,1},{25,9},{2,18},{10... | collective-permute-start | bytes 786440 | tf_op jit(solution)/shard_map/ppermute | solution.py:741
  4.4 0.1 collective-permute-start.6
  4.5 0.0 collective-permute-done.refs_6_.refs_1_
  4.5 1.6 %copy-done = s32[1,512,1024]{2,1,0:T(8,128)S(1)} copy-done((s32[1,512,1024]{2,1,0:T(8,128)S(1)}, s32[1,512,1024]{2,1,0:T(8,128)}, u32[]{:S(2)}) %copy-start) | copy-done | bytes 2097176
  6.0 1.2 %copy-done.2 = f32[2,1,256,512]{3,2,1,0:T(8,128)S(1)} copy-done((f32[2,1,256,512]{3,2,1,0:T(8,128)S(1)}, f32[2,1,256,512]{3,2,1,0:T(8,128)}, u32[]{:S(2)}) %copy-start.2) | copy-done | bytes 1048600
  7.3 1.1 %rows.1 = (f32[24,1024]{1,0:T(8,128)S(1)}, f32[24,1024]{1,0:T(8,128)S(1)}) custom-call(bf16[4,1,512,1024]{3,2,1,0:T(8,128)(2,1)} %refs_4_.9, bf16[4,1,512,1024]{3,2,1,0:T(8,128)(2,1)} %refs_4_.9, s32[1,512,1024]{2,1,0:T(8,128)S(1)} %copy-done, s32[1,512,1024]{2,1,0:T(8,128)S(1)} %copy-done, f32[2,1,256,512]{3,2,1,0:T(8,128)S(1)} %copy-done.2, ...), custom_call_target="tpu_custom_call" | custom-call | bytes 2097152 | tf_op jit(solution)/shard_map/rows/pallas_call | solution.py:722
  8.4 1.8 %collective-permute-start.1 = (f32[24,1024]{1,0:T(8,128)S(1)}, f32[24,1024]{1,0:T(8,128)S(1)}, u32[]{:S(2)}, u32[]{:S(2)}) collective-permute-start(f32[24,1024]{1,0:T(8,128)S(1)} %get-tuple-element.34), channel_id=1, source_target_pairs={{0,1},{1,2},{2,3},{3,4},{4,5},{5,6},{6,7},{7,0},{8,9},{9,10},{10,1... | collective-permute-start | bytes 294920 | tf_op jit(solution)/shard_map/ppermute | solution.py:737
  10.2 3.1 %collective-permute-start.2 = (f32[24,1024]{1,0:T(8,128)S(1)}, f32[24,1024]{1,0:T(8,128)S(1)}, u32[]{:S(2)}, u32[]{:S(2)}) collective-permute-start(f32[24,1024]{1,0:T(8,128)S(1)} %get-tuple-element.35), channel_id=1, source_target_pairs={{0,7},{1,0},{2,1},{3,2},{4,3},{5,4},{6,5},{7,6},{8,15},{9,8},{10,9... | collective-permute-start | bytes 294920 | tf_op jit(solution)/shard_map/ppermute | solution.py:737
  13.3 0.0 collective-permute-done.5.refs_2_
  13.3 3.3 %collective-permute-done.6.refs_3_ = f32[2,64,512]{2,1,0:T(8,128)S(1)} collective-permute-done((f32[2,64,512]{2,1,0:T(8,128)S(1)}, f32[2,64,512]{2,1,0:T(8,128)S(1)}, u32[]{:S(2)}, u32[]{:S(2)}) %collective-permute-start.6) | collective-permute-done | bytes 262176 | tf_op jit(solution)/shard_map/ppermute | solution.py:741
  16.6 0.0 collective-permute-done.1.refs_7_.refs_3_.refs_8_.refs_6_
  16.7 0.4 collective-permute-done.2.refs_8_.refs_4_.refs_9_.refs_7_
  17.1 2.0 %forward_x.1 = (f32[32,64,128]{2,1,0:T(8,128)}, f32[8,128]{1,0:T(8,128)S(1)}) custom-call(f32[2,64,512]{2,1,0:T(8,128)S(1)} %get-tuple-element.48.refs_0_, f32[2,64,512]{2,1,0:T(8,128)S(1)} %collective-permute-done.refs_6_.refs_1_, f32[2,64,512]{2,1,0:T(8,128)S(1)} %collective-permute-done.5.refs_2_, f32[2,64,512]{2,1,0:T(8,128)S(1)} %collective-permute-done.6.refs_3_, ...), custom_call_target="tpu_custom_call" | custom-call | flops 1000000000 | bytes 4194304 | tf_op jit(solution)/shard_map/forward_x/pallas_call | solution.py:722
  19.2 5.5 %all-to-all-start = ((f32[32,64,128]{2,1,0:T(8,128)}), f32[32,64,128]{2,1,0:T(8,128)S(1)}, u32[]{:S(2)}, u32[]{:S(2)}) async-start(f32[32,64,128]{2,1,0:T(8,128)} %get-tuple-element.51), calls=%async_computation | async-start | bytes 2097152 | tf_op jit(solution)/shard_map/all_to_all | solution.py:771
  24.7 0.6 add_convert_fusion.refs_0_
  25.3 3.0 %columns.1 = (f32[48,640]{1,0:T(8,128)}, f32[48,640]{1,0:T(8,128)}) custom-call(f32[4]{0:T(128)} %add_convert_fusion.refs_0_, bf16[4,1,512,1024]{3,2,1,0:T(8,128)(2,1)} %refs_4_.9, bf16[4,1,512,1024]{3,2,1,0:T(8,128)(2,1)} %refs_4_.9, s32[1,512,1024]{2,1,0:T(8,128)} %refs_7_.3, s32[1,512,1024]{2,1,0:T(8,128)} %refs_7_.3, f32[2,1,256,512]{3,2,1,0:T(8,128)} %refs_2_.9, ...), custom_call_target="tpu_custom_call" | custom-call | bytes 8388608 | tf_op jit(solution)/shard_map/columns/pallas_call | solution.py:722
  28.3 0.3 collective-permute-start.3
  28.5 1.5 %collective-permute-start.4 = (f32[48,640]{1,0:T(8,128)}, f32[48,640]{1,0:T(8,128)S(1)}, u32[]{:S(2)}, u32[]{:S(2)}) collective-permute-start(f32[48,640]{1,0:T(8,128)} %get-tuple-element.37), channel_id=1, source_target_pairs={{0,24},{8,0},{16,8},{24,16},{1,25},{9,1},{17,9},{25,17},{2,26},{10... | collective-permute-start | bytes 368648 | tf_op jit(solution)/shard_map/ppermute | solution.py:737
  30.0 0.6 pad_add_fusion.refs_0_
  30.6 3.0 %tables.1 = (bf16[2,5,256,256]{3,2,1,0:T(8,128)(2,1)}, bf16[4,144,240]{2,1,0:T(8,128)(2,1)}, s32[1]{0:T(128)}) custom-call(s32[2]{0:T(128)} %pad_add_fusion.refs_0_, f32[4,4096]{1,0:T(4,128)} %refs_1_.4, f32[4,4096]{1,0:T(4,128)} %refs_2_.6), custom_call_target="tpu_custom_call" | custom-call | bytes 4194304 | tf_op jit(solution)/shard_map/tables/pallas_call | solution.py:722
  33.6 4.3 %collective-permute-done.3.refs_5_ = f32[48,640]{1,0:T(8,128)S(1)} collective-permute-done((f32[48,640]{1,0:T(8,128)}, f32[48,640]{1,0:T(8,128)S(1)}, u32[]{:S(2)}, u32[]{:S(2)}) %collective-permute-start.3) | collective-permute-done | bytes 122912 | tf_op jit(solution)/shard_map/ppermute | solution.py:737
  37.9 0.0 collective-permute-done.4.refs_6_
  37.9 0.6 copy-done.14
  38.6 0.0 copy-done.15
  38.6 3.8 %sides.1 = (f32[5,640,128]{2,1,0:T(8,128)}, f32[272,640]{1,0:T(8,128)}, s32[1]{0:T(128)}) custom-call(f32[4]{0:T(128)} %add_convert_fusion.refs_0_, s32[1]{0:T(128)} %get-tuple-element.32.refs_1_, f32[2,1,256,512]{3,2,1,0:T(8,128)} %refs_2_.9, f32[24,1024]{1,0:T(8,128)} %copy-done.3, f32[24,1024]{1,0:T(8,128)} %copy-done.4, f32[48,640]{1,0:T(8,128)} %copy-done.14, ...), custom_call_target="tpu_custom_call" | custom-call | bytes 8388608 | tf_op jit(solution)/shard_map/sides/pallas_call | solution.py:722
  43.0 0.7 constant_dynamic-slice_fusion.refs_2_
  43.7 7.2 %all-to-all-done.refs_0_ = f32[32,64,128]{2,1,0:T(8,128)S(1)} async-done(((f32[32,64,128]{2,1,0:T(8,128)}), f32[32,64,128]{2,1,0:T(8,128)S(1)}, u32[]{:S(2)}, u32[]{:S(2)}) %all-to-all-start) | async-done | bytes 1048608 | tf_op jit(solution)/shard_map/all_to_all | solution.py:771
  50.9 0.0 copy-done.8
  50.9 4.3 %solve_y.1 = f32[32,40,128]{2,1,0:T(8,128)} custom-call(f32[32,64,128]{2,1,0:T(8,128)S(1)} %all-to-all-done.refs_0_, f32[8,128]{1,0:T(8,128)S(1)} %get-tuple-element.52.refs_1_, f32[1,128]{1,0:T(1,128)S(1)} %constant_dynamic-slice_fusion.refs_2_, bf16[1024,256]{1,0:T(8,128)(2,1)S(1)} %copy-done.8, bf16[256,48]{1,0:T(8,128)(2,1)S(1)} %copy-done.9), custom_call_target="tpu_custom_call" | custom-call | flops 4000000000 | bytes 6291456 | tf_op jit(solution)/shard_map/solve_y/pallas_call | solution.py:722
  55.2 3.8 %all-to-all-start.1 = ((f32[32,40,128]{2,1,0:T(8,128)}), f32[32,40,128]{2,1,0:T(8,128)S(1)}, u32[]{:S(2)}, u32[]{:S(2)}) async-start(f32[32,40,128]{2,1,0:T(8,128)} %solve_y.1), calls=%async_computation.1 | async-start | bytes 1310720 | tf_op jit(solution)/shard_map/all_to_all | solution.py:793
  59.0 0.0 copy-start.6
  59.0 13.5 %quiet_step.2 = (f32[3,512,1024]{2,1,0:T(8,128)}, bf16[4,1,512,1024]{3,2,1,0:T(8,128)(2,1)}, bf16[4,144,1152]{2,1,0:T(8,128)(2,1)}, s32[1]{0:T(128)}) custom-call(f32[4]{0:T(128)} %add_convert_fusion.refs_0_, s32[1]{0:T(128)} %bitcast.4.refs_1_, bf16[4,1,512,1024]{3,2,1,0:T(8,128)(2,1)} %refs_4_.9, bf16[4,1,512,1024]{3,2,1,0:T(8,128)(2,1)} %refs_4_.9, ...), custom_call_target="tpu_custom_call" | custom-call | flops 8999999488 | bytes 37748736 | tf_op jit(solution)/shard_map/quiet_step/pallas_call | solution.py:722
  74.4 0.7 dynamic-slice_bitcast_fusion.refs_2_
  75.1 1.7 %all-to-all-done.1.refs_0_ = f32[32,40,128]{2,1,0:T(8,128)S(1)} async-done(((f32[32,40,128]{2,1,0:T(8,128)}), f32[32,40,128]{2,1,0:T(8,128)S(1)}, u32[]{:S(2)}, u32[]{:S(2)}) %all-to-all-start.1) | async-done | bytes 655392 | tf_op jit(solution)/shard_map/all_to_all | solution.py:793
  76.8 0.9 inverse_x.1
  77.7 0.7 copy-done.5
  78.4 0.1 collective-permute-start.7
  78.4 1.6 %collective-permute-start.8 = (f32[72,640]{1,0:T(8,128)S(1)}, f32[72,640]{1,0:T(8,128)S(1)}, u32[]{:S(2)}, u32[]{:S(2)}) collective-permute-start(f32[72,640]{1,0:T(8,128)S(1)} %get-tuple-element.57), channel_id=1, source_target_pairs={{0,16},{8,24},{16,0},{24,8},{1,17},{9,25},{17,1},{25,9},{2,18},{10... | collective-permute-start | bytes 552968 | tf_op jit(solution)/shard_map/ppermute | solution.py:741
  80.0 0.2 collective-permute-start.9
  80.2 6.7 %quiet_step.3 = (f32[3,512,1024]{2,1,0:T(8,128)}, bf16[4,1,512,1024]{3,2,1,0:T(8,128)(2,1)}, bf16[4,144,1152]{2,1,0:T(8,128)(2,1)}, s32[1]{0:T(128)}) custom-call(f32[4]{0:T(128)} %add_convert_fusion.refs_0_, s32[1]{0:T(128)} %bitcast.4.refs_1_, bf16[4,1,512,1024]{3,2,1,0:T(8,128)(2,1)} %refs_4_.9, ...), custom_call_target="tpu_custom_call", output_to_operand_aliasing={{0}: (14, {}), {1}: (15, {}), {2}: (16, {})} | custom-call | flops 3000000000 | bytes 12582912 | tf_op jit(solution)/shard_map/quiet_step/pallas_call | solution.py:722
  86.9 0.0 collective-permute-done.7.refs_8_
  86.9 0.0 collective-permute-done.8.refs_9_
  86.9 2.0 %collective-permute-done.9.refs_10_ = f32[72,640]{1,0:T(8,128)S(1)} collective-permute-done((f32[72,640]{1,0:T(8,128)S(1)}, f32[72,640]{1,0:T(8,128)S(1)}, u32[]{:S(2)}, u32[]{:S(2)}) %collective-permute-start.9) | collective-permute-done | bytes 184352 | tf_op jit(solution)/shard_map/ppermute | solution.py:741
  88.9 0.7 copy-done.13
  89.6 8.3 %source_step.1 = bf16[4,1,512,1024]{3,2,1,0:T(8,128)(2,1)} custom-call(f32[272,640]{1,0:T(8,128)} %get-tuple-element.38.refs_0_, bf16[4,144,1152]{2,1,0:T(8,128)(2,1)} %get-tuple-element.43.refs_1_, bf16[2,5,256,256]{3,2,1,0:T(8,128)(2,1)} %get-tuple-element.44.refs_2_, ...), custom_call_target="tpu_custom_call", output_to_operand_aliasing={{}: (6, {})} | custom-call | flops 4000000000 | bytes 16777216 | tf_op jit(solution)/shard_map/source_step/pallas_call | solution.py:722
  (23 shorter events, 0.0 us)
Async XLA Ops:
  0.0 1.2 %copy-start.1 = (f32[2,1,256,512]{3,2,1,0:T(8,128)S(1)}, f32[2,1,256,512]{3,2,1,0:T(8,128)}, u32[]{:S(2)}) copy-start(f32[2,1,256,512]{3,2,1,0:T(8,128)} %refs_2_.9) | copy-start | bytes 3145732
  1.3 3.2 %collective-permute-start = (f32[2,64,512]{2,1,0:T(8,128)S(1)}, f32[2,64,512]{2,1,0:T(8,128)S(1)}, u32[]{:S(2)}, u32[]{:S(2)}) collective-permute-start(f32[2,64,512]{2,1,0:T(8,128)S(1)} %get-tuple-element.33), channel_id=1, source_target_pairs={{0,8},{8,0},{16,24},{24,16},{1,9},{9,1},{17,25},{25,17},{2,10},{10... | collective-permute-start | bytes 786440 | tf_op jit(solution)/shard_map/ppermute | solution.py:741
  1.8 11.5 %collective-permute-start.5 = (f32[2,64,512]{2,1,0:T(8,128)S(1)}, f32[2,64,512]{2,1,0:T(8,128)S(1)}, u32[]{:S(2)}, u32[]{:S(2)}) collective-permute-start(f32[2,64,512]{2,1,0:T(8,128)S(1)} %get-tuple-element.49), channel_id=1, source_target_pairs={{0,16},{8,24},{16,0},{24,8},{1,17},{9,25},{17,1},{25,9},{2,18},{10... | collective-permute-start | bytes 786440 | tf_op jit(solution)/shard_map/ppermute | solution.py:741
  4.4 12.3 %collective-permute-start.6 = (f32[2,64,512]{2,1,0:T(8,128)S(1)}, f32[2,64,512]{2,1,0:T(8,128)S(1)}, u32[]{:S(2)}, u32[]{:S(2)}) collective-permute-start(f32[2,64,512]{2,1,0:T(8,128)S(1)} %get-tuple-element.50), channel_id=1, source_target_pairs={{0,24},{8,16},{16,8},{24,0},{1,25},{9,17},{17,9},{25,1},{2,26},{10... | collective-permute-start | bytes 786440 | tf_op jit(solution)/shard_map/ppermute | solution.py:741
  4.5 1.6 %copy-start = (s32[1,512,1024]{2,1,0:T(8,128)S(1)}, s32[1,512,1024]{2,1,0:T(8,128)}, u32[]{:S(2)}) copy-start(s32[1,512,1024]{2,1,0:T(8,128)} %refs_7_.3) | copy-start | bytes 6291460
  6.0 1.2 %copy-start.2 = (f32[2,1,256,512]{3,2,1,0:T(8,128)S(1)}, f32[2,1,256,512]{3,2,1,0:T(8,128)}, u32[]{:S(2)}) copy-start(f32[2,1,256,512]{3,2,1,0:T(8,128)} %refs_2_.9) | copy-start | bytes 3145732
  7.3 9.8 %copy-start.7 = (bf16[1536,512]{1,0:T(8,128)(2,1)S(1)}, bf16[1536,512]{1,0:T(8,128)(2,1)}, u32[]{:S(2)}) copy-start(bf16[1536,512]{1,0:T(8,128)(2,1)} %constant.41.clone.refs_4_) | copy-start | bytes 4718596
  7.3 9.8 %copy-start.10 = (f32[8,256]{1,0:T(8,128)S(1)}, f32[8,256]{1,0:T(8,128)}, u32[]{:S(2)}) copy-start(f32[8,256]{1,0:T(8,128)} %constant.42.clone.refs_5_) | copy-start | bytes 24580
  8.4 8.3 %collective-permute-start.1 = (f32[24,1024]{1,0:T(8,128)S(1)}, f32[24,1024]{1,0:T(8,128)S(1)}, u32[]{:S(2)}, u32[]{:S(2)}) collective-permute-start(f32[24,1024]{1,0:T(8,128)S(1)} %get-tuple-element.34), channel_id=1, source_target_pairs={{0,1},{1,2},{2,3},{3,4},{4,5},{5,6},{6,7},{7,0},{8,9},{9,10},{10,1... | collective-permute-start | bytes 294920 | tf_op jit(solution)/shard_map/ppermute | solution.py:737
  10.2 6.9 %collective-permute-start.2 = (f32[24,1024]{1,0:T(8,128)S(1)}, f32[24,1024]{1,0:T(8,128)S(1)}, u32[]{:S(2)}, u32[]{:S(2)}) collective-permute-start(f32[24,1024]{1,0:T(8,128)S(1)} %get-tuple-element.35), channel_id=1, source_target_pairs={{0,7},{1,0},{2,1},{3,2},{4,3},{5,4},{6,5},{7,6},{8,15},{9,8},{10,9... | collective-permute-start | bytes 294920 | tf_op jit(solution)/shard_map/ppermute | solution.py:737
  16.7 2.5 %copy-start.3 = (f32[24,1024]{1,0:T(8,128)}, f32[24,1024]{1,0:T(8,128)S(1)}, u32[]{:S(2)}) copy-start(f32[24,1024]{1,0:T(8,128)S(1)} %collective-permute-done.1.refs_7_.refs_3_.refs_8_.refs_6_) | copy-start | bytes 294916
  17.1 2.1 %copy-start.4 = (f32[24,1024]{1,0:T(8,128)}, f32[24,1024]{1,0:T(8,128)S(1)}, u32[]{:S(2)}) copy-start(f32[24,1024]{1,0:T(8,128)S(1)} %collective-permute-done.2.refs_8_.refs_4_.refs_9_.refs_7_) | copy-start | bytes 294916
  19.2 31.8 %all-to-all-start = ((f32[32,64,128]{2,1,0:T(8,128)}), f32[32,64,128]{2,1,0:T(8,128)S(1)}, u32[]{:S(2)}, u32[]{:S(2)}) async-start(f32[32,64,128]{2,1,0:T(8,128)} %get-tuple-element.51), calls=%async_computation | async-start | bytes 2097152 | tf_op jit(solution)/shard_map/all_to_all | solution.py:771
  25.3 25.6 %copy-start.8 = (bf16[1024,256]{1,0:T(8,128)(2,1)S(1)}, bf16[1024,256]{1,0:T(8,128)(2,1)}, u32[]{:S(2)}) copy-start(bf16[1024,256]{1,0:T(8,128)(2,1)} %constant.44.clone.refs_3_) | copy-start | bytes 1572868
  25.3 25.6 %copy-start.9 = (bf16[256,48]{1,0:T(8,128)(2,1)S(1)}, bf16[256,48]{1,0:T(8,128)(2,1)}, u32[]{:S(2)}) copy-start(bf16[256,48]{1,0:T(8,128)(2,1)} %constant.45.clone.refs_4_) | copy-start | bytes 73732
  28.3 9.6 %collective-permute-start.3 = (f32[48,640]{1,0:T(8,128)}, f32[48,640]{1,0:T(8,128)S(1)}, u32[]{:S(2)}, u32[]{:S(2)}) collective-permute-start(f32[48,640]{1,0:T(8,128)} %get-tuple-element.36), channel_id=1, source_target_pairs={{0,8},{8,16},{16,24},{24,0},{1,9},{9,17},{17,25},{25,1},{2,10},{10... | collective-permute-start | bytes 368648 | tf_op jit(solution)/shard_map/ppermute | solution.py:737
  28.5 9.4 %collective-permute-start.4 = (f32[48,640]{1,0:T(8,128)}, f32[48,640]{1,0:T(8,128)S(1)}, u32[]{:S(2)}, u32[]{:S(2)}) collective-permute-start(f32[48,640]{1,0:T(8,128)} %get-tuple-element.37), channel_id=1, source_target_pairs={{0,24},{8,0},{16,8},{24,16},{1,25},{9,1},{17,9},{25,17},{2,26},{10... | collective-permute-start | bytes 368648 | tf_op jit(solution)/shard_map/ppermute | solution.py:737
  37.9 0.6 copy-start.14
  37.9 0.7 copy-start.15
  55.2 21.5 %all-to-all-start.1 = ((f32[32,40,128]{2,1,0:T(8,128)}), f32[32,40,128]{2,1,0:T(8,128)S(1)}, u32[]{:S(2)}, u32[]{:S(2)}) async-start(f32[32,40,128]{2,1,0:T(8,128)} %solve_y.1), calls=%async_computation.1 | async-start | bytes 1310720 | tf_op jit(solution)/shard_map/all_to_all | solution.py:793
  59.0 17.7 %copy-start.6 = (bf16[1536,512]{1,0:T(8,128)(2,1)S(1)}, bf16[1536,512]{1,0:T(8,128)(2,1)}, u32[]{:S(2)}) copy-start(bf16[1536,512]{1,0:T(8,128)(2,1)} %constant.47.clone.refs_1_) | copy-start | bytes 4718596
  77.7 0.7 copy-start.5
  78.4 8.5 %collective-permute-start.7 = (f32[72,640]{1,0:T(8,128)S(1)}, f32[72,640]{1,0:T(8,128)S(1)}, u32[]{:S(2)}, u32[]{:S(2)}) collective-permute-start(f32[72,640]{1,0:T(8,128)S(1)} %get-tuple-element.56), channel_id=1, source_target_pairs={{0,8},{8,0},{16,24},{24,16},{1,9},{9,1},{17,25},{25,17},{2,10},{10... | collective-permute-start | bytes 552968 | tf_op jit(solution)/shard_map/ppermute | solution.py:741
  78.4 8.5 %collective-permute-start.8 = (f32[72,640]{1,0:T(8,128)S(1)}, f32[72,640]{1,0:T(8,128)S(1)}, u32[]{:S(2)}, u32[]{:S(2)}) collective-permute-start(f32[72,640]{1,0:T(8,128)S(1)} %get-tuple-element.57), channel_id=1, source_target_pairs={{0,16},{8,24},{16,0},{24,8},{1,17},{9,25},{17,1},{25,9},{2,18},{10... | collective-permute-start | bytes 552968 | tf_op jit(solution)/shard_map/ppermute | solution.py:741
  80.0 8.9 %collective-permute-start.9 = (f32[72,640]{1,0:T(8,128)S(1)}, f32[72,640]{1,0:T(8,128)S(1)}, u32[]{:S(2)}, u32[]{:S(2)}) collective-permute-start(f32[72,640]{1,0:T(8,128)S(1)} %get-tuple-element.58), channel_id=1, source_target_pairs={{0,24},{8,16},{16,8},{24,0},{1,25},{9,17},{17,9},{25,1},{2,26},{10... | collective-permute-start | bytes 552968 | tf_op jit(solution)/shard_map/ppermute | solution.py:741
  86.9 2.0 %copy-start.11 = (f32[72,640]{1,0:T(8,128)}, f32[72,640]{1,0:T(8,128)S(1)}, u32[]{:S(2)}) copy-start(f32[72,640]{1,0:T(8,128)S(1)} %collective-permute-done.7.refs_8_) | copy-start | bytes 552964
  86.9 2.0 %copy-start.12 = (f32[72,640]{1,0:T(8,128)}, f32[72,640]{1,0:T(8,128)S(1)}, u32[]{:S(2)}) copy-start(f32[72,640]{1,0:T(8,128)S(1)} %collective-permute-done.8.refs_9_) | copy-start | bytes 552964
  88.9 0.7 copy-start.13

commit v6 on v5

--- a/solution.py
+++ b/solution.py
@@ -649,7 +649,7 @@
         )
         for mask, piece in enumerate(lines)
     ]
-    for copy in (*pieces, *copies, *tile_copies(0), *tile_copies(1)):
+    for copy in (*pieces, *copies, *tile_copies(0)):
         copy.start()
     for copy in pieces + copies[:1]:
         copy.wait()
@@ -667,6 +667,8 @@
         value = split(exact_dot(around[k], [matrix[part, k, :, :lanes] for part in range(2)]))
         for part in range(2):
             raised[part, :, 2 * k * LANES : 2 * k * LANES + lanes] = value[part]
+    for copy in tile_copies(1):
+        copy.start()
     for copy in copies[2:]:
         copy.wait()
 
@@ -850,7 +852,7 @@
         },
         after=moved[1:2],
         moved=2 << 20,
-        megabytes=50,
+        megabytes=52,
         name="rows",
     )
     above, below = ring(last, "gy", 1), ring(first, "gy", -1)

time: 98.7 us -> 98.8 us (level)
  local copies, waits for them, and re-layouts: 7.5 us -> 5.95 us
  waiting for transfers between devices: 18.9 us -> 20 us
    ppermute x6, waiting for transfers between devices: 5.3 us -> 6.89 us  [swap(): lax.ppermute(array, axis, [(i, i ^ mask) for i in range(lax.axis_size(axi...]
    unnamed x32 -> x30, local copies, waits for them, and re-layouts: 6.09 us -> 4.54 us
  transfers between devices with their start and end apart: 12 -> 12, of which waited for: 6 -> 5; matrix products, arithmetic and copies ran while one was open for 3% -> 3% of each run, Pallas kernels for 32% -> 32%
where the time goes in v6:
time: 98.8 us; the launch traced here: 98.1 us
  Pallas kernels  46.7 us (47%)
  starting transfers between devices  21.4 us (22%)
  waiting for transfers between devices  20 us (20%)
  local copies, waits for them, and re-layouts  5.95 us (6%)
  between operations  2.69 us (3%)
  other arithmetic  1.31 us (1%)
    pallas_call x11, Pallas kernels, call(): pl.pallas_call(body, out_shape=outs, in_specs=in_specs + [pl.BlockSpec(me...  46.7 us
    all_to_all x1, waiting for transfers between devices, pressure_lines(): spectra = lax.all_to_all(spectra, ('gy', 'gx'), 0, 0, tiled=True)  7.15 us
    ppermute x6, waiting for transfers between devices, swap(): lax.ppermute(array, axis, [(i, i ^ mask) for i in range(lax.axis_size(axi...  6.89 us
    ppermute x4, starting transfers between devices, ring(): lax.ppermute(array, axis, [(i, (i + step) % size) for i in range(size)])  6.66 us
    all_to_all x1, starting transfers between devices, pressure_lines(): spectra = lax.all_to_all(spectra, ('gy', 'gx'), 0, 0, tiled=True)  5.93 us
    ppermute x6, starting transfers between devices, swap(): lax.ppermute(array, axis, [(i, i ^ mask) for i in range(lax.axis_size(axi...  5.03 us
    unnamed x30, local copies, waits for them, and re-layouts  4.54 us
    ppermute x4, waiting for transfers between devices, ring(): lax.ppermute(array, axis, [(i, (i + step) % size) for i in range(size)])  4.16 us
  transfers between devices with their start and end apart: 12, of which 5 were waited for; matrix products, arithmetic and copies ran while one was open for 3% of the time, Pallas kernels for 32%

profile of v6, /device:TPU:0, one launch (start us, length us, event | category | flops | bytes accessed | tf_op | source)
XLA Modules:
  0.0 98.1 jit_solution(4635014488902611045)
XLA Ops:
  0.0 1.2 %copy-done = f32[2,1,256,512]{3,2,1,0:T(8,128)S(1)} copy-done((f32[2,1,256,512]{3,2,1,0:T(8,128)S(1)}, f32[2,1,256,512]{3,2,1,0:T(8,128)}, u32[]{:S(2)}) %copy-start) | copy-done | bytes 1048600
  1.2 0.1 pieces.1
  1.3 0.5 collective-permute-start
  1.8 2.6 %collective-permute-start.5 = (f32[2,64,512]{2,1,0:T(8,128)S(1)}, f32[2,64,512]{2,1,0:T(8,128)S(1)}, u32[]{:S(2)}, u32[]{:S(2)}) collective-permute-start(f32[2,64,512]{2,1,0:T(8,128)S(1)} %get-tuple-element.49), channel_id=1, source_target_pairs={{0,16},{8,24},{16,0},{24,8},{1,17},{9,25},{17,1},{25,9},{2,18},{10... | collective-permute-start | bytes 786440 | tf_op jit(solution)/shard_map/ppermute | solution.py:743
  4.4 0.1 collective-permute-start.6
  4.5 0.0 collective-permute-done.refs_6_.refs_1_
  4.5 1.2 %copy-done.1 = f32[2,1,256,512]{3,2,1,0:T(8,128)S(1)} copy-done((f32[2,1,256,512]{3,2,1,0:T(8,128)S(1)}, f32[2,1,256,512]{3,2,1,0:T(8,128)}, u32[]{:S(2)}) %copy-start.1) | copy-done | bytes 1048600
  5.7 1.1 %rows.1 = (f32[24,1024]{1,0:T(8,128)S(1)}, f32[24,1024]{1,0:T(8,128)S(1)}) custom-call(bf16[4,1,512,1024]{3,2,1,0:T(8,128)(2,1)} %refs_4_.9, bf16[4,1,512,1024]{3,2,1,0:T(8,128)(2,1)} %refs_4_.9, s32[1,512,1024]{2,1,0:T(8,128)} %refs_7_.3, s32[1,512,1024]{2,1,0:T(8,128)} %refs_7_.3, f32[2,1,256,512]{3,2,1,0:T(8,128)S(1)} %copy-done.1, ...), custom_call_target="tpu_custom_call" | custom-call | bytes 2097152 | tf_op jit(solution)/shard_map/rows/pallas_call | solution.py:724
  6.8 1.8 %collective-permute-start.1 = (f32[24,1024]{1,0:T(8,128)S(1)}, f32[24,1024]{1,0:T(8,128)S(1)}, u32[]{:S(2)}, u32[]{:S(2)}) collective-permute-start(f32[24,1024]{1,0:T(8,128)S(1)} %get-tuple-element.34), channel_id=1, source_target_pairs={{0,1},{1,2},{2,3},{3,4},{4,5},{5,6},{6,7},{7,0},{8,9},{9,10},{10,1... | collective-permute-start | bytes 294920 | tf_op jit(solution)/shard_map/ppermute | solution.py:739
  8.6 3.1 %collective-permute-start.2 = (f32[24,1024]{1,0:T(8,128)S(1)}, f32[24,1024]{1,0:T(8,128)S(1)}, u32[]{:S(2)}, u32[]{:S(2)}) collective-permute-start(f32[24,1024]{1,0:T(8,128)S(1)} %get-tuple-element.35), channel_id=1, source_target_pairs={{0,7},{1,0},{2,1},{3,2},{4,3},{5,4},{6,5},{7,6},{8,15},{9,8},{10,9... | collective-permute-start | bytes 294920 | tf_op jit(solution)/shard_map/ppermute | solution.py:739
  11.7 0.0 collective-permute-done.5.refs_2_
  11.7 4.9 %collective-permute-done.6.refs_3_ = f32[2,64,512]{2,1,0:T(8,128)S(1)} collective-permute-done((f32[2,64,512]{2,1,0:T(8,128)S(1)}, f32[2,64,512]{2,1,0:T(8,128)S(1)}, u32[]{:S(2)}, u32[]{:S(2)}) %collective-permute-start.6) | collective-permute-done | bytes 262176 | tf_op jit(solution)/shard_map/ppermute | solution.py:743
  16.6 0.0 collective-permute-done.1.refs_7_.refs_3_.refs_8_.refs_6_
  16.6 0.0 collective-permute-done.2.refs_8_.refs_4_.refs_9_.refs_7_
  16.6 0.0 copy-start.3
  16.7 2.0 %forward_x.1 = (f32[32,64,128]{2,1,0:T(8,128)}, f32[8,128]{1,0:T(8,128)S(1)}) custom-call(f32[2,64,512]{2,1,0:T(8,128)S(1)} %get-tuple-element.48.refs_0_, f32[2,64,512]{2,1,0:T(8,128)S(1)} %collective-permute-done.refs_6_.refs_1_, f32[2,64,512]{2,1,0:T(8,128)S(1)} %collective-permute-done.5.refs_2_, f32[2,64,512]{2,1,0:T(8,128)S(1)} %collective-permute-done.6.refs_3_, ...), custom_call_target="tpu_custom_call" | custom-call | flops 1000000000 | bytes 4194304 | tf_op jit(solution)/shard_map/forward_x/pallas_call | solution.py:724
  18.8 5.9 %all-to-all-start = ((f32[32,64,128]{2,1,0:T(8,128)}), f32[32,64,128]{2,1,0:T(8,128)S(1)}, u32[]{:S(2)}, u32[]{:S(2)}) async-start(f32[32,64,128]{2,1,0:T(8,128)} %get-tuple-element.51), calls=%async_computation | async-start | bytes 2097152 | tf_op jit(solution)/shard_map/all_to_all | solution.py:773
  24.7 0.7 add_convert_fusion.refs_0_
  25.4 3.0 %columns.1 = (f32[48,640]{1,0:T(8,128)}, f32[48,640]{1,0:T(8,128)}) custom-call(f32[4]{0:T(128)} %add_convert_fusion.refs_0_, bf16[4,1,512,1024]{3,2,1,0:T(8,128)(2,1)} %refs_4_.9, bf16[4,1,512,1024]{3,2,1,0:T(8,128)(2,1)} %refs_4_.9, s32[1,512,1024]{2,1,0:T(8,128)} %refs_7_.3, s32[1,512,1024]{2,1,0:T(8,128)} %refs_7_.3, f32[2,1,256,512]{3,2,1,0:T(8,128)} %refs_2_.9, ...), custom_call_target="tpu_custom_call" | custom-call | bytes 8388608 | tf_op jit(solution)/shard_map/columns/pallas_call | solution.py:724
  28.4 0.3 collective-permute-start.3
  28.6 1.5 %collective-permute-start.4 = (f32[48,640]{1,0:T(8,128)}, f32[48,640]{1,0:T(8,128)S(1)}, u32[]{:S(2)}, u32[]{:S(2)}) collective-permute-start(f32[48,640]{1,0:T(8,128)} %get-tuple-element.37), channel_id=1, source_target_pairs={{0,24},{8,0},{16,8},{24,16},{1,25},{9,1},{17,9},{25,17},{2,26},{10... | collective-permute-start | bytes 368648 | tf_op jit(solution)/shard_map/ppermute | solution.py:739
  30.1 0.7 pad_add_fusion.refs_0_
  30.8 3.0 %tables.1 = (bf16[2,5,256,256]{3,2,1,0:T(8,128)(2,1)}, bf16[4,144,240]{2,1,0:T(8,128)(2,1)}, s32[1]{0:T(128)}) custom-call(s32[2]{0:T(128)} %pad_add_fusion.refs_0_, f32[4,4096]{1,0:T(4,128)} %refs_1_.4, f32[4,4096]{1,0:T(4,128)} %refs_2_.6), custom_call_target="tpu_custom_call" | custom-call | bytes 4194304 | tf_op jit(solution)/shard_map/tables/pallas_call | solution.py:724
  33.8 4.2 %collective-permute-done.3.refs_5_ = f32[48,640]{1,0:T(8,128)S(1)} collective-permute-done((f32[48,640]{1,0:T(8,128)}, f32[48,640]{1,0:T(8,128)S(1)}, u32[]{:S(2)}, u32[]{:S(2)}) %collective-permute-start.3) | collective-permute-done | bytes 122912 | tf_op jit(solution)/shard_map/ppermute | solution.py:739
  37.9 0.0 collective-permute-done.4.refs_6_
  37.9 0.6 copy-done.13
  38.6 0.1 copy-done.14
  38.6 3.8 %sides.1 = (f32[5,640,128]{2,1,0:T(8,128)}, f32[272,640]{1,0:T(8,128)}, s32[1]{0:T(128)}) custom-call(f32[4]{0:T(128)} %add_convert_fusion.refs_0_, s32[1]{0:T(128)} %get-tuple-element.32.refs_1_, f32[2,1,256,512]{3,2,1,0:T(8,128)} %refs_2_.9, f32[24,1024]{1,0:T(8,128)} %copy-done.2, f32[24,1024]{1,0:T(8,128)} %copy-done.3, f32[48,640]{1,0:T(8,128)} %copy-done.13, ...), custom_call_target="tpu_custom_call" | custom-call | bytes 8388608 | tf_op jit(solution)/shard_map/sides/pallas_call | solution.py:724
  43.1 0.7 constant_dynamic-slice_fusion.refs_2_
  43.8 7.2 %all-to-all-done.refs_0_ = f32[32,64,128]{2,1,0:T(8,128)S(1)} async-done(((f32[32,64,128]{2,1,0:T(8,128)}), f32[32,64,128]{2,1,0:T(8,128)S(1)}, u32[]{:S(2)}, u32[]{:S(2)}) %all-to-all-start) | async-done | bytes 1048608 | tf_op jit(solution)/shard_map/all_to_all | solution.py:773
  50.9 4.2 %solve_y.1 = f32[32,40,128]{2,1,0:T(8,128)} custom-call(f32[32,64,128]{2,1,0:T(8,128)S(1)} %all-to-all-done.refs_0_, f32[8,128]{1,0:T(8,128)S(1)} %get-tuple-element.52.refs_1_, f32[1,128]{1,0:T(1,128)S(1)} %constant_dynamic-slice_fusion.refs_2_, bf16[1024,256]{1,0:T(8,128)(2,1)S(1)} %copy-done.7, bf16[256,48]{1,0:T(8,128)(2,1)S(1)} %copy-done.8), custom_call_target="tpu_custom_call" | custom-call | flops 4000000000 | bytes 6291456 | tf_op jit(solution)/shard_map/solve_y/pallas_call | solution.py:724
  55.2 3.8 %all-to-all-start.1 = ((f32[32,40,128]{2,1,0:T(8,128)}), f32[32,40,128]{2,1,0:T(8,128)S(1)}, u32[]{:S(2)}, u32[]{:S(2)}) async-start(f32[32,40,128]{2,1,0:T(8,128)} %solve_y.1), calls=%async_computation.1 | async-start | bytes 1310720 | tf_op jit(solution)/shard_map/all_to_all | solution.py:795
  59.0 0.0 copy-start.5
  59.0 13.5 %quiet_step.2 = (f32[3,512,1024]{2,1,0:T(8,128)}, bf16[4,1,512,1024]{3,2,1,0:T(8,128)(2,1)}, bf16[4,144,1152]{2,1,0:T(8,128)(2,1)}, s32[1]{0:T(128)}) custom-call(f32[4]{0:T(128)} %add_convert_fusion.refs_0_, s32[1]{0:T(128)} %bitcast.4.refs_1_, bf16[4,1,512,1024]{3,2,1,0:T(8,128)(2,1)} %refs_4_.9, bf16[4,1,512,1024]{3,2,1,0:T(8,128)(2,1)} %refs_4_.9, ...), custom_call_target="tpu_custom_call" | custom-call | flops 8999999488 | bytes 37748736 | tf_op jit(solution)/shard_map/quiet_step/pallas_call | solution.py:724
  74.2 0.7 dynamic-slice_bitcast_fusion.refs_2_
  74.9 1.8 %all-to-all-done.1.refs_0_ = f32[32,40,128]{2,1,0:T(8,128)S(1)} async-done(((f32[32,40,128]{2,1,0:T(8,128)}), f32[32,40,128]{2,1,0:T(8,128)S(1)}, u32[]{:S(2)}, u32[]{:S(2)}) %all-to-all-start.1) | async-done | bytes 655392 | tf_op jit(solution)/shard_map/all_to_all | solution.py:795
  76.7 0.9 inverse_x.1
  77.7 0.0 copy-start.4
  77.7 0.7 copy-done.4
  78.3 0.1 collective-permute-start.7
  78.4 1.6 %collective-permute-start.8 = (f32[72,640]{1,0:T(8,128)S(1)}, f32[72,640]{1,0:T(8,128)S(1)}, u32[]{:S(2)}, u32[]{:S(2)}) collective-permute-start(f32[72,640]{1,0:T(8,128)S(1)} %get-tuple-element.57), channel_id=1, source_target_pairs={{0,16},{8,24},{16,0},{24,8},{1,17},{9,25},{17,1},{25,9},{2,18},{10... | collective-permute-start | bytes 552968 | tf_op jit(solution)/shard_map/ppermute | solution.py:743
  80.0 0.2 collective-permute-start.9
  80.2 6.7 %quiet_step.3 = (f32[3,512,1024]{2,1,0:T(8,128)}, bf16[4,1,512,1024]{3,2,1,0:T(8,128)(2,1)}, bf16[4,144,1152]{2,1,0:T(8,128)(2,1)}, s32[1]{0:T(128)}) custom-call(f32[4]{0:T(128)} %add_convert_fusion.refs_0_, s32[1]{0:T(128)} %bitcast.4.refs_1_, bf16[4,1,512,1024]{3,2,1,0:T(8,128)(2,1)} %refs_4_.9, ...), custom_call_target="tpu_custom_call", output_to_operand_aliasing={{0}: (14, {}), {1}: (15, {}), {2}: (16, {})} | custom-call | flops 3000000000 | bytes 12582912 | tf_op jit(solution)/shard_map/quiet_step/pallas_call | solution.py:724
  86.9 0.0 collective-permute-done.7.refs_8_
  86.9 0.0 collective-permute-done.8.refs_9_
  86.9 2.0 %collective-permute-done.9.refs_10_ = f32[72,640]{1,0:T(8,128)S(1)} collective-permute-done((f32[72,640]{1,0:T(8,128)S(1)}, f32[72,640]{1,0:T(8,128)S(1)}, u32[]{:S(2)}, u32[]{:S(2)}) %collective-permute-start.9) | collective-permute-done | bytes 184352 | tf_op jit(solution)/shard_map/ppermute | solution.py:743
  88.9 0.7 copy-done.12
  89.6 8.3 %source_step.1 = bf16[4,1,512,1024]{3,2,1,0:T(8,128)(2,1)} custom-call(f32[272,640]{1,0:T(8,128)} %get-tuple-element.38.refs_0_, bf16[4,144,1152]{2,1,0:T(8,128)(2,1)} %get-tuple-element.43.refs_1_, bf16[2,5,256,256]{3,2,1,0:T(8,128)(2,1)} %get-tuple-element.44.refs_2_, ...), custom_call_target="tpu_custom_call", output_to_operand_aliasing={{}: (6, {})} | custom-call | flops 4000000000 | bytes 16777216 | tf_op jit(solution)/shard_map/source_step/pallas_call | solution.py:724
  (21 shorter events, 0.0 us)
Async XLA Ops:
  0.0 1.2 %copy-start = (f32[2,1,256,512]{3,2,1,0:T(8,128)S(1)}, f32[2,1,256,512]{3,2,1,0:T(8,128)}, u32[]{:S(2)}) copy-start(f32[2,1,256,512]{3,2,1,0:T(8,128)} %refs_2_.9) | copy-start | bytes 3145732
  1.3 3.2 %collective-permute-start = (f32[2,64,512]{2,1,0:T(8,128)S(1)}, f32[2,64,512]{2,1,0:T(8,128)S(1)}, u32[]{:S(2)}, u32[]{:S(2)}) collective-permute-start(f32[2,64,512]{2,1,0:T(8,128)S(1)} %get-tuple-element.33), channel_id=1, source_target_pairs={{0,8},{8,0},{16,24},{24,16},{1,9},{9,1},{17,25},{25,17},{2,10},{10... | collective-permute-start | bytes 786440 | tf_op jit(solution)/shard_map/ppermute | solution.py:743
  1.8 9.9 %collective-permute-start.5 = (f32[2,64,512]{2,1,0:T(8,128)S(1)}, f32[2,64,512]{2,1,0:T(8,128)S(1)}, u32[]{:S(2)}, u32[]{:S(2)}) collective-permute-start(f32[2,64,512]{2,1,0:T(8,128)S(1)} %get-tuple-element.49), channel_id=1, source_target_pairs={{0,16},{8,24},{16,0},{24,8},{1,17},{9,25},{17,1},{25,9},{2,18},{10... | collective-permute-start | bytes 786440 | tf_op jit(solution)/shard_map/ppermute | solution.py:743
  4.4 12.3 %collective-permute-start.6 = (f32[2,64,512]{2,1,0:T(8,128)S(1)}, f32[2,64,512]{2,1,0:T(8,128)S(1)}, u32[]{:S(2)}, u32[]{:S(2)}) collective-permute-start(f32[2,64,512]{2,1,0:T(8,128)S(1)} %get-tuple-element.50), channel_id=1, source_target_pairs={{0,24},{8,16},{16,8},{24,0},{1,25},{9,17},{17,9},{25,1},{2,26},{10... | collective-permute-start | bytes 786440 | tf_op jit(solution)/shard_map/ppermute | solution.py:743
  4.5 1.2 %copy-start.1 = (f32[2,1,256,512]{3,2,1,0:T(8,128)S(1)}, f32[2,1,256,512]{3,2,1,0:T(8,128)}, u32[]{:S(2)}) copy-start(f32[2,1,256,512]{3,2,1,0:T(8,128)} %refs_2_.9) | copy-start | bytes 3145732
  5.7 11.0 %copy-start.6 = (bf16[1536,512]{1,0:T(8,128)(2,1)S(1)}, bf16[1536,512]{1,0:T(8,128)(2,1)}, u32[]{:S(2)}) copy-start(bf16[1536,512]{1,0:T(8,128)(2,1)} %constant.41.clone.refs_4_) | copy-start | bytes 4718596
  5.7 11.0 %copy-start.9 = (f32[8,256]{1,0:T(8,128)S(1)}, f32[8,256]{1,0:T(8,128)}, u32[]{:S(2)}) copy-start(f32[8,256]{1,0:T(8,128)} %constant.42.clone.refs_5_) | copy-start | bytes 24580
  6.8 9.8 %collective-permute-start.1 = (f32[24,1024]{1,0:T(8,128)S(1)}, f32[24,1024]{1,0:T(8,128)S(1)}, u32[]{:S(2)}, u32[]{:S(2)}) collective-permute-start(f32[24,1024]{1,0:T(8,128)S(1)} %get-tuple-element.34), channel_id=1, source_target_pairs={{0,1},{1,2},{2,3},{3,4},{4,5},{5,6},{6,7},{7,0},{8,9},{9,10},{10,1... | collective-permute-start | bytes 294920 | tf_op jit(solution)/shard_map/ppermute | solution.py:739
  8.6 8.0 %collective-permute-start.2 = (f32[24,1024]{1,0:T(8,128)S(1)}, f32[24,1024]{1,0:T(8,128)S(1)}, u32[]{:S(2)}, u32[]{:S(2)}) collective-permute-start(f32[24,1024]{1,0:T(8,128)S(1)} %get-tuple-element.35), channel_id=1, source_target_pairs={{0,7},{1,0},{2,1},{3,2},{4,3},{5,4},{6,5},{7,6},{8,15},{9,8},{10,9... | collective-permute-start | bytes 294920 | tf_op jit(solution)/shard_map/ppermute | solution.py:739
  16.6 2.1 %copy-start.2 = (f32[24,1024]{1,0:T(8,128)}, f32[24,1024]{1,0:T(8,128)S(1)}, u32[]{:S(2)}) copy-start(f32[24,1024]{1,0:T(8,128)S(1)} %collective-permute-done.1.refs_7_.refs_3_.refs_8_.refs_6_) | copy-start | bytes 294916
  16.6 2.1 %copy-start.3 = (f32[24,1024]{1,0:T(8,128)}, f32[24,1024]{1,0:T(8,128)S(1)}, u32[]{:S(2)}) copy-start(f32[24,1024]{1,0:T(8,128)S(1)} %collective-permute-done.2.refs_8_.refs_4_.refs_9_.refs_7_) | copy-start | bytes 294916
  18.8 32.2 %all-to-all-start = ((f32[32,64,128]{2,1,0:T(8,128)}), f32[32,64,128]{2,1,0:T(8,128)S(1)}, u32[]{:S(2)}, u32[]{:S(2)}) async-start(f32[32,64,128]{2,1,0:T(8,128)} %get-tuple-element.51), calls=%async_computation | async-start | bytes 2097152 | tf_op jit(solution)/shard_map/all_to_all | solution.py:773
  25.4 25.6 %copy-start.7 = (bf16[1024,256]{1,0:T(8,128)(2,1)S(1)}, bf16[1024,256]{1,0:T(8,128)(2,1)}, u32[]{:S(2)}) copy-start(bf16[1024,256]{1,0:T(8,128)(2,1)} %constant.44.clone.refs_3_) | copy-start | bytes 1572868
  25.4 25.6 %copy-start.8 = (bf16[256,48]{1,0:T(8,128)(2,1)S(1)}, bf16[256,48]{1,0:T(8,128)(2,1)}, u32[]{:S(2)}) copy-start(bf16[256,48]{1,0:T(8,128)(2,1)} %constant.45.clone.refs_4_) | copy-start | bytes 73732
  28.4 9.6 %collective-permute-start.3 = (f32[48,640]{1,0:T(8,128)}, f32[48,640]{1,0:T(8,128)S(1)}, u32[]{:S(2)}, u32[]{:S(2)}) collective-permute-start(f32[48,640]{1,0:T(8,128)} %get-tuple-element.36), channel_id=1, source_target_pairs={{0,8},{8,16},{16,24},{24,0},{1,9},{9,17},{17,25},{25,1},{2,10},{10... | collective-permute-start | bytes 368648 | tf_op jit(solution)/shard_map/ppermute | solution.py:739
  28.6 9.3 %collective-permute-start.4 = (f32[48,640]{1,0:T(8,128)}, f32[48,640]{1,0:T(8,128)S(1)}, u32[]{:S(2)}, u32[]{:S(2)}) collective-permute-start(f32[48,640]{1,0:T(8,128)} %get-tuple-element.37), channel_id=1, source_target_pairs={{0,24},{8,0},{16,8},{24,16},{1,25},{9,1},{17,9},{25,17},{2,26},{10... | collective-permute-start | bytes 368648 | tf_op jit(solution)/shard_map/ppermute | solution.py:739
  37.9 0.6 copy-start.13
  37.9 0.7 copy-start.14
  55.2 21.5 %all-to-all-start.1 = ((f32[32,40,128]{2,1,0:T(8,128)}), f32[32,40,128]{2,1,0:T(8,128)S(1)}, u32[]{:S(2)}, u32[]{:S(2)}) async-start(f32[32,40,128]{2,1,0:T(8,128)} %solve_y.1), calls=%async_computation.1 | async-start | bytes 1310720 | tf_op jit(solution)/shard_map/all_to_all | solution.py:795
  59.0 17.7 %copy-start.5 = (bf16[1536,512]{1,0:T(8,128)(2,1)S(1)}, bf16[1536,512]{1,0:T(8,128)(2,1)}, u32[]{:S(2)}) copy-start(bf16[1536,512]{1,0:T(8,128)(2,1)} %constant.47.clone.refs_1_) | copy-start | bytes 4718596
  77.7 0.7 copy-start.4
  78.3 8.5 %collective-permute-start.7 = (f32[72,640]{1,0:T(8,128)S(1)}, f32[72,640]{1,0:T(8,128)S(1)}, u32[]{:S(2)}, u32[]{:S(2)}) collective-permute-start(f32[72,640]{1,0:T(8,128)S(1)} %get-tuple-element.56), channel_id=1, source_target_pairs={{0,8},{8,0},{16,24},{24,16},{1,9},{9,1},{17,25},{25,17},{2,10},{10... | collective-permute-start | bytes 552968 | tf_op jit(solution)/shard_map/ppermute | solution.py:743
  78.4 8.5 %collective-permute-start.8 = (f32[72,640]{1,0:T(8,128)S(1)}, f32[72,640]{1,0:T(8,128)S(1)}, u32[]{:S(2)}, u32[]{:S(2)}) collective-permute-start(f32[72,640]{1,0:T(8,128)S(1)} %get-tuple-element.57), channel_id=1, source_target_pairs={{0,16},{8,24},{16,0},{24,8},{1,17},{9,25},{17,1},{25,9},{2,18},{10... | collective-permute-start | bytes 552968 | tf_op jit(solution)/shard_map/ppermute | solution.py:743
  80.0 8.9 %collective-permute-start.9 = (f32[72,640]{1,0:T(8,128)S(1)}, f32[72,640]{1,0:T(8,128)S(1)}, u32[]{:S(2)}, u32[]{:S(2)}) collective-permute-start(f32[72,640]{1,0:T(8,128)S(1)} %get-tuple-element.58), channel_id=1, source_target_pairs={{0,24},{8,16},{16,8},{24,0},{1,25},{9,17},{17,9},{25,1},{2,26},{10... | collective-permute-start | bytes 552968 | tf_op jit(solution)/shard_map/ppermute | solution.py:743
  86.9 2.0 %copy-start.10 = (f32[72,640]{1,0:T(8,128)}, f32[72,640]{1,0:T(8,128)S(1)}, u32[]{:S(2)}) copy-start(f32[72,640]{1,0:T(8,128)S(1)} %collective-permute-done.7.refs_8_) | copy-start | bytes 552964
  86.9 2.0 %copy-start.11 = (f32[72,640]{1,0:T(8,128)}, f32[72,640]{1,0:T(8,128)S(1)}, u32[]{:S(2)}) copy-start(f32[72,640]{1,0:T(8,128)S(1)} %collective-permute-done.8.refs_9_) | copy-start | bytes 552964
  88.9 0.7 copy-start.12

commit v7 on v5

--- a/solution.py
+++ b/solution.py
@@ -889,7 +889,7 @@
         megabytes=54,
         name="tables",
     )
-    sides, squares, beside = call(
+    sides, squares, _ = call(
         sides_kernel,
         (has, listed, velocity, above, below, from_left, from_right),
         (
@@ -962,12 +962,11 @@
             name="quiet_step",
         )
 
-    early = max(steps * 3 // 4, 1)
-    *begun, stepped = quiet_tiles(0, early, ())
-    if early < steps:
-        *begun, _ = quiet_tiles(early, steps - early, begun)
+    early = max(steps // 4, 1)
+    *begun, spread = quiet_tiles(0, early, ())
+    *begun, stepped = quiet_tiles(early, steps - early, begun)
     quiet, final, opened = begun
-    lines = pressure_lines(moved, (above, below), beside, stepped)
+    lines = pressure_lines(moved, (above, below), spread, stepped)
     operands = (squares, opened, rise_x, rise_y, quiet, across, final, *lines)
     anywhere = pl.BlockSpec(memory_space=pl.ANY)
     specs = {k: anywhere for k in range(len(operands))}

time: 98.7 us -> 99.3 us (level)
    ppermute x6, waiting for transfers between devices: 5.3 us -> 12 us  [swap(): lax.ppermute(array, axis, [(i, i ^ mask) for i in range(lax.axis_size(axi...]
    all_to_all x1, waiting for transfers between devices: 7.23 us -> 0.54 us  [pressure_lines(): spectra = lax.all_to_all(spectra, ('gy', 'gx'), 0, 0, tiled=True)]
  transfers between devices with their start and end apart: 12 -> 12, of which waited for: 6 -> 7; matrix products, arithmetic and copies ran while one was open for 3% -> 3% of each run, Pallas kernels for 32% -> 31%
where the time goes in v7:
time: 99.3 us; the launch traced here: 98.6 us
  Pallas kernels  46.6 us (47%)
  starting transfers between devices  21.6 us (22%)
  waiting for transfers between devices  19 us (19%)
  local copies, waits for them, and re-layouts  7.51 us (8%)
  between operations  2.74 us (3%)
  other arithmetic  1.16 us (1%)
    pallas_call x11, Pallas kernels, call(): pl.pallas_call(body, out_shape=outs, in_specs=in_specs + [pl.BlockSpec(me...  46.6 us
    ppermute x6, waiting for transfers between devices, swap(): lax.ppermute(array, axis, [(i, i ^ mask) for i in range(lax.axis_size(axi...  12 us
    ppermute x4, starting transfers between devices, ring(): lax.ppermute(array, axis, [(i, (i + step) % size) for i in range(size)])  6.66 us
    unnamed x32, local copies, waits for them, and re-layouts  6.11 us
    all_to_all x1, starting transfers between devices, pressure_lines(): spectra = lax.all_to_all(spectra, ('gy', 'gx'), 0, 0, tiled=True)  5.52 us
    ppermute x6, starting transfers between devices, swap(): lax.ppermute(array, axis, [(i, i ^ mask) for i in range(lax.axis_size(axi...  5.01 us
    ppermute x4, waiting for transfers between devices, ring(): lax.ppermute(array, axis, [(i, (i + step) % size) for i in range(size)])  4.79 us
    all_to_all x1, starting transfers between devices, pressure_lines(): solved = lax.all_to_all(solved, ('gy', 'gx'), 0, 0, tiled=True)  4.38 us
  transfers between devices with their start and end apart: 12, of which 7 were waited for; matrix products, arithmetic and copies ran while one was open for 3% of the time, Pallas kernels for 31%

profile of v7, /device:TPU:0, one launch (start us, length us, event | category | flops | bytes accessed | tf_op | source)
XLA Modules:
  0.0 98.6 jit_solution(17755586018638841895)
XLA Ops:
  0.0 1.2 %copy-done.1 = f32[2,1,256,512]{3,2,1,0:T(8,128)S(1)} copy-done((f32[2,1,256,512]{3,2,1,0:T(8,128)S(1)}, f32[2,1,256,512]{3,2,1,0:T(8,128)}, u32[]{:S(2)}) %copy-start.1) | copy-done | bytes 1048600
  1.2 0.1 pieces.1
  1.3 0.5 collective-permute-start
  1.8 2.6 %collective-permute-start.5 = (f32[2,64,512]{2,1,0:T(8,128)S(1)}, f32[2,64,512]{2,1,0:T(8,128)S(1)}, u32[]{:S(2)}, u32[]{:S(2)}) collective-permute-start(f32[2,64,512]{2,1,0:T(8,128)S(1)} %get-tuple-element.49), channel_id=1, source_target_pairs={{0,16},{8,24},{16,0},{24,8},{1,17},{9,25},{17,1},{25,9},{2,18},{10... | collective-permute-start | bytes 786440 | tf_op jit(solution)/shard_map/ppermute | solution.py:741
  4.4 0.1 collective-permute-start.6
  4.5 0.0 collective-permute-done.refs_6_.refs_1_
  4.5 1.6 %copy-done = s32[1,512,1024]{2,1,0:T(8,128)S(1)} copy-done((s32[1,512,1024]{2,1,0:T(8,128)S(1)}, s32[1,512,1024]{2,1,0:T(8,128)}, u32[]{:S(2)}) %copy-start) | copy-done | bytes 2097176
  6.0 1.2 %copy-done.2 = f32[2,1,256,512]{3,2,1,0:T(8,128)S(1)} copy-done((f32[2,1,256,512]{3,2,1,0:T(8,128)S(1)}, f32[2,1,256,512]{3,2,1,0:T(8,128)}, u32[]{:S(2)}) %copy-start.2) | copy-done | bytes 1048600
  7.3 1.1 %rows.1 = (f32[24,1024]{1,0:T(8,128)S(1)}, f32[24,1024]{1,0:T(8,128)S(1)}) custom-call(bf16[4,1,512,1024]{3,2,1,0:T(8,128)(2,1)} %refs_4_.9, bf16[4,1,512,1024]{3,2,1,0:T(8,128)(2,1)} %refs_4_.9, s32[1,512,1024]{2,1,0:T(8,128)S(1)} %copy-done, s32[1,512,1024]{2,1,0:T(8,128)S(1)} %copy-done, f32[2,1,256,512]{3,2,1,0:T(8,128)S(1)} %copy-done.2, ...), custom_call_target="tpu_custom_call" | custom-call | bytes 2097152 | tf_op jit(solution)/shard_map/rows/pallas_call | solution.py:722
  8.4 1.8 %collective-permute-start.1 = (f32[24,1024]{1,0:T(8,128)S(1)}, f32[24,1024]{1,0:T(8,128)S(1)}, u32[]{:S(2)}, u32[]{:S(2)}) collective-permute-start(f32[24,1024]{1,0:T(8,128)S(1)} %get-tuple-element.34), channel_id=1, source_target_pairs={{0,1},{1,2},{2,3},{3,4},{4,5},{5,6},{6,7},{7,0},{8,9},{9,10},{10,1... | collective-permute-start | bytes 294920 | tf_op jit(solution)/shard_map/ppermute | solution.py:737
  10.2 3.1 %collective-permute-start.2 = (f32[24,1024]{1,0:T(8,128)S(1)}, f32[24,1024]{1,0:T(8,128)S(1)}, u32[]{:S(2)}, u32[]{:S(2)}) collective-permute-start(f32[24,1024]{1,0:T(8,128)S(1)} %get-tuple-element.35), channel_id=1, source_target_pairs={{0,7},{1,0},{2,1},{3,2},{4,3},{5,4},{6,5},{7,6},{8,15},{9,8},{10,9... | collective-permute-start | bytes 294920 | tf_op jit(solution)/shard_map/ppermute | solution.py:737
  13.3 0.0 collective-permute-done.5.refs_2_
  13.3 3.3 %collective-permute-done.6.refs_3_ = f32[2,64,512]{2,1,0:T(8,128)S(1)} collective-permute-done((f32[2,64,512]{2,1,0:T(8,128)S(1)}, f32[2,64,512]{2,1,0:T(8,128)S(1)}, u32[]{:S(2)}, u32[]{:S(2)}) %collective-permute-start.6) | collective-permute-done | bytes 262176 | tf_op jit(solution)/shard_map/ppermute | solution.py:741
  16.6 0.0 collective-permute-done.1.refs_7_.refs_3_.refs_8_.refs_6_
  16.7 0.4 collective-permute-done.2.refs_8_.refs_4_.refs_9_.refs_7_
  17.1 2.1 %forward_x.1 = (f32[32,64,128]{2,1,0:T(8,128)}, f32[8,128]{1,0:T(8,128)S(1)}) custom-call(f32[2,64,512]{2,1,0:T(8,128)S(1)} %get-tuple-element.48.refs_0_, f32[2,64,512]{2,1,0:T(8,128)S(1)} %collective-permute-done.refs_6_.refs_1_, f32[2,64,512]{2,1,0:T(8,128)S(1)} %collective-permute-done.5.refs_2_, f32[2,64,512]{2,1,0:T(8,128)S(1)} %collective-permute-done.6.refs_3_, ...), custom_call_target="tpu_custom_call" | custom-call | flops 1000000000 | bytes 4194304 | tf_op jit(solution)/shard_map/forward_x/pallas_call | solution.py:722
  19.2 5.5 %all-to-all-start = ((f32[32,64,128]{2,1,0:T(8,128)}), f32[32,64,128]{2,1,0:T(8,128)S(1)}, u32[]{:S(2)}, u32[]{:S(2)}) async-start(f32[32,64,128]{2,1,0:T(8,128)} %get-tuple-element.51), calls=%async_computation | async-start | bytes 2097152 | tf_op jit(solution)/shard_map/all_to_all | solution.py:771
  24.7 0.6 add_convert_fusion.refs_0_
  25.3 2.9 %columns.1 = (f32[48,640]{1,0:T(8,128)}, f32[48,640]{1,0:T(8,128)}) custom-call(f32[4]{0:T(128)} %add_convert_fusion.refs_0_, bf16[4,1,512,1024]{3,2,1,0:T(8,128)(2,1)} %refs_4_.9, bf16[4,1,512,1024]{3,2,1,0:T(8,128)(2,1)} %refs_4_.9, s32[1,512,1024]{2,1,0:T(8,128)} %refs_7_.3, s32[1,512,1024]{2,1,0:T(8,128)} %refs_7_.3, f32[2,1,256,512]{3,2,1,0:T(8,128)} %refs_2_.9, ...), custom_call_target="tpu_custom_call" | custom-call | bytes 8388608 | tf_op jit(solution)/shard_map/columns/pallas_call | solution.py:722
  28.2 0.3 collective-permute-start.3
  28.5 1.5 %collective-permute-start.4 = (f32[48,640]{1,0:T(8,128)}, f32[48,640]{1,0:T(8,128)S(1)}, u32[]{:S(2)}, u32[]{:S(2)}) collective-permute-start(f32[48,640]{1,0:T(8,128)} %get-tuple-element.37), channel_id=1, source_target_pairs={{0,24},{8,0},{16,8},{24,16},{1,25},{9,1},{17,9},{25,17},{2,26},{10... | collective-permute-start | bytes 368648 | tf_op jit(solution)/shard_map/ppermute | solution.py:737
  30.0 0.6 pad_add_fusion.refs_0_
  30.5 3.0 %tables.1 = (bf16[2,5,256,256]{3,2,1,0:T(8,128)(2,1)}, bf16[4,144,240]{2,1,0:T(8,128)(2,1)}, s32[1]{0:T(128)}) custom-call(s32[2]{0:T(128)} %pad_add_fusion.refs_0_, f32[4,4096]{1,0:T(4,128)} %refs_1_.4, f32[4,4096]{1,0:T(4,128)} %refs_2_.6), custom_call_target="tpu_custom_call" | custom-call | bytes 4194304 | tf_op jit(solution)/shard_map/tables/pallas_call | solution.py:722
  33.6 4.3 %collective-permute-done.3.refs_5_ = f32[48,640]{1,0:T(8,128)S(1)} collective-permute-done((f32[48,640]{1,0:T(8,128)}, f32[48,640]{1,0:T(8,128)S(1)}, u32[]{:S(2)}, u32[]{:S(2)}) %collective-permute-start.3) | collective-permute-done | bytes 122912 | tf_op jit(solution)/shard_map/ppermute | solution.py:737
  37.9 0.0 collective-permute-done.4.refs_6_
  37.9 0.6 copy-done.14
  38.6 0.1 copy-done.15
  38.6 3.7 %sides.1 = (f32[5,640,128]{2,1,0:T(8,128)}, f32[272,640]{1,0:T(8,128)}, s32[1]{0:T(128)}) custom-call(f32[4]{0:T(128)} %add_convert_fusion.refs_0_, s32[1]{0:T(128)} %get-tuple-element.32.refs_1_, f32[2,1,256,512]{3,2,1,0:T(8,128)} %refs_2_.9, f32[24,1024]{1,0:T(8,128)} %copy-done.3, f32[24,1024]{1,0:T(8,128)} %copy-done.4, f32[48,640]{1,0:T(8,128)} %copy-done.14, ...), custom_call_target="tpu_custom_call" | custom-call | bytes 8388608 | tf_op jit(solution)/shard_map/sides/pallas_call | solution.py:722
  42.3 0.0 copy-start.8
  42.3 0.0 copy-start.9
  42.4 6.8 %quiet_step.2 = (f32[3,512,1024]{2,1,0:T(8,128)}, bf16[4,1,512,1024]{3,2,1,0:T(8,128)(2,1)}, bf16[4,144,1152]{2,1,0:T(8,128)(2,1)}, s32[1]{0:T(128)}) custom-call(f32[4]{0:T(128)} %add_convert_fusion.refs_0_, s32[1]{0:T(128)} %bitcast.4.refs_1_, bf16[4,1,512,1024]{3,2,1,0:T(8,128)(2,1)} %refs_4_.9, bf16[4,1,512,1024]{3,2,1,0:T(8,128)(2,1)} %refs_4_.9, ...), custom_call_target="tpu_custom_call" | custom-call | flops 3000000000 | bytes 12582912 | tf_op jit(solution)/shard_map/quiet_step/pallas_call | solution.py:722
  49.7 0.7 constant_dynamic-slice_fusion.refs_2_
  50.4 0.5 all-to-all-done.refs_0_
  50.9 4.2 %solve_y.1 = f32[32,40,128]{2,1,0:T(8,128)} custom-call(f32[32,64,128]{2,1,0:T(8,128)S(1)} %all-to-all-done.refs_0_, f32[8,128]{1,0:T(8,128)S(1)} %get-tuple-element.52.refs_1_, f32[1,128]{1,0:T(1,128)S(1)} %constant_dynamic-slice_fusion.refs_2_, bf16[1024,256]{1,0:T(8,128)(2,1)S(1)} %copy-done.8, bf16[256,48]{1,0:T(8,128)(2,1)S(1)} %copy-done.9), custom_call_target="tpu_custom_call" | custom-call | flops 4000000000 | bytes 6291456 | tf_op jit(solution)/shard_map/solve_y/pallas_call | solution.py:722
  55.2 4.4 %all-to-all-start.1 = ((f32[32,40,128]{2,1,0:T(8,128)}), f32[32,40,128]{2,1,0:T(8,128)S(1)}, u32[]{:S(2)}, u32[]{:S(2)}) async-start(f32[32,40,128]{2,1,0:T(8,128)} %solve_y.1), calls=%async_computation.1 | async-start | bytes 1310720 | tf_op jit(solution)/shard_map/all_to_all | solution.py:793
  59.6 0.0 copy-start.6
  59.6 13.4 %quiet_step.3 = (f32[3,512,1024]{2,1,0:T(8,128)}, bf16[4,1,512,1024]{3,2,1,0:T(8,128)(2,1)}, bf16[4,144,1152]{2,1,0:T(8,128)(2,1)}, s32[1]{0:T(128)}) custom-call(f32[4]{0:T(128)} %add_convert_fusion.refs_0_, s32[1]{0:T(128)} %bitcast.4.refs_1_, bf16[4,1,512,1024]{3,2,1,0:T(8,128)(2,1)} %refs_4_.9, ...), custom_call_target="tpu_custom_call", output_to_operand_aliasing={{0}: (14, {}), {1}: (15, {}), {2}: (16, {})} | custom-call | flops 8999999488 | bytes 37748736 | tf_op jit(solution)/shard_map/quiet_step/pallas_call | solution.py:722
  74.9 0.7 dynamic-slice_bitcast_fusion.refs_2_
  75.6 1.7 %all-to-all-done.1.refs_0_ = f32[32,40,128]{2,1,0:T(8,128)S(1)} async-done(((f32[32,40,128]{2,1,0:T(8,128)}), f32[32,40,128]{2,1,0:T(8,128)S(1)}, u32[]{:S(2)}, u32[]{:S(2)}) %all-to-all-start.1) | async-done | bytes 655392 | tf_op jit(solution)/shard_map/all_to_all | solution.py:793
  77.3 0.9 inverse_x.1
  78.2 0.7 copy-done.5
  78.9 0.1 collective-permute-start.7
  79.0 1.6 %collective-permute-start.8 = (f32[72,640]{1,0:T(8,128)S(1)}, f32[72,640]{1,0:T(8,128)S(1)}, u32[]{:S(2)}, u32[]{:S(2)}) collective-permute-start(f32[72,640]{1,0:T(8,128)S(1)} %get-tuple-element.57), channel_id=1, source_target_pairs={{0,16},{8,24},{16,0},{24,8},{1,17},{9,25},{17,1},{25,9},{2,18},{10... | collective-permute-start | bytes 552968 | tf_op jit(solution)/shard_map/ppermute | solution.py:741
  80.6 0.2 collective-permute-start.9
  80.8 5.7 %collective-permute-done.8.refs_9_ = f32[72,640]{1,0:T(8,128)S(1)} collective-permute-done((f32[72,640]{1,0:T(8,128)S(1)}, f32[72,640]{1,0:T(8,128)S(1)}, u32[]{:S(2)}, u32[]{:S(2)}) %collective-permute-start.8) | collective-permute-done | bytes 184352 | tf_op jit(solution)/shard_map/ppermute | solution.py:741
  86.4 3.0 %collective-permute-done.9.refs_10_ = f32[72,640]{1,0:T(8,128)S(1)} collective-permute-done((f32[72,640]{1,0:T(8,128)S(1)}, f32[72,640]{1,0:T(8,128)S(1)}, u32[]{:S(2)}, u32[]{:S(2)}) %collective-permute-start.9) | collective-permute-done | bytes 184352 | tf_op jit(solution)/shard_map/ppermute | solution.py:741
  89.4 0.7 copy-done.13
  90.1 8.3 %source_step.1 = bf16[4,1,512,1024]{3,2,1,0:T(8,128)(2,1)} custom-call(f32[272,640]{1,0:T(8,128)} %get-tuple-element.38.refs_0_, bf16[4,144,1152]{2,1,0:T(8,128)(2,1)} %get-tuple-element.43.refs_1_, bf16[2,5,256,256]{3,2,1,0:T(8,128)(2,1)} %get-tuple-element.44.refs_2_, ...), custom_call_target="tpu_custom_call", output_to_operand_aliasing={{}: (6, {})} | custom-call | flops 4000000000 | bytes 16777216 | tf_op jit(solution)/shard_map/source_step/pallas_call | solution.py:722
  (23 shorter events, 0.0 us)
Async XLA Ops:
  0.0 1.2 %copy-start.1 = (f32[2,1,256,512]{3,2,1,0:T(8,128)S(1)}, f32[2,1,256,512]{3,2,1,0:T(8,128)}, u32[]{:S(2)}) copy-start(f32[2,1,256,512]{3,2,1,0:T(8,128)} %refs_2_.9) | copy-start | bytes 3145732
  1.3 3.2 %collective-permute-start = (f32[2,64,512]{2,1,0:T(8,128)S(1)}, f32[2,64,512]{2,1,0:T(8,128)S(1)}, u32[]{:S(2)}, u32[]{:S(2)}) collective-permute-start(f32[2,64,512]{2,1,0:T(8,128)S(1)} %get-tuple-element.33), channel_id=1, source_target_pairs={{0,8},{8,0},{16,24},{24,16},{1,9},{9,1},{17,25},{25,17},{2,10},{10... | collective-permute-start | bytes 786440 | tf_op jit(solution)/shard_map/ppermute | solution.py:741
  1.8 11.5 %collective-permute-start.5 = (f32[2,64,512]{2,1,0:T(8,128)S(1)}, f32[2,64,512]{2,1,0:T(8,128)S(1)}, u32[]{:S(2)}, u32[]{:S(2)}) collective-permute-start(f32[2,64,512]{2,1,0:T(8,128)S(1)} %get-tuple-element.49), channel_id=1, source_target_pairs={{0,16},{8,24},{16,0},{24,8},{1,17},{9,25},{17,1},{25,9},{2,18},{10... | collective-permute-start | bytes 786440 | tf_op jit(solution)/shard_map/ppermute | solution.py:741
  4.4 12.3 %collective-permute-start.6 = (f32[2,64,512]{2,1,0:T(8,128)S(1)}, f32[2,64,512]{2,1,0:T(8,128)S(1)}, u32[]{:S(2)}, u32[]{:S(2)}) collective-permute-start(f32[2,64,512]{2,1,0:T(8,128)S(1)} %get-tuple-element.50), channel_id=1, source_target_pairs={{0,24},{8,16},{16,8},{24,0},{1,25},{9,17},{17,9},{25,1},{2,26},{10... | collective-permute-start | bytes 786440 | tf_op jit(solution)/shard_map/ppermute | solution.py:741
  4.5 1.6 %copy-start = (s32[1,512,1024]{2,1,0:T(8,128)S(1)}, s32[1,512,1024]{2,1,0:T(8,128)}, u32[]{:S(2)}) copy-start(s32[1,512,1024]{2,1,0:T(8,128)} %refs_7_.3) | copy-start | bytes 6291460
  6.0 1.2 %copy-start.2 = (f32[2,1,256,512]{3,2,1,0:T(8,128)S(1)}, f32[2,1,256,512]{3,2,1,0:T(8,128)}, u32[]{:S(2)}) copy-start(f32[2,1,256,512]{3,2,1,0:T(8,128)} %refs_2_.9) | copy-start | bytes 3145732
  7.3 9.8 %copy-start.7 = (bf16[1536,512]{1,0:T(8,128)(2,1)S(1)}, bf16[1536,512]{1,0:T(8,128)(2,1)}, u32[]{:S(2)}) copy-start(bf16[1536,512]{1,0:T(8,128)(2,1)} %constant.41.clone.refs_4_) | copy-start | bytes 4718596
  7.3 9.8 %copy-start.10 = (f32[8,256]{1,0:T(8,128)S(1)}, f32[8,256]{1,0:T(8,128)}, u32[]{:S(2)}) copy-start(f32[8,256]{1,0:T(8,128)} %constant.42.clone.refs_5_) | copy-start | bytes 24580
  8.4 8.3 %collective-permute-start.1 = (f32[24,1024]{1,0:T(8,128)S(1)}, f32[24,1024]{1,0:T(8,128)S(1)}, u32[]{:S(2)}, u32[]{:S(2)}) collective-permute-start(f32[24,1024]{1,0:T(8,128)S(1)} %get-tuple-element.34), channel_id=1, source_target_pairs={{0,1},{1,2},{2,3},{3,4},{4,5},{5,6},{6,7},{7,0},{8,9},{9,10},{10,1... | collective-permute-start | bytes 294920 | tf_op jit(solution)/shard_map/ppermute | solution.py:737
  10.2 6.9 %collective-permute-start.2 = (f32[24,1024]{1,0:T(8,128)S(1)}, f32[24,1024]{1,0:T(8,128)S(1)}, u32[]{:S(2)}, u32[]{:S(2)}) collective-permute-start(f32[24,1024]{1,0:T(8,128)S(1)} %get-tuple-element.35), channel_id=1, source_target_pairs={{0,7},{1,0},{2,1},{3,2},{4,3},{5,4},{6,5},{7,6},{8,15},{9,8},{10,9... | collective-permute-start | bytes 294920 | tf_op jit(solution)/shard_map/ppermute | solution.py:737
  16.7 2.5 %copy-start.3 = (f32[24,1024]{1,0:T(8,128)}, f32[24,1024]{1,0:T(8,128)S(1)}, u32[]{:S(2)}) copy-start(f32[24,1024]{1,0:T(8,128)S(1)} %collective-permute-done.1.refs_7_.refs_3_.refs_8_.refs_6_) | copy-start | bytes 294916
  17.1 2.1 %copy-start.4 = (f32[24,1024]{1,0:T(8,128)}, f32[24,1024]{1,0:T(8,128)S(1)}, u32[]{:S(2)}) copy-start(f32[24,1024]{1,0:T(8,128)S(1)} %collective-permute-done.2.refs_8_.refs_4_.refs_9_.refs_7_) | copy-start | bytes 294916
  19.2 31.8 %all-to-all-start = ((f32[32,64,128]{2,1,0:T(8,128)}), f32[32,64,128]{2,1,0:T(8,128)S(1)}, u32[]{:S(2)}, u32[]{:S(2)}) async-start(f32[32,64,128]{2,1,0:T(8,128)} %get-tuple-element.51), calls=%async_computation | async-start | bytes 2097152 | tf_op jit(solution)/shard_map/all_to_all | solution.py:771
  28.2 9.7 %collective-permute-start.3 = (f32[48,640]{1,0:T(8,128)}, f32[48,640]{1,0:T(8,128)S(1)}, u32[]{:S(2)}, u32[]{:S(2)}) collective-permute-start(f32[48,640]{1,0:T(8,128)} %get-tuple-element.36), channel_id=1, source_target_pairs={{0,8},{8,16},{16,24},{24,0},{1,9},{9,17},{17,25},{25,1},{2,10},{10... | collective-permute-start | bytes 368648 | tf_op jit(solution)/shard_map/ppermute | solution.py:737
  28.5 9.4 %collective-permute-start.4 = (f32[48,640]{1,0:T(8,128)}, f32[48,640]{1,0:T(8,128)S(1)}, u32[]{:S(2)}, u32[]{:S(2)}) collective-permute-start(f32[48,640]{1,0:T(8,128)} %get-tuple-element.37), channel_id=1, source_target_pairs={{0,24},{8,0},{16,8},{24,16},{1,25},{9,1},{17,9},{25,17},{2,26},{10... | collective-permute-start | bytes 368648 | tf_op jit(solution)/shard_map/ppermute | solution.py:737
  37.9 0.6 copy-start.14
  37.9 0.7 copy-start.15
  42.3 8.6 %copy-start.8 = (bf16[1024,256]{1,0:T(8,128)(2,1)S(1)}, bf16[1024,256]{1,0:T(8,128)(2,1)}, u32[]{:S(2)}) copy-start(bf16[1024,256]{1,0:T(8,128)(2,1)} %constant.44.clone.refs_3_) | copy-start | bytes 1572868
  42.3 8.6 %copy-start.9 = (bf16[256,48]{1,0:T(8,128)(2,1)S(1)}, bf16[256,48]{1,0:T(8,128)(2,1)}, u32[]{:S(2)}) copy-start(bf16[256,48]{1,0:T(8,128)(2,1)} %constant.45.clone.refs_4_) | copy-start | bytes 73732
  55.2 22.1 %all-to-all-start.1 = ((f32[32,40,128]{2,1,0:T(8,128)}), f32[32,40,128]{2,1,0:T(8,128)S(1)}, u32[]{:S(2)}, u32[]{:S(2)}) async-start(f32[32,40,128]{2,1,0:T(8,128)} %solve_y.1), calls=%async_computation.1 | async-start | bytes 1310720 | tf_op jit(solution)/shard_map/all_to_all | solution.py:793
  59.6 17.7 %copy-start.6 = (bf16[1536,512]{1,0:T(8,128)(2,1)S(1)}, bf16[1536,512]{1,0:T(8,128)(2,1)}, u32[]{:S(2)}) copy-start(bf16[1536,512]{1,0:T(8,128)(2,1)} %constant.47.clone.refs_1_) | copy-start | bytes 4718596
  78.2 0.7 copy-start.5
  78.9 1.9 %collective-permute-start.7 = (f32[72,640]{1,0:T(8,128)S(1)}, f32[72,640]{1,0:T(8,128)S(1)}, u32[]{:S(2)}, u32[]{:S(2)}) collective-permute-start(f32[72,640]{1,0:T(8,128)S(1)} %get-tuple-element.56), channel_id=1, source_target_pairs={{0,8},{8,0},{16,24},{24,16},{1,9},{9,1},{17,25},{25,17},{2,10},{10... | collective-permute-start | bytes 552968 | tf_op jit(solution)/shard_map/ppermute | solution.py:741
  79.0 7.4 %collective-permute-start.8 = (f32[72,640]{1,0:T(8,128)S(1)}, f32[72,640]{1,0:T(8,128)S(1)}, u32[]{:S(2)}, u32[]{:S(2)}) collective-permute-start(f32[72,640]{1,0:T(8,128)S(1)} %get-tuple-element.57), channel_id=1, source_target_pairs={{0,16},{8,24},{16,0},{24,8},{1,17},{9,25},{17,1},{25,9},{2,18},{10... | collective-permute-start | bytes 552968 | tf_op jit(solution)/shard_map/ppermute | solution.py:741
  80.6 8.9 %collective-permute-start.9 = (f32[72,640]{1,0:T(8,128)S(1)}, f32[72,640]{1,0:T(8,128)S(1)}, u32[]{:S(2)}, u32[]{:S(2)}) collective-permute-start(f32[72,640]{1,0:T(8,128)S(1)} %get-tuple-element.58), channel_id=1, source_target_pairs={{0,24},{8,16},{16,8},{24,0},{1,25},{9,17},{17,9},{25,1},{2,26},{10... | collective-permute-start | bytes 552968 | tf_op jit(solution)/shard_map/ppermute | solution.py:741
  80.8 8.7 %copy-start.11 = (f32[72,640]{1,0:T(8,128)}, f32[72,640]{1,0:T(8,128)S(1)}, u32[]{:S(2)}) copy-start(f32[72,640]{1,0:T(8,128)S(1)} %collective-permute-done.7.refs_8_) | copy-start | bytes 552964
  86.4 3.0 %copy-start.12 = (f32[72,640]{1,0:T(8,128)}, f32[72,640]{1,0:T(8,128)S(1)}, u32[]{:S(2)}) copy-start(f32[72,640]{1,0:T(8,128)S(1)} %collective-permute-done.8.refs_9_) | copy-start | bytes 552964
  89.4 0.7 copy-start.13
